TPU v7x, 512 devices: a whole 4x8x8 slice. The times are simulated.
512 devices in a mesh: row: 16 (over x, y_lo), col: 32 (over z, y_hi, core).
Axes of the slice: x: 4, y: 8 (y_hi: 2, y_lo: 4; y = y_hi * 4 + y_lo), z: 8, core: 2. Of those that a mesh axis runs over, the one named last changes fastest.
Arguments:
- pair_repr: bfloat16 [1280, 1280, 128], P('row', 'col'), may hold values from -6 to 6
- norm_gain: float32 [128], replicated, may hold values from 0.25 to 1.75
- a_gate: bfloat16 [128, 128], replicated, may hold values from -0.5 to 0.5
- a_proj: bfloat16 [128, 128], replicated, may hold values from -0.5 to 0.5
- b_gate: bfloat16 [128, 128], replicated, may hold values from -0.5 to 0.5
- b_proj: bfloat16 [128, 128], replicated, may hold values from -0.5 to 0.5
- out_gate: bfloat16 [128, 128], replicated, may hold values from -0.5 to 0.5
- out_proj: bfloat16 [128, 128], replicated, may hold values from -0.5 to 0.5
- out_gain: float32 [128], replicated, may hold values from 0.25 to 1.75
Outputs:
- mirrored: bfloat16 [1280, 1280, 128], P('row', 'col')
All inputs are finite; a program needn't handle non-finite values.
Results may differ from a plain program's by a relative error of at most 0.0083.
Values may be sent and summed in bfloat16 or wider, within the bound.
No kernel may reach another device: no remote copies, remote signals or barrier semaphores. Data moves between devices by JAX's collectives and lax.ppermute only.
A program may use at most 64 MiB of HBM per device.

v0:
```python
import jax
import jax.numpy as jnp
from jax import lax
from jax.experimental import pallas as pl
from jax.experimental.pallas import tpu as pltpu
from jax.sharding import Mesh, PartitionSpec as P

PLANE = ("zh", "yl", "z0", "yh", "core")
F32 = jnp.float32
BF16 = jnp.bfloat16
ROWS, COLS, CHANS = 80, 40, 128
CELLS = ROWS * COLS
HALF = ROWS // 2
VMEM_LIMIT = 48 * 1024 * 1024


def call(kernel, outs, scratch, flops, args):
    moved = sum(a.size * a.dtype.itemsize for a in (*args, *outs))
    return pl.pallas_call(
        kernel,
        out_shape=outs if len(outs) > 1 else outs[0],
        in_specs=[pl.BlockSpec(memory_space=pltpu.SMEM if a.dtype == jnp.int32 else pltpu.VMEM) for a in args],
        out_specs=[pl.BlockSpec(memory_space=pltpu.VMEM)] * len(outs) if len(outs) > 1 else pl.BlockSpec(memory_space=pltpu.VMEM),
        scratch_shapes=scratch,
        compiler_params=pltpu.CompilerParams(vmem_limit_bytes=VMEM_LIMIT),
        cost_estimate=pl.CostEstimate(flops=flops, bytes_accessed=moved, transcendentals=0),
    )(*args)


def shape(dims, dtype=BF16):
    return jax.ShapeDtypeStruct(dims, dtype)


def dot_nt(weight, cells):
    return lax.dot_general(weight, cells, (((1,), (1,)), ((), ())), preferred_element_type=F32)


def left_kernel(z_ref, gain_ref, gate_ref, proj_ref, left_ref, normed_ref, rows_ref):
    gain = gain_ref[...]
    for t in range(10):
        part = pl.ds(t * 320, 320)
        values = z_ref[part, :].astype(F32)
        centred = values - jnp.mean(values, axis=-1, keepdims=True)
        var_val = jnp.mean(centred * centred, axis=-1, keepdims=True)
        rows_ref[part, :] = centred * lax.rsqrt(var_val + 1e-05) * gain
    for k in range(COLS):
        normed_ref[pl.ds(k * ROWS, ROWS), :] = rows_ref[pl.ds(k, ROWS, stride=COLS), :].astype(BF16)
    for t in range(5):
        part = pl.ds(t * 640, 640)
        cells = normed_ref[part, :]
        edge = jax.nn.sigmoid(dot_nt(gate_ref[...], cells)) * dot_nt(proj_ref[...], cells)
        left_ref[:, part] = edge.astype(BF16)


def right_kernel(normed_ref, gate_ref, proj_ref, out_ref, right_ref, opened_ref, rows_ref):
    for t in range(5):
        part = pl.ds(t * 640, 640)
        cells = normed_ref[part, :]
        rows_ref[part, :] = cells.astype(F32)
        edge = jax.nn.sigmoid(dot_nt(gate_ref[...], cells)) * dot_nt(proj_ref[...], cells)
        right_ref[:, part] = edge.astype(BF16)
    for t in range(5):
        pieces = []
        for q in range(t * 5, t * 5 + 5):
            for h in range(2):
                for g in range(q * 8, q * 8 + 8):
                    pieces.append(rows_ref[pl.ds((g // 5) * ROWS + h * HALF + (g % 5) * 8, 8), :])
        cells = jnp.concatenate(pieces, axis=0).astype(BF16)
        opened_ref[:, pl.ds(t * 640, 640)] = jax.nn.sigmoid(dot_nt(out_ref[...], cells)).astype(BF16)


def lay_out(wide_ref, tall_ref, yl):
    for k in range(COLS):
        for zh in range(4):
            tall_ref[pl.ds(k * 32 + zh * 8, 8), 0:ROWS] = wide_ref[pl.ds(zh * 32 + yl * 8, 8), pl.ds(k * ROWS, ROWS)]


def left_unpack_kernel(first_ref, second_ref, out_ref, wide_ref, tall_ref):
    wide_ref[:, 0 : CELLS // 2] = first_ref[...].astype(F32)
    wide_ref[:, CELLS // 2 : CELLS] = second_ref[...].astype(F32)
    for yl in range(4):
        lay_out(wide_ref, tall_ref, yl)
        for t in range(10):
            block = jnp.transpose(tall_ref[pl.ds(t * 128, 128), :])
            out_ref[pl.ds(yl * ROWS, ROWS), pl.ds(t * 128, 128)] = block[:ROWS].astype(BF16)


def right_unpack_kernel(edge_ref, out_ref, wide_ref, tall_ref):
    wide_ref[...] = edge_ref[...].astype(F32)
    tall_ref[...] = jnp.zeros_like(tall_ref)
    for yl in range(4):
        lay_out(wide_ref, tall_ref, yl)
        out_ref[:, pl.ds(yl * 128, 128)] = tall_ref[...].astype(BF16)


def triangle_kernel(slot_ref, l0, l1, l2a, l2b, l3, right_ref, out_ref, prod_ref, wide_ref):
    right = right_ref[...]
    for n, parts in enumerate(((l0,), (l1,), (l2a, l2b), (l3,))):
        base = 0
        for part in parts:
            size = part.shape[0]
            prod = jnp.dot(part[...], right, preferred_element_type=F32)
            for yl in range(4):
                prod_ref[yl, pl.ds(base, size), :] = prod[:, yl * 128 : (yl + 1) * 128]
            base += size
        for yl in range(4):
            for i in range(HALF):
                wide_ref[pl.ds(yl * 8, 8), pl.ds(i * ROWS, ROWS)] = prod_ref[yl, pl.ds(i, 8, stride=HALF), :][:, :ROWS]
        out_ref[pl.ds(pl.multiple_of(slot_ref[n] * 32, 32), 32), :] = wide_ref[...].astype(BF16)


def turn_kernel(gate_ref, out_ref, in_rows, out_rows):
    for t in range(25):
        in_rows[t] = gate_ref[:, pl.ds(t * 128, 128)].astype(F32)
    low = lax.broadcasted_iota(jnp.int32, (4, 128), 1) < 64
    for t in range(25):
        for x in range(4):
            for mid in range(4):
                zero = in_rows[t, pl.ds(x * 32 + mid * 2, 4, stride=8), :]
                one = in_rows[t, pl.ds(x * 32 + mid * 2 + 1, 4, stride=8), :]
                out_rows[t, pl.ds(x * 32 + mid * 8, 4, stride=2), :] = jnp.where(low, zero, pltpu.roll(one, 64, 1))
                out_rows[t, pl.ds(x * 32 + mid * 8 + 1, 4, stride=2), :] = jnp.where(low, pltpu.roll(zero, 64, 1), one)
        out_ref[:, pl.ds(t * 128, 128)] = out_rows[t].astype(BF16)


def output_kernel(tri_ref, gate_ref, gain_ref, proj_ref, out_ref, prod_ref, open_ref):
    for t in range(25):
        lanes = pl.ds(t * 128, 128)
        values = tri_ref[:, lanes].astype(F32)
        centred = values - jnp.mean(values, axis=0, keepdims=True)
        var_val = jnp.mean(centred * centred, axis=0, keepdims=True)
        normed = (centred * lax.rsqrt(var_val + 1e-05) * gain_ref[...]).astype(BF16)
        prod_ref[lanes, :] = lax.dot_general(normed, proj_ref[...], (((0,), (0,)), ((), ())), preferred_element_type=F32)
        turned = jnp.transpose(gate_ref[:, lanes].astype(F32))
        for core in range(2):
            for g in range(t * 8, t * 8 + 8):
                open_ref[pl.ds((core * 40 + g // 5) * HALF + (g % 5) * 8, 8), :] = turned[core * 64 + (g % 8) * 8 : core * 64 + (g % 8) * 8 + 8]
    for j in range(0, ROWS, 2):
        pair = [prod_ref[pl.ds(j + n, HALF, stride=ROWS), :] * open_ref[pl.ds((j + n) * HALF, HALF), :] for n in range(2)]
        out_ref[pl.ds(j * HALF, ROWS), :] = jnp.concatenate(pair, axis=0).astype(BF16)


def plane_swap(chunks):
    return lax.all_to_all(chunks, PLANE, split_axis=0, concat_axis=0, tiled=True)


def gather_x(block):
    up = [(i, (i + 1) % 4) for i in range(4)]
    down = [(i, (i - 1) % 4) for i in range(4)]
    before = lax.ppermute(block, "x", up)
    after = lax.ppermute(block, "x", down)
    half = block.shape[0] // 2
    return block, before, lax.ppermute(before[:half], "x", up), lax.ppermute(after[half:], "x", down), after


def left_edges(pair, gain, gate, proj):
    return call(left_kernel, (shape((CHANS, CELLS)), shape((CELLS, CHANS))), [pltpu.VMEM((CELLS, CHANS), F32)],
                4 * CELLS * CHANS * CHANS, (pair, gain, gate, proj))


def right_edges(normed, gate, proj, out):
    return call(right_kernel, (shape((CHANS, CELLS)), shape((CHANS, CELLS))), [pltpu.VMEM((CELLS, CHANS), F32)],
                6 * CELLS * CHANS * CHANS, (normed, gate, proj, out))


UNPACK = [pltpu.VMEM((128, CELLS), F32), pltpu.VMEM((1280, 128), F32)]


def left_unpack(first, second):
    return call(left_unpack_kernel, (shape((320, 1280)),), UNPACK, 10**7, (first, second))


def right_unpack(edge):
    return call(right_unpack_kernel, (shape((1280, 512)),), UNPACK, 10**7, (edge,))


def triangle(slots, lefts, right):
    return call(triangle_kernel, (shape((128, CELLS)),), [pltpu.VMEM((4, 320, 128), F32), pltpu.VMEM((32, CELLS), F32)],
                2 * 1280 * 1280 * 512, (slots, *lefts, right))


def turn(gate):
    return call(turn_kernel, (shape((128, CELLS)),), [pltpu.VMEM((25, 128, 128), F32)] * 2, 10**7, (gate,))


def output(tri, gate, gain, proj):
    return call(output_kernel, (shape((CELLS, CHANS)),), [pltpu.VMEM((CELLS, CHANS), F32)] * 2,
                2 * CELLS * CHANS * CHANS, (tri, gate, gain, proj))


def body(pair_repr, norm_gain, a_gate, a_proj, b_gate, b_proj, out_gate, out_proj, out_gain):
    pair = pair_repr.reshape(CELLS, CHANS)
    left, normed = left_edges(pair, norm_gain.reshape(1, CHANS), a_gate.T, a_proj.T)
    left = plane_swap(left.reshape(CHANS, 2, CELLS // 2))
    right, opened = right_edges(normed, b_gate.T, b_proj.T, out_gate.T)
    both = plane_swap(jnp.stack([right, opened], axis=1))
    lefts = gather_x(left_unpack(left[:, 0], left[:, 1]))
    gate = lax.all_to_all(both[:, 1].reshape(4, 32, CELLS), "x", split_axis=0, concat_axis=0, tiled=True)
    right = right_unpack(both[:, 0])
    slots = (lax.axis_index("x") - jnp.arange(4, dtype=jnp.int32)) % 4
    tri = triangle(slots.astype(jnp.int32), lefts, right)
    back = plane_swap(jnp.stack([tri, turn(gate.reshape(128, CELLS))], axis=1))
    update = output(back[:, 0], back[:, 1], out_gain.reshape(CHANS, 1), out_proj)
    return update.reshape(ROWS, COLS, CHANS)


def solution(mesh):
    fine = Mesh(mesh.devices.reshape(4, 4, 4, 2, 2, 2), ("x", "yl", "zh", "z0", "yh", "core"))
    tile = P(("x", "yl"), ("zh", "z0", "yh", "core"), None)
    return jax.shard_map(
        body,
        mesh=fine,
        in_specs=(tile, P(), P(), P(), P(), P(), P(), P(), P()),
        out_specs=tile,
        check_vma=False,
    )
```

profile of v0, /device:TPU:1, one launch (start us, length us, event | category | flops | bytes accessed | tf_op | source)
XLA Modules:
  0.0 197.8 jit_solution(3637847810169845099)
XLA Ops:
  1.8 1.1 copy-done
  3.6 1.6 shard_map.91
  6.0 2.1 %copy.42 = bf16[128,2,1600]{2,1,0:T(2,128)(2,1)} copy(bf16[128,2,1600]{0,2,1:T(8,128)(2,1)S(1)} %bitcast.45) | data formatting | bytes 1638400 | tf_op jit(solution)/shard_map/reshape | solution.py:194
  8.1 18.4 %all-to-all-start = ((bf16[128,2,1600]{2,1,0:T(2,128)(2,1)}), bf16[128,2,1600]{2,1,0:T(2,128)(2,1)S(1)}, u32[]{:S(2)}, u32[]{:S(2)}) async-start(bf16[128,2,1600]{2,1,0:T(2,128)(2,1)} %copy.42), calls=%async_computation | async-start | bytes 1703936 | tf_op jit(solution)/shard_map/all_to_all | solution.py:144
  28.1 2.9 %copy.48 = bf16[128,2,3200]{2,1,0:T(2,128)(2,1)} copy(bf16[128,2,3200]{2,0,1:T(8,128)(2,1)S(1)} %pad_maximum_fusion) | data formatting | bytes 3276800 | tf_op jit(solution)/shard_map/stack | solution.py:196
  31.0 21.0 %all-to-all-done = bf16[128,2,1600]{2,1,0:T(2,128)(2,1)S(1)} async-done(((bf16[128,2,1600]{2,1,0:T(2,128)(2,1)}), bf16[128,2,1600]{2,1,0:T(2,128)(2,1)S(1)}, u32[]{:S(2)}, u32[]{:S(2)}) %all-to-all-start) | async-done | bytes 819232 | tf_op jit(solution)/shard_map/all_to_all | solution.py:144
  52.0 8.2 %all-to-all-start.1 = ((bf16[128,2,3200]{2,1,0:T(2,128)(2,1)}), bf16[128,2,3200]{2,1,0:T(2,128)(2,1)}, u32[]{:S(2)}, u32[]{:S(2)}) async-start(bf16[128,2,3200]{2,1,0:T(2,128)(2,1)} %copy.48), calls=%async_computation.1 | async-start | bytes 3276800 | tf_op jit(solution)/shard_map/all_to_all | solution.py:144
  60.3 1.2 fusion.3
  61.6 1.1 shard_map.92.l0
  62.6 3.1 %collective-permute-start = (bf16[320,1280]{1,0:T(8,128)(2,1)S(1)}, bf16[320,1280]{1,0:T(8,128)(2,1)S(1)}, u32[]{:S(2)}, u32[]{:S(2)}) collective-permute-start(bf16[320,1280]{1,0:T(8,128)(2,1)S(1)} %shard_map.92.l0), channel_id=1, source_target_pairs={{0,128},{128,256},{256,384},{384,0},{1,129},{129,257},{257,385},{3... | collective-permute-start | bytes 2457608 | tf_op jit(solution)/shard_map/ppermute | solution.py:150
  65.8 3.6 %collective-permute-start.2 = (bf16[320,1280]{1,0:T(8,128)(2,1)S(1)}, bf16[320,1280]{1,0:T(8,128)(2,1)S(1)}, u32[]{:S(2)}, u32[]{:S(2)}) collective-permute-start(bf16[320,1280]{1,0:T(8,128)(2,1)S(1)} %shard_map.92.l0), channel_id=1, source_target_pairs={{0,384},{128,0},{256,128},{384,256},{1,385},{129,1},{257,129},{385... | collective-permute-start | bytes 2457608 | tf_op jit(solution)/shard_map/ppermute | solution.py:151
  69.3 32.8 %all-to-all-done.1 = bf16[128,2,3200]{2,1,0:T(2,128)(2,1)} async-done(((bf16[128,2,3200]{2,1,0:T(2,128)(2,1)}), bf16[128,2,3200]{2,1,0:T(2,128)(2,1)}, u32[]{:S(2)}, u32[]{:S(2)}) %all-to-all-start.1) | async-done | bytes 1638432 | tf_op jit(solution)/shard_map/all_to_all | solution.py:144
  102.1 5.6 %fusion.2 = (bf16[128,1,3200]{2,1,0:T(2,128)(2,1)}, bf16[128,1,3200]{2,1,0:T(2,128)(2,1)S(1)}) fusion(bf16[128,2,3200]{2,1,0:T(2,128)(2,1)} %all-to-all-done.1), kind=kLoop, calls=%fused_computation.12 | loop fusion | bytes 3276800 | tf_op jit(solution)/shard_map/slice | solution.py:199
  108.7 4.0 %all-to-all-start.2 = ((bf16[4,32,3200]{2,1,0:T(8,128)(2,1)}), bf16[4,32,3200]{2,1,0:T(8,128)(2,1)S(1)}, u32[]{:S(2)}, u32[]{:S(2)}) async-start(bf16[4,32,3200]{2,1,0:T(8,128)(2,1)} %bitcast.44), calls=%async_computation.2 | async-start | bytes 1638400 | tf_op jit(solution)/shard_map/all_to_all | solution.py:198
  113.5 3.4 %collective-permute-start.1 = (bf16[160,1280]{1,0:T(8,128)(2,1)}, bf16[160,1280]{1,0:T(8,128)(2,1)}, u32[]{:S(2)}, u32[]{:S(2)}) collective-permute-start(bf16[160,1280]{1,0:T(8,128)(2,1)} %slice.34), channel_id=1, source_target_pairs={{0,128},{128,256},{256,384},{384,0},{1,129},{129,257},{257,385},{3... | collective-permute-start | bytes 1228808 | tf_op jit(solution)/shard_map/ppermute | solution.py:153
  117.8 3.1 %collective-permute-start.3 = (bf16[160,1280]{1,0:T(8,128)(2,1)}, bf16[160,1280]{1,0:T(8,128)(2,1)}, u32[]{:S(2)}, u32[]{:S(2)}) collective-permute-start(bf16[160,1280]{1,0:T(8,128)(2,1)} %slice.35), channel_id=1, source_target_pairs={{0,384},{128,0},{256,128},{384,256},{1,385},{129,1},{257,129},{385... | collective-permute-start | bytes 1228808 | tf_op jit(solution)/shard_map/ppermute | solution.py:153
  120.9 1.5 copy.68
  123.2 9.4 %collective-permute-done.1.l2a = bf16[160,1280]{1,0:T(8,128)(2,1)} collective-permute-done((bf16[160,1280]{1,0:T(8,128)(2,1)}, bf16[160,1280]{1,0:T(8,128)(2,1)}, u32[]{:S(2)}, u32[]{:S(2)}) %collective-permute-start.1) | collective-permute-done | bytes 409632 | tf_op jit(solution)/shard_map/ppermute | solution.py:153
  132.6 3.4 %shard_map.95 = bf16[128,3200]{1,0:T(8,128)(2,1)S(1)} custom-call(s32[4]{0:T(128)S(1)} %and_select_fusion.slot_ref, bf16[320,1280]{1,0:T(8,128)(2,1)S(1)} %shard_map.92.l0, bf16[320,1280]{1,0:T(8,128)(2,1)S(1)} %collective-permute-done.l1, bf16[160,1280]{1,0:T(8,128)(2,1)} %collective-permute-done.1.l2a, bf16[160,1280]{1,0:T(8,128)(2,1)} %collective-permute-done.3.l2b, ...), custom_call_target="tpu_custom_call" | custom-call | flops 1677721600 | bytes 5406736 | tf_op jit(solution)/shard_map/pallas_call | solution.py:19
  137.2 2.9 %copy.51 = bf16[128,2,3200]{2,1,0:T(2,128)(2,1)} copy(bf16[128,2,3200]{2,0,1:T(8,128)(2,1)S(1)} %pad_maximum_fusion.1) | data formatting | bytes 3276800 | tf_op jit(solution)/shard_map/stack | solution.py:202
  140.1 9.6 %all-to-all-start.3 = ((bf16[128,2,3200]{2,1,0:T(2,128)(2,1)}), bf16[128,2,3200]{2,1,0:T(2,128)(2,1)S(1)}, u32[]{:S(2)}, u32[]{:S(2)}) async-start(bf16[128,2,3200]{2,1,0:T(2,128)(2,1)} %copy.51), calls=%async_computation.3 | async-start | bytes 3276800 | tf_op jit(solution)/shard_map/all_to_all | solution.py:144
  149.9 42.0 %all-to-all-done.3 = bf16[128,2,3200]{2,1,0:T(2,128)(2,1)S(1)} async-done(((bf16[128,2,3200]{2,1,0:T(2,128)(2,1)}), bf16[128,2,3200]{2,1,0:T(2,128)(2,1)S(1)}, u32[]{:S(2)}, u32[]{:S(2)}) %all-to-all-start.3) | async-done | bytes 1638432 | tf_op jit(solution)/shard_map/all_to_all | solution.py:144
  191.9 2.3 %fusion.1 = (bf16[128,1,3200]{2,1,0:T(2,128)(2,1)S(1)}, bf16[128,1,3200]{2,1,0:T(2,128)(2,1)S(1)}) fusion(bf16[128,2,3200]{2,1,0:T(2,128)(2,1)S(1)} %all-to-all-done.3), kind=kLoop, calls=%fused_computation.11 | loop fusion | bytes 3276800 | tf_op jit(solution)/shard_map/slice | solution.py:203
  195.1 2.8 %shard_map.97 = bf16[3200,128]{1,0:T(8,128)(2,1)} custom-call(bf16[128,3200]{1,0:T(8,128)(2,1)S(1)} %bitcast.30, bf16[128,3200]{1,0:T(8,128)(2,1)S(1)} %bitcast.31, f32[128,1]{1,0:T(8,128)S(1)} %copy.54.gain_ref, bf16[128,128]{1,0:T(8,128)(2,1)S(1)} %copy-done.3), custom_call_target="tpu_custom_call" | custom-call | flops 104857600 | bytes 2490880 | tf_op jit(solution)/shard_map/pallas_call | solution.py:19
  (40 shorter events, 10.4 us)
Async XLA Ops:
  1.7 1.2 copy-start
  2.9 0.7 copy-start.4
  5.9 20.6 %copy-start.5 = (bf16[128,128]{1,0:T(8,128)(2,1)S(1)}, bf16[128,128]{1,0:T(8,128)(2,1)}, u32[]{:S(2)}) copy-start(bf16[128,128]{1,0:T(8,128)(2,1)} %param.13) | copy-start | bytes 98308
  6.0 20.7 %copy-start.6 = (bf16[128,128]{1,0:T(8,128)(2,1)S(1)}, bf16[128,128]{1,0:T(8,128)(2,1)}, u32[]{:S(2)}) copy-start(bf16[128,128]{1,0:T(8,128)(2,1)} %param.14) | copy-start | bytes 98308
  6.0 20.8 %copy-start.7 = (bf16[128,128]{1,0:T(8,128)(2,1)S(1)}, bf16[128,128]{1,0:T(8,128)(2,1)}, u32[]{:S(2)}) copy-start(bf16[128,128]{1,0:T(8,128)(2,1)} %param.15) | copy-start | bytes 98308
  8.1 43.9 %all-to-all-start = ((bf16[128,2,1600]{2,1,0:T(2,128)(2,1)}), bf16[128,2,1600]{2,1,0:T(2,128)(2,1)S(1)}, u32[]{:S(2)}, u32[]{:S(2)}) async-start(bf16[128,2,1600]{2,1,0:T(2,128)(2,1)} %copy.42), calls=%async_computation | async-start | bytes 1703936 | tf_op jit(solution)/shard_map/all_to_all | solution.py:144
  52.0 50.1 %all-to-all-start.1 = ((bf16[128,2,3200]{2,1,0:T(2,128)(2,1)}), bf16[128,2,3200]{2,1,0:T(2,128)(2,1)}, u32[]{:S(2)}, u32[]{:S(2)}) async-start(bf16[128,2,3200]{2,1,0:T(2,128)(2,1)} %copy.48), calls=%async_computation.1 | async-start | bytes 3276800 | tf_op jit(solution)/shard_map/all_to_all | solution.py:144
  62.6 50.1 %collective-permute-start = (bf16[320,1280]{1,0:T(8,128)(2,1)S(1)}, bf16[320,1280]{1,0:T(8,128)(2,1)S(1)}, u32[]{:S(2)}, u32[]{:S(2)}) collective-permute-start(bf16[320,1280]{1,0:T(8,128)(2,1)S(1)} %shard_map.92.l0), channel_id=1, source_target_pairs={{0,128},{128,256},{256,384},{384,0},{1,129},{129,257},{257,385},{3... | collective-permute-start | bytes 2457608 | tf_op jit(solution)/shard_map/ppermute | solution.py:150
  65.8 51.2 %collective-permute-start.2 = (bf16[320,1280]{1,0:T(8,128)(2,1)S(1)}, bf16[320,1280]{1,0:T(8,128)(2,1)S(1)}, u32[]{:S(2)}, u32[]{:S(2)}) collective-permute-start(bf16[320,1280]{1,0:T(8,128)(2,1)S(1)} %shard_map.92.l0), channel_id=1, source_target_pairs={{0,384},{128,0},{256,128},{384,256},{1,385},{129,1},{257,129},{385... | collective-permute-start | bytes 2457608 | tf_op jit(solution)/shard_map/ppermute | solution.py:151
  108.7 27.3 %all-to-all-start.2 = ((bf16[4,32,3200]{2,1,0:T(8,128)(2,1)}), bf16[4,32,3200]{2,1,0:T(8,128)(2,1)S(1)}, u32[]{:S(2)}, u32[]{:S(2)}) async-start(bf16[4,32,3200]{2,1,0:T(8,128)(2,1)} %bitcast.44), calls=%async_computation.2 | async-start | bytes 1638400 | tf_op jit(solution)/shard_map/all_to_all | solution.py:198
  113.5 19.1 %collective-permute-start.1 = (bf16[160,1280]{1,0:T(8,128)(2,1)}, bf16[160,1280]{1,0:T(8,128)(2,1)}, u32[]{:S(2)}, u32[]{:S(2)}) collective-permute-start(bf16[160,1280]{1,0:T(8,128)(2,1)} %slice.34), channel_id=1, source_target_pairs={{0,128},{128,256},{256,384},{384,0},{1,129},{129,257},{257,385},{3... | collective-permute-start | bytes 1228808 | tf_op jit(solution)/shard_map/ppermute | solution.py:153
  116.9 5.5 %copy-start.1 = (bf16[320,1280]{1,0:T(8,128)(2,1)}, bf16[320,1280]{1,0:T(8,128)(2,1)S(1)}, u32[]{:S(2)}) copy-start(bf16[320,1280]{1,0:T(8,128)(2,1)S(1)} %collective-permute-done.2.l3) | copy-start | bytes 2457604
  117.8 14.9 %collective-permute-start.3 = (bf16[160,1280]{1,0:T(8,128)(2,1)}, bf16[160,1280]{1,0:T(8,128)(2,1)}, u32[]{:S(2)}, u32[]{:S(2)}) collective-permute-start(bf16[160,1280]{1,0:T(8,128)(2,1)} %slice.35), channel_id=1, source_target_pairs={{0,384},{128,0},{256,128},{384,256},{1,385},{129,1},{257,129},{385... | collective-permute-start | bytes 1228808 | tf_op jit(solution)/shard_map/ppermute | solution.py:153
  122.4 10.2 %copy-start.2 = (bf16[320,1280]{1,0:T(8,128)(2,1)S(1)}, bf16[320,1280]{1,0:T(8,128)(2,1)}, u32[]{:S(2)}) copy-start(bf16[320,1280]{1,0:T(8,128)(2,1)} %copy-done.1) | copy-start | bytes 2457604
  140.1 9.6 %copy-start.8 = (f32[128]{0:T(128)S(1)}, f32[128]{0:T(128)}, u32[]{:S(2)}) copy-start(f32[128]{0:T(128)} %param.17) | copy-start | bytes 1540
  140.1 51.8 %all-to-all-start.3 = ((bf16[128,2,3200]{2,1,0:T(2,128)(2,1)}), bf16[128,2,3200]{2,1,0:T(2,128)(2,1)S(1)}, u32[]{:S(2)}, u32[]{:S(2)}) async-start(bf16[128,2,3200]{2,1,0:T(2,128)(2,1)} %copy.51), calls=%async_computation.3 | async-start | bytes 3276800 | tf_op jit(solution)/shard_map/all_to_all | solution.py:144
  194.3 0.8 copy-start.3
where the time goes:
time: 199 us; the launch traced here: 198 us
  waiting for transfers between devices  105 us (53%)
  starting transfers between devices  53.4 us (27%)
  local copies, waits for them, and re-layouts  27 us (14%)
  Pallas kernels  11.5 us (6%)
    all_to_all x3, waiting for transfers between devices, plane_swap(): lax.all_to_all(chunks, PLANE, split_axis=0, concat_axis=0, tiled=True)  95.8 us
    all_to_all x3, starting transfers between devices, plane_swap(): lax.all_to_all(chunks, PLANE, split_axis=0, concat_axis=0, tiled=True)  36.3 us
    pallas_call x7, Pallas kernels, call(): pl.pallas_call(kernel, out_shape=outs if len(outs) > 1 else outs[0], in_s...  11.5 us
    ppermute x1, waiting for transfers between devices, gather_x(): lax.ppermute(before[:half], 'x', up)  9.44 us
    unnamed x27, local copies, waits for them, and re-layouts  7.25 us
    slice x1, local copies, waits for them, and re-layouts, body(): right = right_unpack(both[:, 0])  5.64 us
    all_to_all x1, starting transfers between devices, body(): lax.all_to_all(both[:, 1].reshape(4, 32, CELLS), 'x', split_axis=0, conca...  4.01 us
  transfers between devices with their start and end apart: 8, of which 4 were waited for; matrix products, arithmetic and copies ran while one was open for 7% of the time, Pallas kernels for 3%

commit v1 on v0

--- a/solution.py
+++ b/solution.py
@@ -11,7 +11,8 @@
 ROWS, COLS, CHANS = 80, 40, 128
 CELLS = ROWS * COLS
 HALF = ROWS // 2
-VMEM_LIMIT = 48 * 1024 * 1024
+SPLIT = 13 * 128
+VMEM_LIMIT = 20 * 1024 * 1024
 
 
 def call(kernel, outs, scratch, flops, args):
@@ -32,7 +33,7 @@
 
 
 def dot_nt(weight, cells):
-    return lax.dot_general(weight, cells, (((1,), (1,)), ((), ())), preferred_element_type=F32)
+    return lax.dot_general(weight, cells, (((0,), (1,)), ((), ())), preferred_element_type=F32)
 
 
 def left_kernel(z_ref, gain_ref, gate_ref, proj_ref, left_ref, normed_ref, rows_ref):
@@ -45,20 +46,20 @@
         rows_ref[part, :] = centred * lax.rsqrt(var_val + 1e-05) * gain
     for k in range(COLS):
         normed_ref[pl.ds(k * ROWS, ROWS), :] = rows_ref[pl.ds(k, ROWS, stride=COLS), :].astype(BF16)
-    for t in range(5):
-        part = pl.ds(t * 640, 640)
-        cells = normed_ref[part, :]
+    left_ref[:, 1, CELLS - SPLIT : SPLIT] = jnp.zeros((CHANS, 2 * SPLIT - CELLS), BF16)
+    for half, start, size in ((0, 0, 640), (0, 640, 640), (0, 1280, 384), (1, 0, 640), (1, 640, 640), (1, 1280, 256)):
+        cells = normed_ref[pl.ds(half * SPLIT + start, size), :]
         edge = jax.nn.sigmoid(dot_nt(gate_ref[...], cells)) * dot_nt(proj_ref[...], cells)
-        left_ref[:, part] = edge.astype(BF16)
-
-
-def right_kernel(normed_ref, gate_ref, proj_ref, out_ref, right_ref, opened_ref, rows_ref):
+        left_ref[:, half, pl.ds(start, size)] = edge.astype(BF16)
+
+
+def right_kernel(normed_ref, gate_ref, proj_ref, out_ref, both_ref, rows_ref):
     for t in range(5):
         part = pl.ds(t * 640, 640)
         cells = normed_ref[part, :]
         rows_ref[part, :] = cells.astype(F32)
         edge = jax.nn.sigmoid(dot_nt(gate_ref[...], cells)) * dot_nt(proj_ref[...], cells)
-        right_ref[:, part] = edge.astype(BF16)
+        both_ref[:, 0, part] = edge.astype(BF16)
     for t in range(5):
         pieces = []
         for q in range(t * 5, t * 5 + 5):
@@ -66,7 +67,17 @@
                 for g in range(q * 8, q * 8 + 8):
                     pieces.append(rows_ref[pl.ds((g // 5) * ROWS + h * HALF + (g % 5) * 8, 8), :])
         cells = jnp.concatenate(pieces, axis=0).astype(BF16)
-        opened_ref[:, pl.ds(t * 640, 640)] = jax.nn.sigmoid(dot_nt(out_ref[...], cells)).astype(BF16)
+        both_ref[:, 1, pl.ds(t * 640, 640)] = jax.nn.sigmoid(dot_nt(out_ref[...], cells)).astype(BF16)
+
+
+def widen(pairs_ref, lane, wide_ref, start):
+    def step(c, _):
+        rows = pl.ds(pl.multiple_of(c * 8, 8), 8)
+        values = pairs_ref[rows].astype(F32)[:, lane, :]
+        wide_ref[rows, start : start + values.shape[-1]] = values
+        return 0
+
+    lax.fori_loop(0, 16, step, 0)
 
 
 def lay_out(wide_ref, tall_ref, yl):
@@ -75,9 +86,9 @@
             tall_ref[pl.ds(k * 32 + zh * 8, 8), 0:ROWS] = wide_ref[pl.ds(zh * 32 + yl * 8, 8), pl.ds(k * ROWS, ROWS)]
 
 
-def left_unpack_kernel(first_ref, second_ref, out_ref, wide_ref, tall_ref):
-    wide_ref[:, 0 : CELLS // 2] = first_ref[...].astype(F32)
-    wide_ref[:, CELLS // 2 : CELLS] = second_ref[...].astype(F32)
+def left_unpack_kernel(pairs_ref, out_ref, wide_ref, tall_ref):
+    widen(pairs_ref, 0, wide_ref, 0)
+    widen(pairs_ref, 1, wide_ref, SPLIT)
     for yl in range(4):
         lay_out(wide_ref, tall_ref, yl)
         for t in range(10):
@@ -85,8 +96,8 @@
             out_ref[pl.ds(yl * ROWS, ROWS), pl.ds(t * 128, 128)] = block[:ROWS].astype(BF16)
 
 
-def right_unpack_kernel(edge_ref, out_ref, wide_ref, tall_ref):
-    wide_ref[...] = edge_ref[...].astype(F32)
+def right_unpack_kernel(pairs_ref, out_ref, wide_ref, tall_ref):
+    widen(pairs_ref, 0, wide_ref, 0)
     tall_ref[...] = jnp.zeros_like(tall_ref)
     for yl in range(4):
         lay_out(wide_ref, tall_ref, yl)
@@ -109,7 +120,12 @@
         out_ref[pl.ds(pl.multiple_of(slot_ref[n] * 32, 32), 32), :] = wide_ref[...].astype(BF16)
 
 
-def turn_kernel(gate_ref, out_ref, in_rows, out_rows):
+def gate_kernel(pairs_ref, out_ref, wide_ref):
+    widen(pairs_ref, 1, wide_ref, 0)
+    out_ref[...] = wide_ref[...].astype(BF16)
+
+
+def turn_kernel(tri_ref, gate_ref, out_ref, in_rows, out_rows):
     for t in range(25):
         in_rows[t] = gate_ref[:, pl.ds(t * 128, 128)].astype(F32)
     low = lax.broadcasted_iota(jnp.int32, (4, 128), 1) < 64
@@ -120,18 +136,23 @@
                 one = in_rows[t, pl.ds(x * 32 + mid * 2 + 1, 4, stride=8), :]
                 out_rows[t, pl.ds(x * 32 + mid * 8, 4, stride=2), :] = jnp.where(low, zero, pltpu.roll(one, 64, 1))
                 out_rows[t, pl.ds(x * 32 + mid * 8 + 1, 4, stride=2), :] = jnp.where(low, pltpu.roll(zero, 64, 1), one)
-        out_ref[:, pl.ds(t * 128, 128)] = out_rows[t].astype(BF16)
-
-
-def output_kernel(tri_ref, gate_ref, gain_ref, proj_ref, out_ref, prod_ref, open_ref):
+        out_ref[:, 1, pl.ds(t * 128, 128)] = out_rows[t].astype(BF16)
+    for t in range(5):
+        lanes = pl.ds(t * 640, 640)
+        out_ref[:, 0, lanes] = tri_ref[:, lanes]
+
+
+def output_kernel(pairs_ref, gain_ref, proj_ref, out_ref, prod_ref, open_ref, tri_ref, gate_ref):
+    widen(pairs_ref, 0, tri_ref, 0)
+    widen(pairs_ref, 1, gate_ref, 0)
     for t in range(25):
         lanes = pl.ds(t * 128, 128)
-        values = tri_ref[:, lanes].astype(F32)
+        values = tri_ref[:, lanes]
         centred = values - jnp.mean(values, axis=0, keepdims=True)
         var_val = jnp.mean(centred * centred, axis=0, keepdims=True)
         normed = (centred * lax.rsqrt(var_val + 1e-05) * gain_ref[...]).astype(BF16)
         prod_ref[lanes, :] = lax.dot_general(normed, proj_ref[...], (((0,), (0,)), ((), ())), preferred_element_type=F32)
-        turned = jnp.transpose(gate_ref[:, lanes].astype(F32))
+        turned = jnp.transpose(gate_ref[:, lanes])
         for core in range(2):
             for g in range(t * 8, t * 8 + 8):
                 open_ref[pl.ds((core * 40 + g // 5) * HALF + (g % 5) * 8, 8), :] = turned[core * 64 + (g % 8) * 8 : core * 64 + (g % 8) * 8 + 8]
@@ -154,24 +175,29 @@
 
 
 def left_edges(pair, gain, gate, proj):
-    return call(left_kernel, (shape((CHANS, CELLS)), shape((CELLS, CHANS))), [pltpu.VMEM((CELLS, CHANS), F32)],
+    return call(left_kernel, (shape((CHANS, 2, SPLIT)), shape((CELLS, CHANS))), [pltpu.VMEM((CELLS, CHANS), F32)],
                 4 * CELLS * CHANS * CHANS, (pair, gain, gate, proj))
 
 
 def right_edges(normed, gate, proj, out):
-    return call(right_kernel, (shape((CHANS, CELLS)), shape((CHANS, CELLS))), [pltpu.VMEM((CELLS, CHANS), F32)],
+    return call(right_kernel, (shape((CHANS, 2, CELLS)),), [pltpu.VMEM((CELLS, CHANS), F32)],
                 6 * CELLS * CHANS * CHANS, (normed, gate, proj, out))
 
 
-UNPACK = [pltpu.VMEM((128, CELLS), F32), pltpu.VMEM((1280, 128), F32)]
-
-
-def left_unpack(first, second):
-    return call(left_unpack_kernel, (shape((320, 1280)),), UNPACK, 10**7, (first, second))
-
-
-def right_unpack(edge):
-    return call(right_unpack_kernel, (shape((1280, 512)),), UNPACK, 10**7, (edge,))
+WIDE = pltpu.VMEM((128, CELLS), F32)
+TALL = pltpu.VMEM((1280, 128), F32)
+
+
+def left_unpack(pairs):
+    return call(left_unpack_kernel, (shape((320, 1280)),), [pltpu.VMEM((128, 2 * SPLIT), F32), TALL], 10**7, (pairs,))
+
+
+def right_unpack(pairs):
+    return call(right_unpack_kernel, (shape((1280, 512)),), [WIDE, TALL], 10**7, (pairs,))
+
+
+def gate_unpack(pairs):
+    return call(gate_kernel, (shape((128, CELLS)),), [WIDE], 10**7, (pairs,))
 
 
 def triangle(slots, lefts, right):
@@ -179,28 +205,28 @@
                 2 * 1280 * 1280 * 512, (slots, *lefts, right))
 
 
-def turn(gate):
-    return call(turn_kernel, (shape((128, CELLS)),), [pltpu.VMEM((25, 128, 128), F32)] * 2, 10**7, (gate,))
-
-
-def output(tri, gate, gain, proj):
-    return call(output_kernel, (shape((CELLS, CHANS)),), [pltpu.VMEM((CELLS, CHANS), F32)] * 2,
-                2 * CELLS * CHANS * CHANS, (tri, gate, gain, proj))
+def turn(tri, gate):
+    return call(turn_kernel, (shape((128, 2, CELLS)),), [pltpu.VMEM((25, 128, 128), F32)] * 2, 10**7, (tri, gate))
+
+
+def output(pairs, gain, proj):
+    return call(output_kernel, (shape((CELLS, CHANS)),), [pltpu.VMEM((CELLS, CHANS), F32)] * 2 + [WIDE] * 2,
+                2 * CELLS * CHANS * CHANS, (pairs, gain, proj))
 
 
 def body(pair_repr, norm_gain, a_gate, a_proj, b_gate, b_proj, out_gate, out_proj, out_gain):
     pair = pair_repr.reshape(CELLS, CHANS)
-    left, normed = left_edges(pair, norm_gain.reshape(1, CHANS), a_gate.T, a_proj.T)
-    left = plane_swap(left.reshape(CHANS, 2, CELLS // 2))
-    right, opened = right_edges(normed, b_gate.T, b_proj.T, out_gate.T)
-    both = plane_swap(jnp.stack([right, opened], axis=1))
-    lefts = gather_x(left_unpack(left[:, 0], left[:, 1]))
-    gate = lax.all_to_all(both[:, 1].reshape(4, 32, CELLS), "x", split_axis=0, concat_axis=0, tiled=True)
-    right = right_unpack(both[:, 0])
+    left, normed = left_edges(pair, norm_gain.reshape(1, CHANS), a_gate, a_proj)
+    left = plane_swap(left)
+    both = plane_swap(right_edges(normed, b_gate, b_proj, out_gate))
+    lefts = gather_x(left_unpack(left))
+    both, lefts = lax.optimization_barrier((both, lefts))
+    gate = lax.all_to_all(gate_unpack(both).reshape(4, 32, CELLS), "x", split_axis=0, concat_axis=0, tiled=True)
+    right = right_unpack(both)
     slots = (lax.axis_index("x") - jnp.arange(4, dtype=jnp.int32)) % 4
     tri = triangle(slots.astype(jnp.int32), lefts, right)
-    back = plane_swap(jnp.stack([tri, turn(gate.reshape(128, CELLS))], axis=1))
-    update = output(back[:, 0], back[:, 1], out_gain.reshape(CHANS, 1), out_proj)
+    back = plane_swap(turn(tri, gate.reshape(128, CELLS)))
+    update = output(back, out_gain.reshape(CHANS, 1), out_proj)
     return update.reshape(ROWS, COLS, CHANS)
 
 

time: 199 us -> 183 us (0.920)
  local copies, waits for them, and re-layouts: 27 us -> 5.06 us
  Pallas kernels: 11.5 us -> 22.9 us
  waiting for transfers between devices: 105 us -> 95.3 us
  starting transfers between devices: 53.4 us -> 58 us
    all_to_all x3, waiting for transfers between devices: 95.8 us -> 68.6 us  [plane_swap(): lax.all_to_all(chunks, PLANE, split_axis=0, concat_axis=0, tiled=True)]
    ppermute x1, waiting for transfers between devices: 0.01 us -> 15.5 us  [gather_x(): before = lax.ppermute(block, 'x', up)]
    pallas_call x7 -> x8, Pallas kernels: 11.5 us -> 22.9 us  [call(): pl.pallas_call(kernel, out_shape=outs if len(outs) > 1 else outs[0], in_s...]
    slice x3 -> x0, local copies, waits for them, and re-layouts: 9.13 us -> none  [the longest x1 5.64 us: body(): right = right_unpack(both[:, 0])]
    another operation x2 -> x0, local copies, waits for them, and re-layouts: 5.81 us -> none  [the longest x1 2.9 us: body(): both = plane_swap(jnp.stack([right, opened], axis=1))]
    all_to_all x1, waiting for transfers between devices: 0.01 us -> 5.41 us  [body(): lax.all_to_all(gate_unpack(both).reshape(4, 32, CELLS), 'x', split_axis=0...]
    all_to_all x3, starting transfers between devices: 36.3 us -> 41 us  [plane_swap(): lax.all_to_all(chunks, PLANE, split_axis=0, concat_axis=0, tiled=True)]
    ppermute x1, waiting for transfers between devices: 9.44 us -> 5.7 us  [gather_x(): lax.ppermute(before[:half], 'x', up)]
  transfers between devices with their start and end apart: 8 -> 8, of which waited for: 4 -> 7; matrix products, arithmetic and copies ran while one was open for 7% -> 0% of each run, Pallas kernels for 3% -> 5%
where the time goes in v1:
time: 183 us; the launch traced here: 182 us
  waiting for transfers between devices  95.3 us (52%)
  starting transfers between devices  58 us (32%)
  Pallas kernels  22.9 us (13%)
  local copies, waits for them, and re-layouts  5.06 us (3%)
    all_to_all x3, waiting for transfers between devices, plane_swap(): lax.all_to_all(chunks, PLANE, split_axis=0, concat_axis=0, tiled=True)  68.6 us
    all_to_all x3, starting transfers between devices, plane_swap(): lax.all_to_all(chunks, PLANE, split_axis=0, concat_axis=0, tiled=True)  41 us
    pallas_call x8, Pallas kernels, call(): pl.pallas_call(kernel, out_shape=outs if len(outs) > 1 else outs[0], in_s...  22.9 us
    ppermute x1, waiting for transfers between devices, gather_x(): before = lax.ppermute(block, 'x', up)  15.5 us
    ppermute x1, waiting for transfers between devices, gather_x(): lax.ppermute(before[:half], 'x', up)  5.7 us
    all_to_all x1, waiting for transfers between devices, body(): lax.all_to_all(gate_unpack(both).reshape(4, 32, CELLS), 'x', split_axis=0...  5.41 us
    unnamed x34, local copies, waits for them, and re-layouts  4.89 us
    ppermute x1, starting transfers between devices, gather_x(): lax.ppermute(after[half:], 'x', down)  4.57 us
  transfers between devices with their start and end apart: 8, of which 7 were waited for; matrix products, arithmetic and copies ran while one was open for 0% of the time, Pallas kernels for 5%

profile of v1, /device:TPU:1, one launch (start us, length us, event | category | flops | bytes accessed | tf_op | source)
XLA Modules:
  0.0 181.5 jit_solution(17226017604723421945)
XLA Ops:
  0.0 1.1 copy-done
  3.3 3.0 %shard_map.91 = (bf16[128,2,1664]{2,1,0:T(2,128)(2,1)}, bf16[3200,128]{1,0:T(8,128)(2,1)S(1)}) custom-call(bf16[3200,128]{1,0:T(8,128)(2,1)S(1)} %bitcast.7, f32[1,128]{1,0:T(1,128)S(1)} %bitcast.8, bf16[128,128]{1,0:T(8,128)(2,1)S(1)} %copy-done.9, bf16[128,128]{1,0:T(8,128)(2,1)S(1)} %copy-done.10), custom_call_target="tpu_custom_call" | custom-call | flops 209715200 | bytes 2556416 | tf_op jit(solution)/shard_map/pallas_call | solution.py:20
  6.3 18.4 %all-to-all-start.1 = ((bf16[128,2,1664]{2,1,0:T(2,128)(2,1)}), bf16[128,2,1664]{2,1,0:T(2,128)(2,1)S(1)}, u32[]{:S(2)}, u32[]{:S(2)}) async-start(bf16[128,2,1664]{2,1,0:T(2,128)(2,1)} %get-tuple-element.14), calls=%async_computation.1 | async-start | bytes 1703936 | tf_op jit(solution)/shard_map/all_to_all | solution.py:165
  24.8 2.8 %shard_map.92 = bf16[128,2,3200]{2,1,0:T(2,128)(2,1)} custom-call(bf16[3200,128]{1,0:T(8,128)(2,1)S(1)} %get-tuple-element.13.normed_ref, bf16[128,128]{1,0:T(8,128)(2,1)S(1)} %copy-done.5, bf16[128,128]{1,0:T(8,128)(2,1)S(1)} %copy-done.6, bf16[128,128]{1,0:T(8,128)(2,1)S(1)} %copy-done.7), custom_call_target="tpu_custom_call" | custom-call | flops 314572800 | bytes 2555904 | tf_op jit(solution)/shard_map/pallas_call | solution.py:20
  27.6 22.6 %all-to-all-done.1.pairs_ref = bf16[128,2,1664]{2,1,0:T(2,128)(2,1)S(1)} async-done(((bf16[128,2,1664]{2,1,0:T(2,128)(2,1)}), bf16[128,2,1664]{2,1,0:T(2,128)(2,1)S(1)}, u32[]{:S(2)}, u32[]{:S(2)}) %all-to-all-start.1) | async-done | bytes 852000 | tf_op jit(solution)/shard_map/all_to_all | solution.py:165
  50.2 7.8 %all-to-all-start = ((bf16[128,2,3200]{2,1,0:T(2,128)(2,1)}), bf16[128,2,3200]{2,1,0:T(2,128)(2,1)S(1)}, u32[]{:S(2)}, u32[]{:S(2)}) async-start(bf16[128,2,3200]{2,1,0:T(2,128)(2,1)} %shard_map.92), calls=%async_computation | async-start | bytes 3276800 | tf_op jit(solution)/shard_map/all_to_all | solution.py:165
  58.1 2.2 %shard_map.93.l0 = bf16[320,1280]{1,0:T(8,128)(2,1)S(1)} custom-call(bf16[128,2,1664]{2,1,0:T(2,128)(2,1)S(1)} %all-to-all-done.1.pairs_ref), custom_call_target="tpu_custom_call" | custom-call | flops 10000000 | bytes 1671168 | tf_op jit(solution)/shard_map/pallas_call | solution.py:20
  60.3 3.1 %collective-permute-start = (bf16[320,1280]{1,0:T(8,128)(2,1)S(1)}, bf16[320,1280]{1,0:T(8,128)(2,1)S(1)}, u32[]{:S(2)}, u32[]{:S(2)}) collective-permute-start(bf16[320,1280]{1,0:T(8,128)(2,1)S(1)} %shard_map.93.l0), channel_id=1, source_target_pairs={{0,128},{128,256},{256,384},{384,0},{1,129},{129,257},{257,385},{3... | collective-permute-start | bytes 2457608 | tf_op jit(solution)/shard_map/ppermute | solution.py:171
  63.4 3.4 %collective-permute-start.2 = (bf16[320,1280]{1,0:T(8,128)(2,1)S(1)}, bf16[320,1280]{1,0:T(8,128)(2,1)S(1)}, u32[]{:S(2)}, u32[]{:S(2)}) collective-permute-start(bf16[320,1280]{1,0:T(8,128)(2,1)S(1)} %shard_map.93.l0), channel_id=1, source_target_pairs={{0,384},{128,0},{256,128},{384,256},{1,385},{129,1},{257,129},{385... | collective-permute-start | bytes 2457608 | tf_op jit(solution)/shard_map/ppermute | solution.py:172
  66.8 15.5 %collective-permute-done.l1 = bf16[320,1280]{1,0:T(8,128)(2,1)S(1)} collective-permute-done((bf16[320,1280]{1,0:T(8,128)(2,1)S(1)}, bf16[320,1280]{1,0:T(8,128)(2,1)S(1)}, u32[]{:S(2)}, u32[]{:S(2)}) %collective-permute-start) | collective-permute-done | bytes 819232 | tf_op jit(solution)/shard_map/ppermute | solution.py:171
  82.3 1.9 %collective-permute-start.1 = (bf16[160,1280]{1,0:T(8,128)(2,1)S(1)}, bf16[160,1280]{1,0:T(8,128)(2,1)S(1)}, u32[]{:S(2)}, u32[]{:S(2)}) collective-permute-start(bf16[160,1280]{1,0:T(8,128)(2,1)S(1)} %slice.8), channel_id=1, source_target_pairs={{0,128},{128,256},{256,384},{384,0},{1,129},{129,257},{257,385},{3... | collective-permute-start | bytes 1228808 | tf_op jit(solution)/shard_map/ppermute | solution.py:174
  84.3 4.6 %collective-permute-start.3 = (bf16[160,1280]{1,0:T(8,128)(2,1)S(1)}, bf16[160,1280]{1,0:T(8,128)(2,1)S(1)}, u32[]{:S(2)}, u32[]{:S(2)}) collective-permute-start(bf16[160,1280]{1,0:T(8,128)(2,1)S(1)} %slice.9), channel_id=1, source_target_pairs={{0,384},{128,0},{256,128},{384,256},{1,385},{129,1},{257,129},{385... | collective-permute-start | bytes 1228808 | tf_op jit(solution)/shard_map/ppermute | solution.py:174
  88.9 5.7 %collective-permute-done.1.l2a = bf16[160,1280]{1,0:T(8,128)(2,1)S(1)} collective-permute-done((bf16[160,1280]{1,0:T(8,128)(2,1)S(1)}, bf16[160,1280]{1,0:T(8,128)(2,1)S(1)}, u32[]{:S(2)}, u32[]{:S(2)}) %collective-permute-start.1) | collective-permute-done | bytes 409632 | tf_op jit(solution)/shard_map/ppermute | solution.py:174
  94.6 0.8 copy-done.12
  96.3 3.9 %all-to-all-done.pairs_ref = bf16[128,2,3200]{2,1,0:T(2,128)(2,1)S(1)} async-done(((bf16[128,2,3200]{2,1,0:T(2,128)(2,1)}), bf16[128,2,3200]{2,1,0:T(2,128)(2,1)S(1)}, u32[]{:S(2)}, u32[]{:S(2)}) %all-to-all-start) | async-done | bytes 1638432 | tf_op jit(solution)/shard_map/all_to_all | solution.py:165
  100.2 1.7 shard_map.96
  101.9 4.0 %all-to-all-start.2 = ((bf16[4,32,3200]{2,1,0:T(8,128)(2,1)}), bf16[4,32,3200]{2,1,0:T(8,128)(2,1)S(1)}, u32[]{:S(2)}, u32[]{:S(2)}) async-start(bf16[4,32,3200]{2,1,0:T(8,128)(2,1)} %bitcast.2), calls=%async_computation.2 | async-start | bytes 1638400 | tf_op jit(solution)/shard_map/all_to_all | solution.py:224
  106.0 2.0 %shard_map.94.right_ref = bf16[1280,512]{1,0:T(8,128)(2,1)S(1)} custom-call(bf16[128,2,3200]{2,1,0:T(2,128)(2,1)S(1)} %all-to-all-done.pairs_ref), custom_call_target="tpu_custom_call" | custom-call | flops 10000000 | bytes 2949120 | tf_op jit(solution)/shard_map/pallas_call | solution.py:20
  108.1 2.7 %shard_map.95.tri_ref = bf16[128,3200]{1,0:T(8,128)(2,1)S(1)} custom-call(s32[4]{0:T(128)S(1)} %and_select_fusion.slot_ref, bf16[320,1280]{1,0:T(8,128)(2,1)S(1)} %shard_map.93.l0, bf16[320,1280]{1,0:T(8,128)(2,1)S(1)} %copy-done.2, bf16[160,1280]{1,0:T(8,128)(2,1)S(1)} %copy-done.13, bf16[160,1280]{1,0:T(8,128)(2,1)S(1)} %copy-done.15, ...), custom_call_target="tpu_custom_call" | custom-call | flops 1677721600 | bytes 5406736 | tf_op jit(solution)/shard_map/pallas_call | solution.py:20
  110.8 5.4 %all-to-all-done.2 = bf16[4,32,3200]{2,1,0:T(8,128)(2,1)S(1)} async-done(((bf16[4,32,3200]{2,1,0:T(8,128)(2,1)}), bf16[4,32,3200]{2,1,0:T(8,128)(2,1)S(1)}, u32[]{:S(2)}, u32[]{:S(2)}) %all-to-all-start.2) | async-done | bytes 819232 | tf_op jit(solution)/shard_map/all_to_all | solution.py:224
  116.2 3.9 %shard_map.97 = bf16[128,2,3200]{2,1,0:T(2,128)(2,1)} custom-call(bf16[128,3200]{1,0:T(8,128)(2,1)S(1)} %shard_map.95.tri_ref, bf16[128,3200]{1,0:T(8,128)(2,1)S(1)} %bitcast.6), custom_call_target="tpu_custom_call" | custom-call | flops 10000000 | bytes 3276800 | tf_op jit(solution)/shard_map/pallas_call | solution.py:20
  120.2 14.7 %all-to-all-start.3 = ((bf16[128,2,3200]{2,1,0:T(2,128)(2,1)}), bf16[128,2,3200]{2,1,0:T(2,128)(2,1)S(1)}, u32[]{:S(2)}, u32[]{:S(2)}) async-start(bf16[128,2,3200]{2,1,0:T(2,128)(2,1)} %shard_map.97), calls=%async_computation.3 | async-start | bytes 3276800 | tf_op jit(solution)/shard_map/all_to_all | solution.py:165
  135.0 42.0 %all-to-all-done.3.pairs_ref = bf16[128,2,3200]{2,1,0:T(2,128)(2,1)S(1)} async-done(((bf16[128,2,3200]{2,1,0:T(2,128)(2,1)}), bf16[128,2,3200]{2,1,0:T(2,128)(2,1)S(1)}, u32[]{:S(2)}, u32[]{:S(2)}) %all-to-all-start.3) | async-done | bytes 1638432 | tf_op jit(solution)/shard_map/all_to_all | solution.py:165
  177.0 4.5 %shard_map.98 = bf16[3200,128]{1,0:T(8,128)(2,1)} custom-call(bf16[128,2,3200]{2,1,0:T(2,128)(2,1)S(1)} %all-to-all-done.3.pairs_ref, f32[128,1]{1,0:T(8,128)S(1)} %copy.10.gain_ref, bf16[128,128]{1,0:T(8,128)(2,1)S(1)} %copy-done.8), custom_call_target="tpu_custom_call" | custom-call | flops 104857600 | bytes 2490880 | tf_op jit(solution)/shard_map/pallas_call | solution.py:20
  (38 shorter events, 3.3 us)
Async XLA Ops:
  0.0 1.1 copy-start
  1.1 0.8 copy-start.9
  1.9 0.8 copy-start.10
  3.3 21.4 %copy-start.5 = (bf16[128,128]{1,0:T(8,128)(2,1)S(1)}, bf16[128,128]{1,0:T(8,128)(2,1)}, u32[]{:S(2)}) copy-start(bf16[128,128]{1,0:T(8,128)(2,1)} %gate_ref.3) | copy-start | bytes 98308
  3.3 21.4 %copy-start.6 = (bf16[128,128]{1,0:T(8,128)(2,1)S(1)}, bf16[128,128]{1,0:T(8,128)(2,1)}, u32[]{:S(2)}) copy-start(bf16[128,128]{1,0:T(8,128)(2,1)} %proj_ref.4) | copy-start | bytes 98308
  3.3 21.5 %copy-start.7 = (bf16[128,128]{1,0:T(8,128)(2,1)S(1)}, bf16[128,128]{1,0:T(8,128)(2,1)}, u32[]{:S(2)}) copy-start(bf16[128,128]{1,0:T(8,128)(2,1)} %out_ref.1) | copy-start | bytes 98308
  6.3 43.9 %all-to-all-start.1 = ((bf16[128,2,1664]{2,1,0:T(2,128)(2,1)}), bf16[128,2,1664]{2,1,0:T(2,128)(2,1)S(1)}, u32[]{:S(2)}, u32[]{:S(2)}) async-start(bf16[128,2,1664]{2,1,0:T(2,128)(2,1)} %get-tuple-element.14), calls=%async_computation.1 | async-start | bytes 1703936 | tf_op jit(solution)/shard_map/all_to_all | solution.py:165
  50.2 50.0 %all-to-all-start = ((bf16[128,2,3200]{2,1,0:T(2,128)(2,1)}), bf16[128,2,3200]{2,1,0:T(2,128)(2,1)S(1)}, u32[]{:S(2)}, u32[]{:S(2)}) async-start(bf16[128,2,3200]{2,1,0:T(2,128)(2,1)} %shard_map.92), calls=%async_computation | async-start | bytes 3276800 | tf_op jit(solution)/shard_map/all_to_all | solution.py:165
  60.3 22.0 %collective-permute-start = (bf16[320,1280]{1,0:T(8,128)(2,1)S(1)}, bf16[320,1280]{1,0:T(8,128)(2,1)S(1)}, u32[]{:S(2)}, u32[]{:S(2)}) collective-permute-start(bf16[320,1280]{1,0:T(8,128)(2,1)S(1)} %shard_map.93.l0), channel_id=1, source_target_pairs={{0,128},{128,256},{256,384},{384,0},{1,129},{129,257},{257,385},{3... | collective-permute-start | bytes 2457608 | tf_op jit(solution)/shard_map/ppermute | solution.py:171
  63.4 20.8 %collective-permute-start.2 = (bf16[320,1280]{1,0:T(8,128)(2,1)S(1)}, bf16[320,1280]{1,0:T(8,128)(2,1)S(1)}, u32[]{:S(2)}, u32[]{:S(2)}) collective-permute-start(bf16[320,1280]{1,0:T(8,128)(2,1)S(1)} %shard_map.93.l0), channel_id=1, source_target_pairs={{0,384},{128,0},{256,128},{384,256},{1,385},{129,1},{257,129},{385... | collective-permute-start | bytes 2457608 | tf_op jit(solution)/shard_map/ppermute | solution.py:172
  82.3 19.6 %copy-start.1 = (bf16[320,1280]{1,0:T(8,128)(2,1)}, bf16[320,1280]{1,0:T(8,128)(2,1)S(1)}, u32[]{:S(2)}) copy-start(bf16[320,1280]{1,0:T(8,128)(2,1)S(1)} %collective-permute-done.l1) | copy-start | bytes 2457604
  82.3 12.3 %collective-permute-start.1 = (bf16[160,1280]{1,0:T(8,128)(2,1)S(1)}, bf16[160,1280]{1,0:T(8,128)(2,1)S(1)}, u32[]{:S(2)}, u32[]{:S(2)}) collective-permute-start(bf16[160,1280]{1,0:T(8,128)(2,1)S(1)} %slice.8), channel_id=1, source_target_pairs={{0,128},{128,256},{256,384},{384,0},{1,129},{129,257},{257,385},{3... | collective-permute-start | bytes 1228808 | tf_op jit(solution)/shard_map/ppermute | solution.py:174
  84.2 10.3 %copy-start.3 = (bf16[320,1280]{1,0:T(8,128)(2,1)}, bf16[320,1280]{1,0:T(8,128)(2,1)S(1)}, u32[]{:S(2)}) copy-start(bf16[320,1280]{1,0:T(8,128)(2,1)S(1)} %collective-permute-done.2.l3) | copy-start | bytes 2457604
  84.3 11.2 %collective-permute-start.3 = (bf16[160,1280]{1,0:T(8,128)(2,1)S(1)}, bf16[160,1280]{1,0:T(8,128)(2,1)S(1)}, u32[]{:S(2)}, u32[]{:S(2)}) collective-permute-start(bf16[160,1280]{1,0:T(8,128)(2,1)S(1)} %slice.9), channel_id=1, source_target_pairs={{0,384},{128,0},{256,128},{384,256},{1,385},{129,1},{257,129},{385... | collective-permute-start | bytes 1228808 | tf_op jit(solution)/shard_map/ppermute | solution.py:174
  94.6 0.8 copy-start.12
  95.5 0.8 copy-start.14
  101.9 14.3 %all-to-all-start.2 = ((bf16[4,32,3200]{2,1,0:T(8,128)(2,1)}), bf16[4,32,3200]{2,1,0:T(8,128)(2,1)S(1)}, u32[]{:S(2)}, u32[]{:S(2)}) async-start(bf16[4,32,3200]{2,1,0:T(8,128)(2,1)} %bitcast.2), calls=%async_computation.2 | async-start | bytes 1638400 | tf_op jit(solution)/shard_map/all_to_all | solution.py:224
  105.9 2.1 %copy-start.2 = (bf16[320,1280]{1,0:T(8,128)(2,1)S(1)}, bf16[320,1280]{1,0:T(8,128)(2,1)}, u32[]{:S(2)}) copy-start(bf16[320,1280]{1,0:T(8,128)(2,1)} %copy-done.1) | copy-start | bytes 2457604
  105.9 2.1 %copy-start.4 = (bf16[320,1280]{1,0:T(8,128)(2,1)S(1)}, bf16[320,1280]{1,0:T(8,128)(2,1)}, u32[]{:S(2)}) copy-start(bf16[320,1280]{1,0:T(8,128)(2,1)} %copy-done.3) | copy-start | bytes 2457604
  105.9 2.1 %copy-start.13 = (bf16[160,1280]{1,0:T(8,128)(2,1)S(1)}, bf16[160,1280]{1,0:T(8,128)(2,1)}, u32[]{:S(2)}) copy-start(bf16[160,1280]{1,0:T(8,128)(2,1)} %copy-done.12) | copy-start | bytes 1228804
  105.9 2.1 %copy-start.15 = (bf16[160,1280]{1,0:T(8,128)(2,1)S(1)}, bf16[160,1280]{1,0:T(8,128)(2,1)}, u32[]{:S(2)}) copy-start(bf16[160,1280]{1,0:T(8,128)(2,1)} %copy-done.14) | copy-start | bytes 1228804
  120.1 14.7 %copy-start.16 = (f32[128]{0:T(128)S(1)}, f32[128]{0:T(128)}, u32[]{:S(2)}) copy-start(f32[128]{0:T(128)} %param.17) | copy-start | bytes 1540
  120.2 56.9 %copy-start.8 = (bf16[128,128]{1,0:T(8,128)(2,1)S(1)}, bf16[128,128]{1,0:T(8,128)(2,1)}, u32[]{:S(2)}) copy-start(bf16[128,128]{1,0:T(8,128)(2,1)} %proj_ref.5) | copy-start | bytes 98308
  120.2 56.9 %all-to-all-start.3 = ((bf16[128,2,3200]{2,1,0:T(2,128)(2,1)}), bf16[128,2,3200]{2,1,0:T(2,128)(2,1)S(1)}, u32[]{:S(2)}, u32[]{:S(2)}) async-start(bf16[128,2,3200]{2,1,0:T(2,128)(2,1)} %shard_map.97), calls=%async_computation.3 | async-start | bytes 3276800 | tf_op jit(solution)/shard_map/all_to_all | solution.py:165
  (1 other events, 0.7 us)

commit v2 on v1

v2 whole, which is shorter than its diff:
```python
import jax
import jax.numpy as jnp
from jax import lax
from jax.experimental import pallas as pl
from jax.experimental.pallas import tpu as pltpu
from jax.sharding import Mesh, PartitionSpec as P

PLANE = ("zh", "yl", "z0", "yh", "core")
F32 = jnp.float32
BF16 = jnp.bfloat16
ROWS, COLS, CHANS = 80, 40, 128
CELLS = ROWS * COLS
HALF = ROWS // 2
SPLIT = 13 * 128
VMEM_LIMIT = 20 * 1024 * 1024


def call(kernel, outs, scratch, flops, args):
    moved = sum(a.size * a.dtype.itemsize for a in (*args, *outs))
    return pl.pallas_call(
        kernel,
        out_shape=outs if len(outs) > 1 else outs[0],
        in_specs=[pl.BlockSpec(memory_space=pltpu.SMEM if a.dtype == jnp.int32 else pltpu.VMEM) for a in args],
        out_specs=[pl.BlockSpec(memory_space=pltpu.VMEM)] * len(outs) if len(outs) > 1 else pl.BlockSpec(memory_space=pltpu.VMEM),
        scratch_shapes=scratch,
        compiler_params=pltpu.CompilerParams(vmem_limit_bytes=VMEM_LIMIT),
        cost_estimate=pl.CostEstimate(flops=flops, bytes_accessed=moved, transcendentals=0),
    )(*args)


def shape(dims, dtype=BF16):
    return jax.ShapeDtypeStruct(dims, dtype)


def dot_nt(weight, cells):
    return lax.dot_general(weight, cells, (((0,), (1,)), ((), ())), preferred_element_type=F32)


def edges_kernel(z_ref, gain_ref, a_gate, a_proj, b_gate, b_proj, pairs_ref, normed_ref, rows_ref):
    gain = gain_ref[...]
    for t in range(10):
        part = pl.ds(t * 320, 320)
        values = z_ref[part, :].astype(F32)
        centred = values - jnp.mean(values, axis=-1, keepdims=True)
        var_val = jnp.mean(centred * centred, axis=-1, keepdims=True)
        rows_ref[part, :] = centred * lax.rsqrt(var_val + 1e-05) * gain
    for k in range(COLS):
        normed_ref[pl.ds(k * ROWS, ROWS), :] = rows_ref[pl.ds(k, ROWS, stride=COLS), :].astype(BF16)
    for t in range(5):
        part = pl.ds(t * 640, 640)
        cells = normed_ref[part, :]
        for row, gate_ref, proj_ref in ((0, a_gate, a_proj), (1, b_gate, b_proj)):
            edge = jax.nn.sigmoid(dot_nt(gate_ref[...], cells)) * dot_nt(proj_ref[...], cells)
            pairs_ref[:, row, part] = edge.astype(BF16)


def widen(pairs_ref, places):
    def step(c, _):
        rows = pl.ds(pl.multiple_of(c * 8, 8), 8)
        values = pairs_ref[rows].astype(F32)
        for n, (wide_ref, start) in places.items():
            wide_ref[rows, start : start + values.shape[-1]] = values[:, n, :]
        return 0

    lax.fori_loop(0, 16, step, 0)


def lay_out(wide_ref, tall_ref, yl):
    for k in range(COLS):
        for zh in range(4):
            tall_ref[pl.ds(k * 32 + zh * 8, 8), 0:ROWS] = wide_ref[pl.ds(zh * 32 + yl * 8, 8), pl.ds(k * ROWS, ROWS)]


def left_unpack_kernel(pairs_ref, out_ref, wide_ref, tall_ref):
    widen(pairs_ref, {0: (wide_ref, 0)})
    for yl in range(4):
        lay_out(wide_ref, tall_ref, yl)
        for t in range(10):
            block = jnp.transpose(tall_ref[pl.ds(t * 128, 128), :])
            block = block[:ROWS].astype(BF16)
            for copy in range(4):
                out_ref[copy, pl.ds(yl * ROWS, ROWS), pl.ds(t * 128, 128)] = block


def right_unpack_kernel(pairs_ref, out_ref, wide_ref, tall_ref):
    widen(pairs_ref, {1: (wide_ref, 0)})
    tall_ref[...] = jnp.zeros_like(tall_ref)
    for yl in range(4):
        lay_out(wide_ref, tall_ref, yl)
        out_ref[:, pl.ds(yl * 128, 128)] = tall_ref[...].astype(BF16)


def triangle_kernel(lefts_ref, right_ref, out_ref, prod_ref, wide_ref):
    right = right_ref[...]
    wide_ref[:, CELLS : 2 * SPLIT] = jnp.zeros((32, 2 * SPLIT - CELLS), F32)
    for n in range(4):
        prod = jnp.dot(lefts_ref[n], right, preferred_element_type=F32)
        for yl in range(4):
            prod_ref[yl] = prod[:, yl * 128 : (yl + 1) * 128]
        for yl in range(4):
            for i in range(HALF):
                wide_ref[pl.ds(yl * 8, 8), pl.ds(i * ROWS, ROWS)] = prod_ref[yl, pl.ds(i, 8, stride=HALF), :][:, :ROWS]
        out_ref[n * 32 : n * 32 + 32, 0, :] = wide_ref[:, 0:SPLIT].astype(BF16)
        out_ref[n * 32 : n * 32 + 32, 1, :] = wide_ref[:, SPLIT : 2 * SPLIT].astype(BF16)


def gate_kernel(place_ref, gain_ref, weight_ref, f0, f1, f2, f3, out_ref, open_ref):
    gain = gain_ref[...]
    for e, moved in enumerate((f0, f1, f2, f3)):
        for k in range(2):
            values = moved[k].astype(F32)
            centred = values - jnp.mean(values, axis=-1, keepdims=True)
            var_val = jnp.mean(centred * centred, axis=-1, keepdims=True)
            normed = (centred * lax.rsqrt(var_val + 1e-05) * gain).astype(BF16)
            opened = jax.nn.sigmoid(jnp.dot(normed, weight_ref[...], preferred_element_type=F32))
            base = (place_ref[4] if k == 0 else 1 - place_ref[4]) * 1600 + place_ref[e] * 400
            open_ref[pl.ds(pl.multiple_of(base, 16), 400), :] = opened
    for j in range(0, ROWS, 2):
        pair = [open_ref[pl.ds(((j + n) // COLS) * 1600 + (j + n) % COLS, HALF, stride=COLS), :] for n in range(2)]
        out_ref[pl.ds(j * HALF, ROWS), :] = jnp.concatenate(pair, axis=0).astype(BF16)


def output_kernel(pairs_ref, gate_ref, gain_ref, proj_ref, out_ref, prod_ref, tri_ref):
    widen(pairs_ref, {0: (tri_ref, 0), 1: (tri_ref, SPLIT)})
    for t in range(25):
        lanes = pl.ds(t * 128, 128)
        values = tri_ref[:, lanes]
        centred = values - jnp.mean(values, axis=0, keepdims=True)
        var_val = jnp.mean(centred * centred, axis=0, keepdims=True)
        normed = (centred * lax.rsqrt(var_val + 1e-05) * gain_ref[...]).astype(BF16)
        prod_ref[lanes, :] = lax.dot_general(normed, proj_ref[...], (((0,), (0,)), ((), ())), preferred_element_type=F32)
    for j in range(0, ROWS, 2):
        rows = pl.ds(j * HALF, ROWS)
        pair = jnp.concatenate([prod_ref[pl.ds(j + n, HALF, stride=ROWS), :] for n in range(2)], axis=0)
        out_ref[rows, :] = (pair * gate_ref[rows, :].astype(F32)).astype(BF16)


def plane_swap(chunks):
    return lax.all_to_all(chunks, PLANE, split_axis=0, concat_axis=0, tiled=True)


UP = [(i, (i + 1) % 4) for i in range(4)]
DOWN = [(i, (i - 1) % 4) for i in range(4)]


PAIRS = shape((128, 2, SPLIT))
WIDE = pltpu.VMEM((128, 2 * SPLIT), F32)
FLAT_WIDE = pltpu.VMEM((128, CELLS), F32)
TALL = pltpu.VMEM((1280, 128), F32)
FLAT = pltpu.VMEM((CELLS, CHANS), F32)


def edges(*args):
    return call(edges_kernel, (shape((CHANS, 2, CELLS)),), [pltpu.VMEM((CELLS, CHANS), BF16), FLAT], 8 * CELLS * CHANS * CHANS, args)


def left_unpack(pairs):
    return call(left_unpack_kernel, (shape((4, 320, 1280)),), [FLAT_WIDE, TALL], 10**7, (pairs,))


def right_unpack(pairs):
    return call(right_unpack_kernel, (shape((1280, 512)),), [FLAT_WIDE, TALL], 10**7, (pairs,))


def triangle(lefts, right):
    scratch = [pltpu.VMEM((4, 320, 128), F32), pltpu.VMEM((32, 2 * SPLIT), F32)]
    return call(triangle_kernel, (PAIRS,), scratch, 2 * 1280 * 1280 * 512, (lefts, right))


def output_gate(*args):
    return call(gate_kernel, (shape((CELLS, CHANS)),), [FLAT], 2 * CELLS * CHANS * CHANS, args)


def output(*args):
    return call(output_kernel, (shape((CELLS, CHANS)),), [FLAT, WIDE], 2 * CELLS * CHANS * CHANS, args)


def pick(parts, index):
    return lax.dynamic_index_in_dim(parts, index, 0, keepdims=False)


def swap_core(pair):
    core = lax.axis_index("core")
    other = lax.ppermute(pick(pair, 1 - core), "core", [(0, 1), (1, 0)])
    return jnp.stack([pick(pair, core), other], axis=1)


def spread_x(pieces):
    x = lax.axis_index("x")
    moved = [lax.ppermute(pick(pieces, (x + d) & 3), "x", [(i, (i + d) % 4) for i in range(4)]) for d in (1, 2, 3)]
    return [pick(pieces, x), *moved]


def cross_plane(parts, steps):
    x, zh = lax.axis_index("x"), lax.axis_index("zh")
    moved = []
    for n in steps:
        perm = []
        for yl in range(4):
            for h in range(4):
                for z0 in range(2):
                    for yh in range(2):
                        source = ((yl * 4 + h) * 2 + z0) * 2 + yh
                        target = (((z0 * 2 + yh) * 4 + (h + n) % 4) * 2 + yl // 2) * 2 + yl % 2
                        perm.append((source, target))
        moved.append(lax.ppermute(pick(parts, (x - zh - n) & 3), ("yl", "zh", "z0", "yh"), perm))
    return moved


def land_x(parts):
    x, zh = lax.axis_index("x"), lax.axis_index("zh")
    parts = jnp.stack(parts)
    return [
        part if e == 0 else lax.ppermute(part, "x", [(i, (i + e) % 4) for i in range(4)])
        for e, part in ((e, pick(parts, (zh - x - e) & 3)) for e in range(4))
    ]


def body(pair_repr, norm_gain, a_gate, a_proj, b_gate, b_proj, out_gate, out_proj, out_gain):
    x = lax.axis_index("x")
    gain = norm_gain.reshape(1, CHANS)
    pairs = plane_swap(edges(pair_repr.reshape(CELLS, CHANS), gain, a_gate, a_proj, b_gate, b_proj))
    spread = jnp.stack(spread_x(swap_core(pair_repr.reshape(2, 4, 400, CHANS))))
    pairs, spread = lax.optimization_barrier((pairs, spread))
    near, far = cross_plane(spread, (0, 1)), cross_plane(spread, (2, 3))
    own, right = left_unpack(pairs), right_unpack(pairs)
    lefts = lax.all_to_all(own, "x", split_axis=0, concat_axis=0)
    right, lefts, near, far = lax.optimization_barrier((right, lefts, near, far))
    slots = ((x - jnp.arange(4, dtype=jnp.int32)) & 3).astype(jnp.int32)
    tri = triangle(lefts, right)
    back = plane_swap(tri)
    place = jnp.concatenate([slots, lax.axis_index("core").astype(jnp.int32)[None]])
    gate = output_gate(place, gain, out_gate, *land_x([*near, *far]))
    update = output(back, gate, out_gain.reshape(CHANS, 1), out_proj)
    return update.reshape(ROWS, COLS, CHANS)


def solution(mesh):
    fine = Mesh(mesh.devices.reshape(4, 4, 4, 2, 2, 2), ("x", "yl", "zh", "z0", "yh", "core"))
    tile = P(("x", "yl"), ("zh", "z0", "yh", "core"), None)
    return jax.shard_map(
        body,
        mesh=fine,
        in_specs=(tile, P(), P(), P(), P(), P(), P(), P(), P()),
        out_specs=tile,
        check_vma=False,
    )
```

time: 183 us -> 171 us (0.934)
  waiting for transfers between devices: 95.3 us -> 65.6 us
  starting transfers between devices: 58 us -> 77.5 us
  Pallas kernels: 22.9 us -> 18.3 us
    all_to_all x3 -> x2, waiting for transfers between devices: 68.6 us -> 24.6 us  [plane_swap(): lax.all_to_all(chunks, PLANE, split_axis=0, concat_axis=0, tiled=True)]
    ppermute x4 -> x11, starting transfers between devices: 13 us -> 33.2 us  [the longest x4 10.7 us: cross_plane(): lax.ppermute(pick(parts, x - zh - n & 3), ('yl', 'zh', 'z0', 'yh'), perm)]
    all_to_all x1, waiting for transfers between devices: 5.41 us -> 16.5 us  [body(): lefts = lax.all_to_all(own, 'x', split_axis=0, concat_axis=0)]
    pallas_call x8 -> x6, Pallas kernels: 22.9 us -> 18.3 us  [call(): pl.pallas_call(kernel, out_shape=outs if len(outs) > 1 else outs[0], in_s...]
    ppermute x4 -> x11, waiting for transfers between devices: 21.3 us -> 24.4 us  [the longest x3 9.79 us: spread_x(): lax.ppermute(pick(pieces, x + d & 3), 'x', [(i, (i + d) % 4) for i in ran...]
    unnamed x34 -> x24, local copies, waits for them, and re-layouts: 4.89 us -> 6.56 us
    all_to_all x3 -> x2, starting transfers between devices: 41 us -> 39.6 us  [plane_swap(): lax.all_to_all(chunks, PLANE, split_axis=0, concat_axis=0, tiled=True)]
  transfers between devices with their start and end apart: 8 -> 14, of which waited for: 7 -> 11; matrix products, arithmetic and copies ran while one was open for 0% -> 1% of each run, Pallas kernels for 5% -> 2%
where the time goes in v2:
time: 171 us; the launch traced here: 170 us
  starting transfers between devices  77.5 us (45%)
  waiting for transfers between devices  65.6 us (38%)
  Pallas kernels  18.3 us (11%)
  local copies, waits for them, and re-layouts  6.86 us (4%)
    all_to_all x2, starting transfers between devices, plane_swap(): lax.all_to_all(chunks, PLANE, split_axis=0, concat_axis=0, tiled=True)  39.6 us
    all_to_all x2, waiting for transfers between devices, plane_swap(): lax.all_to_all(chunks, PLANE, split_axis=0, concat_axis=0, tiled=True)  24.6 us
    pallas_call x6, Pallas kernels, call(): pl.pallas_call(kernel, out_shape=outs if len(outs) > 1 else outs[0], in_s...  18.3 us
    all_to_all x1, waiting for transfers between devices, body(): lefts = lax.all_to_all(own, 'x', split_axis=0, concat_axis=0)  16.5 us
    ppermute x4, starting transfers between devices, cross_plane(): lax.ppermute(pick(parts, x - zh - n & 3), ('yl', 'zh', 'z0', 'yh'), perm)  10.7 us
    ppermute x3, starting transfers between devices, land_x(): lax.ppermute(part, 'x', [(i, (i + e) % 4) for i in range(4)])  10.4 us
    ppermute x3, waiting for transfers between devices, spread_x(): lax.ppermute(pick(pieces, x + d & 3), 'x', [(i, (i + d) % 4) for i in ran...  9.79 us
    ppermute x3, starting transfers between devices, spread_x(): lax.ppermute(pick(pieces, x + d & 3), 'x', [(i, (i + d) % 4) for i in ran...  9.33 us
  transfers between devices with their start and end apart: 14, of which 11 were waited for; matrix products, arithmetic and copies ran while one was open for 1% of the time, Pallas kernels for 2%

profile of v2, /device:TPU:1, one launch (start us, length us, event | category | flops | bytes accessed | tf_op | source)
XLA Modules:
  0.0 169.9 jit_solution(17263171780997824956)
XLA Ops:
  4.8 3.8 %shard_map.91 = bf16[128,2,3200]{2,1,0:T(2,128)(2,1)} custom-call(bf16[3200,128]{1,0:T(8,128)(2,1)S(1)} %bitcast.40, f32[1,128]{1,0:T(1,128)S(1)} %bitcast.42, bf16[128,128]{1,0:T(8,128)(2,1)S(1)} %copy-done.3, bf16[128,128]{1,0:T(8,128)(2,1)S(1)} %copy-done.4, bf16[128,128]{1,0:T(8,128)(2,1)S(1)} %copy-done.5, bf16[128,128]{1,0:T(8,128)(2,1)S(1)} %copy-done.6), custom_call_target="tpu_custom_call" | custom-call | flops 419430400 | bytes 2589184 | tf_op jit(solution)/shard_map/pallas_call | solution.py:20
  8.6 18.5 %all-to-all-start = ((bf16[128,2,3200]{2,1,0:T(2,128)(2,1)}), bf16[128,2,3200]{2,1,0:T(2,128)(2,1)S(1)}, u32[]{:S(2)}, u32[]{:S(2)}) async-start(bf16[128,2,3200]{2,1,0:T(2,128)(2,1)} %shard_map.91), calls=%async_computation | async-start | bytes 3276800 | tf_op jit(solution)/shard_map/all_to_all | solution.py:139
  27.3 2.8 %collective-permute-start = (bf16[4,400,128]{2,1,0:T(8,128)(2,1)S(1)}, bf16[4,400,128]{2,1,0:T(8,128)(2,1)S(1)}, u32[]{:S(2)}, u32[]{:S(2)}) collective-permute-start(bf16[4,400,128]{2,1,0:T(8,128)(2,1)S(1)} %get-tuple-element.33), channel_id=1, source_target_pairs={{0,1},{1,0},{2,3},{3,2},{4,5},{5,4},{6,7},{7,6},{8,9},{9,8},{10,11... | collective-permute-start | bytes 1228808 | tf_op jit(solution)/shard_map/ppermute | solution.py:184
  31.5 4.4 %collective-permute-start.3 = (bf16[2,400,128]{2,1,0:T(8,128)(2,1)S(1)}, bf16[2,400,128]{2,1,0:T(8,128)(2,1)S(1)}, u32[]{:S(2)}, u32[]{:S(2)}) collective-permute-start(bf16[2,400,128]{2,1,0:T(8,128)(2,1)S(1)} %get-tuple-element.32), channel_id=1, source_target_pairs={{0,384},{128,0},{256,128},{384,256},{1,385},{129,1},{257,129},{385... | collective-permute-start | bytes 614408 | tf_op jit(solution)/shard_map/ppermute | solution.py:190
  35.9 2.4 %collective-permute-start.2 = (bf16[2,400,128]{2,1,0:T(8,128)(2,1)S(1)}, bf16[2,400,128]{2,1,0:T(8,128)(2,1)S(1)}, u32[]{:S(2)}, u32[]{:S(2)}) collective-permute-start(bf16[2,400,128]{2,1,0:T(8,128)(2,1)S(1)} %get-tuple-element.31), channel_id=1, source_target_pairs={{0,256},{128,384},{256,0},{384,128},{1,257},{129,385},{257,1},{385... | collective-permute-start | bytes 614408 | tf_op jit(solution)/shard_map/ppermute | solution.py:190
  38.3 2.5 %collective-permute-start.1 = (bf16[2,400,128]{2,1,0:T(8,128)(2,1)S(1)}, bf16[2,400,128]{2,1,0:T(8,128)(2,1)S(1)}, u32[]{:S(2)}, u32[]{:S(2)}) collective-permute-start(bf16[2,400,128]{2,1,0:T(8,128)(2,1)S(1)} %get-tuple-element.30), channel_id=1, source_target_pairs={{0,128},{128,256},{256,384},{384,0},{1,129},{129,257},{257,385},{3... | collective-permute-start | bytes 614408 | tf_op jit(solution)/shard_map/ppermute | solution.py:190
  40.8 3.4 %collective-permute-done.3 = bf16[2,400,128]{2,1,0:T(8,128)(2,1)S(1)} collective-permute-done((bf16[2,400,128]{2,1,0:T(8,128)(2,1)S(1)}, bf16[2,400,128]{2,1,0:T(8,128)(2,1)S(1)}, u32[]{:S(2)}, u32[]{:S(2)}) %collective-permute-start.3) | collective-permute-done | bytes 204832 | tf_op jit(solution)/shard_map/ppermute | solution.py:190
  45.3 5.4 %collective-permute-done.1 = bf16[2,400,128]{2,1,0:T(8,128)(2,1)S(1)} collective-permute-done((bf16[2,400,128]{2,1,0:T(8,128)(2,1)S(1)}, bf16[2,400,128]{2,1,0:T(8,128)(2,1)S(1)}, u32[]{:S(2)}, u32[]{:S(2)}) %collective-permute-start.1) | collective-permute-done | bytes 204832 | tf_op jit(solution)/shard_map/ppermute | solution.py:190
  50.7 18.6 %all-to-all-done.pairs_ref = bf16[128,2,3200]{2,1,0:T(2,128)(2,1)S(1)} async-done(((bf16[128,2,3200]{2,1,0:T(2,128)(2,1)}), bf16[128,2,3200]{2,1,0:T(2,128)(2,1)S(1)}, u32[]{:S(2)}, u32[]{:S(2)}) %all-to-all-start) | async-done | bytes 1638432 | tf_op jit(solution)/shard_map/all_to_all | solution.py:139
  73.1 4.7 %all-to-all-start.1 = ((bf16[4,320,1280]{2,1,0:T(8,128)(2,1)}), bf16[4,320,1280]{2,1,0:T(8,128)(2,1)}, u32[]{:S(2)}, u32[]{:S(2)}) async-start(bf16[4,320,1280]{2,1,0:T(8,128)(2,1)} %copy-done), calls=%async_computation.1 | async-start | bytes 6553600 | tf_op jit(solution)/shard_map/all_to_all | solution.py:227
  78.6 2.4 %collective-permute-start.5 = (bf16[2,400,128]{2,1,0:T(8,128)(2,1)S(1)}, bf16[2,400,128]{2,1,0:T(8,128)(2,1)S(1)}, u32[]{:S(2)}, u32[]{:S(2)}) collective-permute-start(bf16[2,400,128]{2,1,0:T(8,128)(2,1)S(1)} %get-tuple-element.27), channel_id=1, source_target_pairs={{0,8},{2,40},{4,72},{6,104},{8,16},{10,48},{12,80},{14,112},{16,24... | collective-permute-start | bytes 614408 | tf_op jit(solution)/shard_map/ppermute | solution.py:206
  81.0 4.5 %collective-permute-start.6 = (bf16[2,400,128]{2,1,0:T(8,128)(2,1)S(1)}, bf16[2,400,128]{2,1,0:T(8,128)(2,1)}, u32[]{:S(2)}, u32[]{:S(2)}) collective-permute-start(bf16[2,400,128]{2,1,0:T(8,128)(2,1)S(1)} %get-tuple-element.26), channel_id=1, source_target_pairs={{0,16},{2,48},{4,80},{6,112},{8,24},{10,56},{12,88},{14,120},{16,0... | collective-permute-start | bytes 614408 | tf_op jit(solution)/shard_map/ppermute | solution.py:206
  85.5 3.2 %collective-permute-start.7 = (bf16[2,400,128]{2,1,0:T(8,128)(2,1)S(1)}, bf16[2,400,128]{2,1,0:T(8,128)(2,1)}, u32[]{:S(2)}, u32[]{:S(2)}) collective-permute-start(bf16[2,400,128]{2,1,0:T(8,128)(2,1)S(1)} %get-tuple-element.25), channel_id=1, source_target_pairs={{0,24},{2,56},{4,88},{6,120},{8,0},{10,32},{12,64},{14,96},{16,8},... | collective-permute-start | bytes 614408 | tf_op jit(solution)/shard_map/ppermute | solution.py:206
  90.7 4.4 %collective-permute-done.5 = bf16[2,400,128]{2,1,0:T(8,128)(2,1)S(1)} collective-permute-done((bf16[2,400,128]{2,1,0:T(8,128)(2,1)S(1)}, bf16[2,400,128]{2,1,0:T(8,128)(2,1)S(1)}, u32[]{:S(2)}, u32[]{:S(2)}) %collective-permute-start.5) | collective-permute-done | bytes 204832 | tf_op jit(solution)/shard_map/ppermute | solution.py:206
  95.1 3.4 %collective-permute-done.6 = bf16[2,400,128]{2,1,0:T(8,128)(2,1)} collective-permute-done((bf16[2,400,128]{2,1,0:T(8,128)(2,1)S(1)}, bf16[2,400,128]{2,1,0:T(8,128)(2,1)}, u32[]{:S(2)}, u32[]{:S(2)}) %collective-permute-start.6) | collective-permute-done | bytes 204832 | tf_op jit(solution)/shard_map/ppermute | solution.py:206
  98.5 16.5 %all-to-all-done.1.lefts_ref = bf16[4,320,1280]{2,1,0:T(8,128)(2,1)} async-done(((bf16[4,320,1280]{2,1,0:T(8,128)(2,1)}), bf16[4,320,1280]{2,1,0:T(8,128)(2,1)}, u32[]{:S(2)}, u32[]{:S(2)}) %all-to-all-start.1) | async-done | bytes 3276832 | tf_op jit(solution)/shard_map/all_to_all | solution.py:227
  115.1 4.9 %shard_map.94 = bf16[128,2,1664]{2,1,0:T(2,128)(2,1)} custom-call(bf16[4,320,1280]{2,1,0:T(8,128)(2,1)} %all-to-all-done.1.lefts_ref, bf16[1280,512]{1,0:T(8,128)(2,1)S(1)} %shard_map.92.right_ref), custom_call_target="tpu_custom_call" | custom-call | flops 1677721600 | bytes 5439488 | tf_op jit(solution)/shard_map/pallas_call | solution.py:20
  120.0 21.1 %all-to-all-start.2 = ((bf16[128,2,1664]{2,1,0:T(2,128)(2,1)}), bf16[128,2,1664]{2,1,0:T(2,128)(2,1)S(1)}, u32[]{:S(2)}, u32[]{:S(2)}) async-start(bf16[128,2,1664]{2,1,0:T(2,128)(2,1)} %shard_map.94), calls=%async_computation.2 | async-start | bytes 1703936 | tf_op jit(solution)/shard_map/all_to_all | solution.py:139
  142.5 3.0 %collective-permute-start.8 = (bf16[2,400,128]{2,1,0:T(8,128)(2,1)S(1)}, bf16[2,400,128]{2,1,0:T(8,128)(2,1)S(1)}, u32[]{:S(2)}, u32[]{:S(2)}) collective-permute-start(bf16[2,400,128]{2,1,0:T(8,128)(2,1)S(1)} %get-tuple-element.23), channel_id=1, source_target_pairs={{0,128},{128,256},{256,384},{384,0},{1,129},{129,257},{257,385},{3... | collective-permute-start | bytes 614408 | tf_op jit(solution)/shard_map/ppermute | solution.py:214
  145.5 4.3 %collective-permute-start.9 = (bf16[2,400,128]{2,1,0:T(8,128)(2,1)S(1)}, bf16[2,400,128]{2,1,0:T(8,128)(2,1)S(1)}, u32[]{:S(2)}, u32[]{:S(2)}) collective-permute-start(bf16[2,400,128]{2,1,0:T(8,128)(2,1)S(1)} %get-tuple-element.22), channel_id=1, source_target_pairs={{0,256},{128,384},{256,0},{384,128},{1,257},{129,385},{257,1},{385... | collective-permute-start | bytes 614408 | tf_op jit(solution)/shard_map/ppermute | solution.py:214
  149.8 3.1 %collective-permute-start.10 = (bf16[2,400,128]{2,1,0:T(8,128)(2,1)S(1)}, bf16[2,400,128]{2,1,0:T(8,128)(2,1)S(1)}, u32[]{:S(2)}, u32[]{:S(2)}) collective-permute-start(bf16[2,400,128]{2,1,0:T(8,128)(2,1)S(1)} %get-tuple-element.21), channel_id=1, source_target_pairs={{0,384},{128,0},{256,128},{384,256},{1,385},{129,1},{257,129},{385... | collective-permute-start | bytes 614408 | tf_op jit(solution)/shard_map/ppermute | solution.py:214
  153.0 3.5 %collective-permute-done.9.f2 = bf16[2,400,128]{2,1,0:T(8,128)(2,1)S(1)} collective-permute-done((bf16[2,400,128]{2,1,0:T(8,128)(2,1)S(1)}, bf16[2,400,128]{2,1,0:T(8,128)(2,1)S(1)}, u32[]{:S(2)}, u32[]{:S(2)}) %collective-permute-start.9) | collective-permute-done | bytes 204832 | tf_op jit(solution)/shard_map/ppermute | solution.py:214
  160.5 6.1 %all-to-all-done.2.pairs_ref = bf16[128,2,1664]{2,1,0:T(2,128)(2,1)S(1)} async-done(((bf16[128,2,1664]{2,1,0:T(2,128)(2,1)}), bf16[128,2,1664]{2,1,0:T(2,128)(2,1)S(1)}, u32[]{:S(2)}, u32[]{:S(2)}) %all-to-all-start.2) | async-done | bytes 852000 | tf_op jit(solution)/shard_map/all_to_all | solution.py:139
  166.6 3.3 %shard_map.96 = bf16[3200,128]{1,0:T(8,128)(2,1)} custom-call(bf16[128,2,1664]{2,1,0:T(2,128)(2,1)S(1)} %all-to-all-done.2.pairs_ref, bf16[3200,128]{1,0:T(8,128)(2,1)S(1)} %shard_map.95.gate_ref, f32[128,1]{1,0:T(8,128)S(1)} %copy.10.gain_ref, bf16[128,128]{1,0:T(8,128)(2,1)S(1)} %copy-done.7), custom_call_target="tpu_custom_call" | custom-call | flops 104857600 | bytes 2523648 | tf_op jit(solution)/shard_map/pallas_call | solution.py:20
  (43 shorter events, 19.5 us)
Async XLA Ops:
  0.0 1.1 copy-start.1
  1.1 0.8 copy-start.3
  1.9 0.8 copy-start.4
  2.7 0.8 copy-start.5
  8.6 18.6 %copy-start.2 = (bf16[80,40,128]{2,1,0:T(8,128)(2,1)S(1)}, bf16[80,40,128]{2,1,0:T(8,128)(2,1)}, u32[]{:S(2)}) copy-start(bf16[80,40,128]{2,1,0:T(8,128)(2,1)} %param.9) | copy-start | bytes 2457604
  8.6 60.7 %all-to-all-start = ((bf16[128,2,3200]{2,1,0:T(2,128)(2,1)}), bf16[128,2,3200]{2,1,0:T(2,128)(2,1)S(1)}, u32[]{:S(2)}, u32[]{:S(2)}) async-start(bf16[128,2,3200]{2,1,0:T(2,128)(2,1)} %shard_map.91), calls=%async_computation | async-start | bytes 3276800 | tf_op jit(solution)/shard_map/all_to_all | solution.py:139
  27.3 4.2 %collective-permute-start = (bf16[4,400,128]{2,1,0:T(8,128)(2,1)S(1)}, bf16[4,400,128]{2,1,0:T(8,128)(2,1)S(1)}, u32[]{:S(2)}, u32[]{:S(2)}) collective-permute-start(bf16[4,400,128]{2,1,0:T(8,128)(2,1)S(1)} %get-tuple-element.33), channel_id=1, source_target_pairs={{0,1},{1,0},{2,3},{3,2},{4,5},{5,4},{6,7},{7,6},{8,9},{9,8},{10,11... | collective-permute-start | bytes 1228808 | tf_op jit(solution)/shard_map/ppermute | solution.py:184
  31.5 12.7 %collective-permute-start.3 = (bf16[2,400,128]{2,1,0:T(8,128)(2,1)S(1)}, bf16[2,400,128]{2,1,0:T(8,128)(2,1)S(1)}, u32[]{:S(2)}, u32[]{:S(2)}) collective-permute-start(bf16[2,400,128]{2,1,0:T(8,128)(2,1)S(1)} %get-tuple-element.32), channel_id=1, source_target_pairs={{0,384},{128,0},{256,128},{384,256},{1,385},{129,1},{257,129},{385... | collective-permute-start | bytes 614408 | tf_op jit(solution)/shard_map/ppermute | solution.py:190
  35.9 9.4 %collective-permute-start.2 = (bf16[2,400,128]{2,1,0:T(8,128)(2,1)S(1)}, bf16[2,400,128]{2,1,0:T(8,128)(2,1)S(1)}, u32[]{:S(2)}, u32[]{:S(2)}) collective-permute-start(bf16[2,400,128]{2,1,0:T(8,128)(2,1)S(1)} %get-tuple-element.31), channel_id=1, source_target_pairs={{0,256},{128,384},{256,0},{384,128},{1,257},{129,385},{257,1},{385... | collective-permute-start | bytes 614408 | tf_op jit(solution)/shard_map/ppermute | solution.py:190
  38.3 12.3 %collective-permute-start.1 = (bf16[2,400,128]{2,1,0:T(8,128)(2,1)S(1)}, bf16[2,400,128]{2,1,0:T(8,128)(2,1)S(1)}, u32[]{:S(2)}, u32[]{:S(2)}) collective-permute-start(bf16[2,400,128]{2,1,0:T(8,128)(2,1)S(1)} %get-tuple-element.30), channel_id=1, source_target_pairs={{0,128},{128,256},{256,384},{384,0},{1,129},{129,257},{257,385},{3... | collective-permute-start | bytes 614408 | tf_op jit(solution)/shard_map/ppermute | solution.py:190
  71.4 1.7 %copy-start = (bf16[4,320,1280]{2,1,0:T(8,128)(2,1)}, bf16[4,320,1280]{2,1,0:T(8,128)(2,1)S(1)}, u32[]{:S(2)}) copy-start(bf16[4,320,1280]{2,1,0:T(8,128)(2,1)S(1)} %shard_map.93) | copy-start | bytes 9830404
  73.1 41.9 %all-to-all-start.1 = ((bf16[4,320,1280]{2,1,0:T(8,128)(2,1)}), bf16[4,320,1280]{2,1,0:T(8,128)(2,1)}, u32[]{:S(2)}, u32[]{:S(2)}) async-start(bf16[4,320,1280]{2,1,0:T(8,128)(2,1)} %copy-done), calls=%async_computation.1 | async-start | bytes 6553600 | tf_op jit(solution)/shard_map/all_to_all | solution.py:227
  77.9 12.8 %collective-permute-start.4 = (bf16[2,400,128]{2,1,0:T(8,128)(2,1)S(1)}, bf16[2,400,128]{2,1,0:T(8,128)(2,1)S(1)}, u32[]{:S(2)}, u32[]{:S(2)}) collective-permute-start(bf16[2,400,128]{2,1,0:T(8,128)(2,1)S(1)} %get-tuple-element.28), channel_id=1, source_target_pairs={{0,0},{2,32},{4,64},{6,96},{8,8},{10,40},{12,72},{14,104},{16,16},... | collective-permute-start | bytes 614408 | tf_op jit(solution)/shard_map/ppermute | solution.py:206
  78.6 16.5 %collective-permute-start.5 = (bf16[2,400,128]{2,1,0:T(8,128)(2,1)S(1)}, bf16[2,400,128]{2,1,0:T(8,128)(2,1)S(1)}, u32[]{:S(2)}, u32[]{:S(2)}) collective-permute-start(bf16[2,400,128]{2,1,0:T(8,128)(2,1)S(1)} %get-tuple-element.27), channel_id=1, source_target_pairs={{0,8},{2,40},{4,72},{6,104},{8,16},{10,48},{12,80},{14,112},{16,24... | collective-permute-start | bytes 614408 | tf_op jit(solution)/shard_map/ppermute | solution.py:206
  81.0 17.5 %collective-permute-start.6 = (bf16[2,400,128]{2,1,0:T(8,128)(2,1)S(1)}, bf16[2,400,128]{2,1,0:T(8,128)(2,1)}, u32[]{:S(2)}, u32[]{:S(2)}) collective-permute-start(bf16[2,400,128]{2,1,0:T(8,128)(2,1)S(1)} %get-tuple-element.26), channel_id=1, source_target_pairs={{0,16},{2,48},{4,80},{6,112},{8,24},{10,56},{12,88},{14,120},{16,0... | collective-permute-start | bytes 614408 | tf_op jit(solution)/shard_map/ppermute | solution.py:206
  85.5 13.1 %collective-permute-start.7 = (bf16[2,400,128]{2,1,0:T(8,128)(2,1)S(1)}, bf16[2,400,128]{2,1,0:T(8,128)(2,1)}, u32[]{:S(2)}, u32[]{:S(2)}) collective-permute-start(bf16[2,400,128]{2,1,0:T(8,128)(2,1)S(1)} %get-tuple-element.25), channel_id=1, source_target_pairs={{0,24},{2,56},{4,88},{6,120},{8,0},{10,32},{12,64},{14,96},{16,8},... | collective-permute-start | bytes 614408 | tf_op jit(solution)/shard_map/ppermute | solution.py:206
  120.0 21.1 %copy-start.11 = (f32[128]{0:T(128)S(1)}, f32[128]{0:T(128)}, u32[]{:S(2)}) copy-start(f32[128]{0:T(128)} %param.17) | copy-start | bytes 1540
  120.0 46.6 %all-to-all-start.2 = ((bf16[128,2,1664]{2,1,0:T(2,128)(2,1)}), bf16[128,2,1664]{2,1,0:T(2,128)(2,1)S(1)}, u32[]{:S(2)}, u32[]{:S(2)}) async-start(bf16[128,2,1664]{2,1,0:T(2,128)(2,1)} %shard_map.94), calls=%async_computation.2 | async-start | bytes 1703936 | tf_op jit(solution)/shard_map/all_to_all | solution.py:139
  141.2 17.1 %copy-start.8 = (bf16[128,128]{1,0:T(8,128)(2,1)S(1)}, bf16[128,128]{1,0:T(8,128)(2,1)}, u32[]{:S(2)}) copy-start(bf16[128,128]{1,0:T(8,128)(2,1)} %weight_ref.1) | copy-start | bytes 98308
  141.2 17.1 %copy-start.10 = (f32[128]{0:T(128)S(1)}, f32[128]{0:T(128)}, u32[]{:S(2)}) copy-start(f32[128]{0:T(128)} %param.10) | copy-start | bytes 1540
  142.4 24.2 %copy-start.7 = (bf16[128,128]{1,0:T(8,128)(2,1)S(1)}, bf16[128,128]{1,0:T(8,128)(2,1)}, u32[]{:S(2)}) copy-start(bf16[128,128]{1,0:T(8,128)(2,1)} %proj_ref.1) | copy-start | bytes 98308
  142.5 10.5 %collective-permute-start.8 = (bf16[2,400,128]{2,1,0:T(8,128)(2,1)S(1)}, bf16[2,400,128]{2,1,0:T(8,128)(2,1)S(1)}, u32[]{:S(2)}, u32[]{:S(2)}) collective-permute-start(bf16[2,400,128]{2,1,0:T(8,128)(2,1)S(1)} %get-tuple-element.23), channel_id=1, source_target_pairs={{0,128},{128,256},{256,384},{384,0},{1,129},{129,257},{257,385},{3... | collective-permute-start | bytes 614408 | tf_op jit(solution)/shard_map/ppermute | solution.py:214
  145.5 11.0 %collective-permute-start.9 = (bf16[2,400,128]{2,1,0:T(8,128)(2,1)S(1)}, bf16[2,400,128]{2,1,0:T(8,128)(2,1)S(1)}, u32[]{:S(2)}, u32[]{:S(2)}) collective-permute-start(bf16[2,400,128]{2,1,0:T(8,128)(2,1)S(1)} %get-tuple-element.22), channel_id=1, source_target_pairs={{0,256},{128,384},{256,0},{384,128},{1,257},{129,385},{257,1},{385... | collective-permute-start | bytes 614408 | tf_op jit(solution)/shard_map/ppermute | solution.py:214
  149.8 8.6 %collective-permute-start.10 = (bf16[2,400,128]{2,1,0:T(8,128)(2,1)S(1)}, bf16[2,400,128]{2,1,0:T(8,128)(2,1)S(1)}, u32[]{:S(2)}, u32[]{:S(2)}) collective-permute-start(bf16[2,400,128]{2,1,0:T(8,128)(2,1)S(1)} %get-tuple-element.21), channel_id=1, source_target_pairs={{0,384},{128,0},{256,128},{384,256},{1,385},{129,1},{257,129},{385... | collective-permute-start | bytes 614408 | tf_op jit(solution)/shard_map/ppermute | solution.py:214
  (2 other events, 1.4 us)

commit v3 on v2

--- a/solution.py
+++ b/solution.py
@@ -13,17 +13,18 @@
 HALF = ROWS // 2
 SPLIT = 13 * 128
 VMEM_LIMIT = 20 * 1024 * 1024
-
-
-def call(kernel, outs, scratch, flops, args):
+VMEM_MOST = 56 * 1024 * 1024
+
+
+def call(kernel, outs, scratch, flops, args, far=(), limit=VMEM_LIMIT):
     moved = sum(a.size * a.dtype.itemsize for a in (*args, *outs))
     return pl.pallas_call(
         kernel,
         out_shape=outs if len(outs) > 1 else outs[0],
-        in_specs=[pl.BlockSpec(memory_space=pltpu.SMEM if a.dtype == jnp.int32 else pltpu.VMEM) for a in args],
-        out_specs=[pl.BlockSpec(memory_space=pltpu.VMEM)] * len(outs) if len(outs) > 1 else pl.BlockSpec(memory_space=pltpu.VMEM),
+        in_specs=[pl.BlockSpec(memory_space=pl.ANY if n in far else pltpu.SMEM if a.dtype == jnp.int32 else pltpu.VMEM) for n, a in enumerate(args)],
+        out_specs=[pl.BlockSpec(memory_space=pltpu.VMEM)] * len(outs) if len(outs) > 1 else pl.BlockSpec(memory_space=pl.ANY if -1 in far else pltpu.VMEM),
         scratch_shapes=scratch,
-        compiler_params=pltpu.CompilerParams(vmem_limit_bytes=VMEM_LIMIT),
+        compiler_params=pltpu.CompilerParams(vmem_limit_bytes=limit),
         cost_estimate=pl.CostEstimate(flops=flops, bytes_accessed=moved, transcendentals=0),
     )(*args)
 
@@ -36,14 +37,28 @@
     return lax.dot_general(weight, cells, (((0,), (1,)), ((), ())), preferred_element_type=F32)
 
 
-def edges_kernel(z_ref, gain_ref, a_gate, a_proj, b_gate, b_proj, pairs_ref, normed_ref, rows_ref):
+def edges_kernel(*refs):
+    sources, pairs_ref, landed, normed_ref, rows_ref, sems = refs[:6], refs[6], refs[7:13], refs[13], refs[14], refs[15]
+    z_ref, gain_ref, a_gate, a_proj, b_gate, b_proj = landed
+    copies = [pltpu.make_async_copy(source, target, sems.at[n]) for n, (source, target) in enumerate(zip(sources[1:], landed[1:]))]
+    parts = [
+        pltpu.make_async_copy(sources[0].at[pl.ds(t * 640, 640), :], z_ref.at[pl.ds(t * 640, 640), :], sems.at[5 + t])
+        for t in range(5)
+    ]
+    for copy in (*parts, *copies):
+        copy.start()
+    copies[0].wait()
     gain = gain_ref[...]
     for t in range(10):
         part = pl.ds(t * 320, 320)
+        if t % 2 == 0:
+            parts[t // 2].wait()
         values = z_ref[part, :].astype(F32)
         centred = values - jnp.mean(values, axis=-1, keepdims=True)
         var_val = jnp.mean(centred * centred, axis=-1, keepdims=True)
         rows_ref[part, :] = centred * lax.rsqrt(var_val + 1e-05) * gain
+    for copy in copies[1:]:
+        copy.wait()
     for k in range(COLS):
         normed_ref[pl.ds(k * ROWS, ROWS), :] = rows_ref[pl.ds(k, ROWS, stride=COLS), :].astype(BF16)
     for t in range(5):
@@ -71,15 +86,20 @@
             tall_ref[pl.ds(k * 32 + zh * 8, 8), 0:ROWS] = wide_ref[pl.ds(zh * 32 + yl * 8, 8), pl.ds(k * ROWS, ROWS)]
 
 
-def left_unpack_kernel(pairs_ref, out_ref, wide_ref, tall_ref):
+def left_unpack_kernel(pairs_ref, out_ref, wide_ref, tall_ref, own_ref, sems):
+    copies = []
     widen(pairs_ref, {0: (wide_ref, 0)})
     for yl in range(4):
         lay_out(wide_ref, tall_ref, yl)
         for t in range(10):
             block = jnp.transpose(tall_ref[pl.ds(t * 128, 128), :])
-            block = block[:ROWS].astype(BF16)
-            for copy in range(4):
-                out_ref[copy, pl.ds(yl * ROWS, ROWS), pl.ds(t * 128, 128)] = block
+            own_ref[pl.ds(yl * ROWS, ROWS), pl.ds(t * 128, 128)] = block[:ROWS].astype(BF16)
+        rows = pl.ds(yl * ROWS, ROWS)
+        for x in range(4):
+            copies.append(pltpu.make_async_copy(own_ref.at[rows, :], out_ref.at[x, rows, :], sems.at[yl * 4 + x]))
+            copies[-1].start()
+    for copy in copies:
+        copy.wait()
 
 
 def right_unpack_kernel(pairs_ref, out_ref, wide_ref, tall_ref):
@@ -90,10 +110,14 @@
         out_ref[:, pl.ds(yl * 128, 128)] = tall_ref[...].astype(BF16)
 
 
-def triangle_kernel(lefts_ref, right_ref, out_ref, prod_ref, wide_ref):
+def triangle_kernel(lefts_hbm, right_ref, out_ref, prod_ref, wide_ref, lefts_ref, sems):
+    copies = [pltpu.make_async_copy(lefts_hbm.at[n], lefts_ref.at[n], sems.at[n]) for n in range(4)]
+    for copy in copies:
+        copy.start()
     right = right_ref[...]
     wide_ref[:, CELLS : 2 * SPLIT] = jnp.zeros((32, 2 * SPLIT - CELLS), F32)
     for n in range(4):
+        copies[n].wait()
         prod = jnp.dot(lefts_ref[n], right, preferred_element_type=F32)
         for yl in range(4):
             prod_ref[yl] = prod[:, yl * 128 : (yl + 1) * 128]
@@ -151,11 +175,13 @@
 
 
 def edges(*args):
-    return call(edges_kernel, (shape((CHANS, 2, CELLS)),), [pltpu.VMEM((CELLS, CHANS), BF16), FLAT], 8 * CELLS * CHANS * CHANS, args)
+    landing = [pltpu.VMEM(a.shape, a.dtype) for a in args]
+    scratch = [*landing, pltpu.VMEM((CELLS, CHANS), BF16), FLAT, pltpu.SemaphoreType.DMA((10,))]
+    return call(edges_kernel, (shape((CHANS, 2, CELLS)),), scratch, 8 * CELLS * CHANS * CHANS, args, range(6), VMEM_MOST)
 
 
 def left_unpack(pairs):
-    return call(left_unpack_kernel, (shape((4, 320, 1280)),), [FLAT_WIDE, TALL], 10**7, (pairs,))
+    return call(left_unpack_kernel, (shape((4, 320, 1280)),), [FLAT_WIDE, TALL, pltpu.VMEM((320, 1280), BF16), pltpu.SemaphoreType.DMA((16,))], 10**7, (pairs,), (-1,), VMEM_MOST)
 
 
 def right_unpack(pairs):
@@ -163,8 +189,8 @@
 
 
 def triangle(lefts, right):
-    scratch = [pltpu.VMEM((4, 320, 128), F32), pltpu.VMEM((32, 2 * SPLIT), F32)]
-    return call(triangle_kernel, (PAIRS,), scratch, 2 * 1280 * 1280 * 512, (lefts, right))
+    scratch = [pltpu.VMEM((4, 320, 128), F32), pltpu.VMEM((32, 2 * SPLIT), F32), pltpu.VMEM((4, 320, 1280), BF16), pltpu.SemaphoreType.DMA((4,))]
+    return call(triangle_kernel, (PAIRS,), scratch, 2 * 1280 * 1280 * 512, (lefts, right), (0,))
 
 
 def output_gate(*args):
@@ -225,9 +251,9 @@
     near, far = cross_plane(spread, (0, 1)), cross_plane(spread, (2, 3))
     own, right = left_unpack(pairs), right_unpack(pairs)
     lefts = lax.all_to_all(own, "x", split_axis=0, concat_axis=0)
-    right, lefts, near, far = lax.optimization_barrier((right, lefts, near, far))
     slots = ((x - jnp.arange(4, dtype=jnp.int32)) & 3).astype(jnp.int32)
     tri = triangle(lefts, right)
+    tri, near, far = lax.optimization_barrier((tri, near, far))
     back = plane_swap(tri)
     place = jnp.concatenate([slots, lax.axis_index("core").astype(jnp.int32)[None]])
     gate = output_gate(place, gain, out_gate, *land_x([*near, *far]))

time: 171 us -> 163 us (0.953)
  starting transfers between devices: 77.5 us -> 71.2 us
  Pallas kernels: 18.3 us -> 22.9 us
  local copies, waits for them, and re-layouts: 6.86 us -> 3.33 us
  waiting for transfers between devices: 65.6 us -> 62.4 us
    all_to_all x2, starting transfers between devices: 39.6 us -> 31.1 us  [plane_swap(): lax.all_to_all(chunks, PLANE, split_axis=0, concat_axis=0, tiled=True)]
    ppermute x4, waiting for transfers between devices: 7.84 us -> 0.01 us  [cross_plane(): lax.ppermute(pick(parts, x - zh - n & 3), ('yl', 'zh', 'z0', 'yh'), perm)]
    all_to_all x1, waiting for transfers between devices: 16.5 us -> 21.3 us  [body(): lefts = lax.all_to_all(own, 'x', split_axis=0, concat_axis=0)]
    pallas_call x6, Pallas kernels: 18.3 us -> 22.9 us  [call(): pl.pallas_call(kernel, out_shape=outs if len(outs) > 1 else outs[0], in_s...]
    unnamed x24 -> x16, local copies, waits for them, and re-layouts: 6.56 us -> 2.16 us
    ppermute x3, waiting for transfers between devices: 9.79 us -> 5.66 us  [spread_x(): lax.ppermute(pick(pieces, x + d & 3), 'x', [(i, (i + d) % 4) for i in ran...]
    ppermute x3, waiting for transfers between devices: 5.39 us -> 9.04 us  [land_x(): lax.ppermute(part, 'x', [(i, (i + e) % 4) for i in range(4)])]
    ppermute x4, starting transfers between devices: 10.7 us -> 12.9 us  [cross_plane(): lax.ppermute(pick(parts, x - zh - n & 3), ('yl', 'zh', 'z0', 'yh'), perm)]
  transfers between devices with their start and end apart: 14 -> 14, of which waited for: 11 -> 8; matrix products, arithmetic and copies ran while one was open for 1% -> 2% of each run, Pallas kernels for 2% -> 5%
where the time goes in v3:
time: 163 us; the launch traced here: 162 us
  starting transfers between devices  71.2 us (44%)
  waiting for transfers between devices  62.4 us (38%)
  Pallas kernels  22.9 us (14%)
  local copies, waits for them, and re-layouts  3.33 us (2%)
    all_to_all x2, starting transfers between devices, plane_swap(): lax.all_to_all(chunks, PLANE, split_axis=0, concat_axis=0, tiled=True)  31.1 us
    all_to_all x2, waiting for transfers between devices, plane_swap(): lax.all_to_all(chunks, PLANE, split_axis=0, concat_axis=0, tiled=True)  25.1 us
    pallas_call x6, Pallas kernels, call(): pl.pallas_call(kernel, out_shape=outs if len(outs) > 1 else outs[0], in_s...  22.9 us
    all_to_all x1, waiting for transfers between devices, body(): lefts = lax.all_to_all(own, 'x', split_axis=0, concat_axis=0)  21.3 us
    ppermute x4, starting transfers between devices, cross_plane(): lax.ppermute(pick(parts, x - zh - n & 3), ('yl', 'zh', 'z0', 'yh'), perm)  12.9 us
    ppermute x3, starting transfers between devices, spread_x(): lax.ppermute(pick(pieces, x + d & 3), 'x', [(i, (i + d) % 4) for i in ran...  10.5 us
    ppermute x3, starting transfers between devices, land_x(): lax.ppermute(part, 'x', [(i, (i + e) % 4) for i in range(4)])  9.2 us
    ppermute x3, waiting for transfers between devices, land_x(): lax.ppermute(part, 'x', [(i, (i + e) % 4) for i in range(4)])  9.04 us
  transfers between devices with their start and end apart: 14, of which 8 were waited for; matrix products, arithmetic and copies ran while one was open for 2% of the time, Pallas kernels for 5%

profile of v3, /device:TPU:1, one launch (start us, length us, event | category | flops | bytes accessed | tf_op | source)
XLA Modules:
  0.0 161.6 jit_solution(4897938463277155182)
XLA Ops:
  0.0 5.8 %shard_map.91 = bf16[128,2,3200]{2,1,0:T(2,128)(2,1)} custom-call(bf16[3200,128]{1,0:T(8,128)(2,1)} %bitcast.42, f32[1,128]{1,0:T(1,128)} %bitcast.40, bf16[128,128]{1,0:T(8,128)(2,1)} %refs_2_.1, bf16[128,128]{1,0:T(8,128)(2,1)} %refs_3_.1, bf16[128,128]{1,0:T(8,128)(2,1)} %refs_4_.1, bf16[128,128]{1,0:T(8,128)(2,1)} %refs_5_.1), custom_call_target="tpu_custom_call" | custom-call | flops 419430400 | bytes 2589184 | tf_op jit(solution)/shard_map/pallas_call | solution.py:21
  5.8 18.6 %all-to-all-start = ((bf16[128,2,3200]{2,1,0:T(2,128)(2,1)}), bf16[128,2,3200]{2,1,0:T(2,128)(2,1)S(1)}, u32[]{:S(2)}, u32[]{:S(2)}) async-start(bf16[128,2,3200]{2,1,0:T(2,128)(2,1)} %shard_map.91), calls=%async_computation | async-start | bytes 3276800 | tf_op jit(solution)/shard_map/all_to_all | solution.py:163
  24.4 2.8 %collective-permute-start = (bf16[4,400,128]{2,1,0:T(8,128)(2,1)S(1)}, bf16[4,400,128]{2,1,0:T(8,128)(2,1)S(1)}, u32[]{:S(2)}, u32[]{:S(2)}) collective-permute-start(bf16[4,400,128]{2,1,0:T(8,128)(2,1)S(1)} %get-tuple-element.31), channel_id=1, source_target_pairs={{0,1},{1,0},{2,3},{3,2},{4,5},{5,4},{6,7},{7,6},{8,9},{9,8},{10,11... | collective-permute-start | bytes 1228808 | tf_op jit(solution)/shard_map/ppermute | solution.py:210
  28.7 3.1 %collective-permute-start.1 = (bf16[2,400,128]{2,1,0:T(8,128)(2,1)S(1)}, bf16[2,400,128]{2,1,0:T(8,128)(2,1)S(1)}, u32[]{:S(2)}, u32[]{:S(2)}) collective-permute-start(bf16[2,400,128]{2,1,0:T(8,128)(2,1)S(1)} %get-tuple-element.28), channel_id=1, source_target_pairs={{0,128},{128,256},{256,384},{384,0},{1,129},{129,257},{257,385},{3... | collective-permute-start | bytes 614408 | tf_op jit(solution)/shard_map/ppermute | solution.py:216
  31.8 4.4 %collective-permute-start.2 = (bf16[2,400,128]{2,1,0:T(8,128)(2,1)S(1)}, bf16[2,400,128]{2,1,0:T(8,128)(2,1)S(1)}, u32[]{:S(2)}, u32[]{:S(2)}) collective-permute-start(bf16[2,400,128]{2,1,0:T(8,128)(2,1)S(1)} %get-tuple-element.29), channel_id=1, source_target_pairs={{0,256},{128,384},{256,0},{384,128},{1,257},{129,385},{257,1},{385... | collective-permute-start | bytes 614408 | tf_op jit(solution)/shard_map/ppermute | solution.py:216
  36.2 3.1 %collective-permute-start.3 = (bf16[2,400,128]{2,1,0:T(8,128)(2,1)S(1)}, bf16[2,400,128]{2,1,0:T(8,128)(2,1)S(1)}, u32[]{:S(2)}, u32[]{:S(2)}) collective-permute-start(bf16[2,400,128]{2,1,0:T(8,128)(2,1)S(1)} %get-tuple-element.30), channel_id=1, source_target_pairs={{0,384},{128,0},{256,128},{384,256},{1,385},{129,1},{257,129},{385... | collective-permute-start | bytes 614408 | tf_op jit(solution)/shard_map/ppermute | solution.py:216
  39.3 4.2 %collective-permute-done.2 = bf16[2,400,128]{2,1,0:T(8,128)(2,1)S(1)} collective-permute-done((bf16[2,400,128]{2,1,0:T(8,128)(2,1)S(1)}, bf16[2,400,128]{2,1,0:T(8,128)(2,1)S(1)}, u32[]{:S(2)}, u32[]{:S(2)}) %collective-permute-start.2) | collective-permute-done | bytes 204832 | tf_op jit(solution)/shard_map/ppermute | solution.py:216
  45.0 21.5 %all-to-all-done.pairs_ref = bf16[128,2,3200]{2,1,0:T(2,128)(2,1)S(1)} async-done(((bf16[128,2,3200]{2,1,0:T(2,128)(2,1)}), bf16[128,2,3200]{2,1,0:T(2,128)(2,1)S(1)}, u32[]{:S(2)}, u32[]{:S(2)}) %all-to-all-start) | async-done | bytes 1638432 | tf_op jit(solution)/shard_map/all_to_all | solution.py:163
  67.7 5.1 %shard_map.92 = bf16[4,320,1280]{2,1,0:T(8,128)(2,1)} custom-call(bf16[128,2,3200]{2,1,0:T(2,128)(2,1)} %copy-done), custom_call_target="tpu_custom_call" | custom-call | flops 10000000 | bytes 4915200 | tf_op jit(solution)/shard_map/pallas_call | solution.py:21
  72.8 4.7 %all-to-all-start.1 = ((bf16[4,320,1280]{2,1,0:T(8,128)(2,1)}), bf16[4,320,1280]{2,1,0:T(8,128)(2,1)}, u32[]{:S(2)}, u32[]{:S(2)}) async-start(bf16[4,320,1280]{2,1,0:T(8,128)(2,1)} %shard_map.92), calls=%async_computation.1 | async-start | bytes 6553600 | tf_op jit(solution)/shard_map/all_to_all | solution.py:253
  78.5 2.9 %collective-permute-start.7 = (bf16[2,400,128]{2,1,0:T(8,128)(2,1)}, bf16[2,400,128]{2,1,0:T(8,128)(2,1)S(1)}, u32[]{:S(2)}, u32[]{:S(2)}) collective-permute-start(bf16[2,400,128]{2,1,0:T(8,128)(2,1)} %get-tuple-element.23), channel_id=1, source_target_pairs={{0,24},{2,56},{4,88},{6,120},{8,0},{10,32},{12,64},{14,96},{16,8},... | collective-permute-start | bytes 614408 | tf_op jit(solution)/shard_map/ppermute | solution.py:232
  81.4 4.7 %collective-permute-start.6 = (bf16[2,400,128]{2,1,0:T(8,128)(2,1)}, bf16[2,400,128]{2,1,0:T(8,128)(2,1)S(1)}, u32[]{:S(2)}, u32[]{:S(2)}) collective-permute-start(bf16[2,400,128]{2,1,0:T(8,128)(2,1)} %get-tuple-element.24), channel_id=1, source_target_pairs={{0,16},{2,48},{4,80},{6,112},{8,24},{10,56},{12,88},{14,120},{16,0... | collective-permute-start | bytes 614408 | tf_op jit(solution)/shard_map/ppermute | solution.py:232
  88.0 3.4 %collective-permute-start.4 = (bf16[2,400,128]{2,1,0:T(8,128)(2,1)}, bf16[2,400,128]{2,1,0:T(8,128)(2,1)}, u32[]{:S(2)}, u32[]{:S(2)}) collective-permute-start(bf16[2,400,128]{2,1,0:T(8,128)(2,1)} %get-tuple-element.26), channel_id=1, source_target_pairs={{0,0},{2,32},{4,64},{6,96},{8,8},{10,40},{12,72},{14,104},{16,16},... | collective-permute-start | bytes 614408 | tf_op jit(solution)/shard_map/ppermute | solution.py:232
  93.5 21.3 %all-to-all-done.1.lefts_hbm = bf16[4,320,1280]{2,1,0:T(8,128)(2,1)} async-done(((bf16[4,320,1280]{2,1,0:T(8,128)(2,1)}), bf16[4,320,1280]{2,1,0:T(8,128)(2,1)}, u32[]{:S(2)}, u32[]{:S(2)}) %all-to-all-start.1) | async-done | bytes 3276832 | tf_op jit(solution)/shard_map/all_to_all | solution.py:253
  114.8 4.6 %shard_map.94 = bf16[128,2,1664]{2,1,0:T(2,128)(2,1)S(1)} custom-call(bf16[4,320,1280]{2,1,0:T(8,128)(2,1)} %all-to-all-done.1.lefts_hbm, bf16[1280,512]{1,0:T(8,128)(2,1)S(1)} %shard_map.93.right_ref), custom_call_target="tpu_custom_call" | custom-call | flops 1677721600 | bytes 5439488 | tf_op jit(solution)/shard_map/pallas_call | solution.py:21
  120.3 12.5 %all-to-all-start.2 = ((bf16[128,2,1664]{2,1,0:T(2,128)(2,1)}), bf16[128,2,1664]{2,1,0:T(2,128)(2,1)S(1)}, u32[]{:S(2)}, u32[]{:S(2)}) async-start(bf16[128,2,1664]{2,1,0:T(2,128)(2,1)} %copy-done.2), calls=%async_computation.2 | async-start | bytes 1703936 | tf_op jit(solution)/shard_map/all_to_all | solution.py:163
  134.2 4.2 %collective-permute-start.10 = (bf16[2,400,128]{2,1,0:T(8,128)(2,1)S(1)}, bf16[2,400,128]{2,1,0:T(8,128)(2,1)S(1)}, u32[]{:S(2)}, u32[]{:S(2)}) collective-permute-start(bf16[2,400,128]{2,1,0:T(8,128)(2,1)S(1)} %get-tuple-element.19), channel_id=1, source_target_pairs={{0,384},{128,0},{256,128},{384,256},{1,385},{129,1},{257,129},{385... | collective-permute-start | bytes 614408 | tf_op jit(solution)/shard_map/ppermute | solution.py:240
  138.4 2.5 %collective-permute-start.9 = (bf16[2,400,128]{2,1,0:T(8,128)(2,1)S(1)}, bf16[2,400,128]{2,1,0:T(8,128)(2,1)S(1)}, u32[]{:S(2)}, u32[]{:S(2)}) collective-permute-start(bf16[2,400,128]{2,1,0:T(8,128)(2,1)S(1)} %get-tuple-element.20), channel_id=1, source_target_pairs={{0,256},{128,384},{256,0},{384,128},{1,257},{129,385},{257,1},{385... | collective-permute-start | bytes 614408 | tf_op jit(solution)/shard_map/ppermute | solution.py:240
  140.9 2.5 %collective-permute-start.8 = (bf16[2,400,128]{2,1,0:T(8,128)(2,1)S(1)}, bf16[2,400,128]{2,1,0:T(8,128)(2,1)S(1)}, u32[]{:S(2)}, u32[]{:S(2)}) collective-permute-start(bf16[2,400,128]{2,1,0:T(8,128)(2,1)S(1)} %get-tuple-element.21), channel_id=1, source_target_pairs={{0,128},{128,256},{256,384},{384,0},{1,129},{129,257},{257,385},{3... | collective-permute-start | bytes 614408 | tf_op jit(solution)/shard_map/ppermute | solution.py:240
  143.5 3.7 %collective-permute-done.9.f2 = bf16[2,400,128]{2,1,0:T(8,128)(2,1)S(1)} collective-permute-done((bf16[2,400,128]{2,1,0:T(8,128)(2,1)S(1)}, bf16[2,400,128]{2,1,0:T(8,128)(2,1)S(1)}, u32[]{:S(2)}, u32[]{:S(2)}) %collective-permute-start.9) | collective-permute-done | bytes 204832 | tf_op jit(solution)/shard_map/ppermute | solution.py:240
  147.2 5.3 %collective-permute-done.8.f1 = bf16[2,400,128]{2,1,0:T(8,128)(2,1)S(1)} collective-permute-done((bf16[2,400,128]{2,1,0:T(8,128)(2,1)S(1)}, bf16[2,400,128]{2,1,0:T(8,128)(2,1)S(1)}, u32[]{:S(2)}, u32[]{:S(2)}) %collective-permute-start.8) | collective-permute-done | bytes 204832 | tf_op jit(solution)/shard_map/ppermute | solution.py:240
  152.5 2.1 %shard_map.95.gate_ref = bf16[3200,128]{1,0:T(8,128)(2,1)S(1)} custom-call(s32[5]{0:T(128)S(1)} %pad_add_fusion.place_ref, f32[1,128]{1,0:T(1,128)S(1)} %bitcast.41, bf16[128,128]{1,0:T(8,128)(2,1)S(1)} %copy-done.4, bf16[2,400,128]{2,1,0:T(8,128)(2,1)S(1)} %get-tuple-element.22.f0, bf16[2,400,128]{2,1,0:T(8,128)(2,1)S(1)} %collective-permute-done.8.f1, ...), custom_call_target="tpu_custom_call" | custom-call | flops 104857600 | bytes 1671700 | tf_op jit(solution)/shard_map/pallas_call | solution.py:21
  154.7 3.6 %all-to-all-done.2.pairs_ref = bf16[128,2,1664]{2,1,0:T(2,128)(2,1)S(1)} async-done(((bf16[128,2,1664]{2,1,0:T(2,128)(2,1)}), bf16[128,2,1664]{2,1,0:T(2,128)(2,1)S(1)}, u32[]{:S(2)}, u32[]{:S(2)}) %all-to-all-start.2) | async-done | bytes 852000 | tf_op jit(solution)/shard_map/all_to_all | solution.py:163
  158.3 3.3 %shard_map.96 = bf16[3200,128]{1,0:T(8,128)(2,1)} custom-call(bf16[128,2,1664]{2,1,0:T(2,128)(2,1)S(1)} %all-to-all-done.2.pairs_ref, bf16[3200,128]{1,0:T(8,128)(2,1)S(1)} %shard_map.95.gate_ref, f32[128,1]{1,0:T(8,128)S(1)} %copy.10.gain_ref, bf16[128,128]{1,0:T(8,128)(2,1)S(1)} %copy-done.3), custom_call_target="tpu_custom_call" | custom-call | flops 104857600 | bytes 2523648 | tf_op jit(solution)/shard_map/pallas_call | solution.py:21
  (35 shorter events, 11.5 us)
Async XLA Ops:
  5.8 18.6 %copy-start.6 = (bf16[80,40,128]{2,1,0:T(8,128)(2,1)S(1)}, bf16[80,40,128]{2,1,0:T(8,128)(2,1)}, u32[]{:S(2)}) copy-start(bf16[80,40,128]{2,1,0:T(8,128)(2,1)} %param.9) | copy-start | bytes 2457604
  5.8 60.7 %all-to-all-start = ((bf16[128,2,3200]{2,1,0:T(2,128)(2,1)}), bf16[128,2,3200]{2,1,0:T(2,128)(2,1)S(1)}, u32[]{:S(2)}, u32[]{:S(2)}) async-start(bf16[128,2,3200]{2,1,0:T(2,128)(2,1)} %shard_map.91), calls=%async_computation | async-start | bytes 3276800 | tf_op jit(solution)/shard_map/all_to_all | solution.py:163
  24.4 4.2 %collective-permute-start = (bf16[4,400,128]{2,1,0:T(8,128)(2,1)S(1)}, bf16[4,400,128]{2,1,0:T(8,128)(2,1)S(1)}, u32[]{:S(2)}, u32[]{:S(2)}) collective-permute-start(bf16[4,400,128]{2,1,0:T(8,128)(2,1)S(1)} %get-tuple-element.31), channel_id=1, source_target_pairs={{0,1},{1,0},{2,3},{3,2},{4,5},{5,4},{6,7},{7,6},{8,9},{9,8},{10,11... | collective-permute-start | bytes 1228808 | tf_op jit(solution)/shard_map/ppermute | solution.py:210
  28.7 10.6 %collective-permute-start.1 = (bf16[2,400,128]{2,1,0:T(8,128)(2,1)S(1)}, bf16[2,400,128]{2,1,0:T(8,128)(2,1)S(1)}, u32[]{:S(2)}, u32[]{:S(2)}) collective-permute-start(bf16[2,400,128]{2,1,0:T(8,128)(2,1)S(1)} %get-tuple-element.28), channel_id=1, source_target_pairs={{0,128},{128,256},{256,384},{384,0},{1,129},{129,257},{257,385},{3... | collective-permute-start | bytes 614408 | tf_op jit(solution)/shard_map/ppermute | solution.py:216
  31.8 11.6 %collective-permute-start.2 = (bf16[2,400,128]{2,1,0:T(8,128)(2,1)S(1)}, bf16[2,400,128]{2,1,0:T(8,128)(2,1)S(1)}, u32[]{:S(2)}, u32[]{:S(2)}) collective-permute-start(bf16[2,400,128]{2,1,0:T(8,128)(2,1)S(1)} %get-tuple-element.29), channel_id=1, source_target_pairs={{0,256},{128,384},{256,0},{384,128},{1,257},{129,385},{257,1},{385... | collective-permute-start | bytes 614408 | tf_op jit(solution)/shard_map/ppermute | solution.py:216
  36.2 8.7 %collective-permute-start.3 = (bf16[2,400,128]{2,1,0:T(8,128)(2,1)S(1)}, bf16[2,400,128]{2,1,0:T(8,128)(2,1)S(1)}, u32[]{:S(2)}, u32[]{:S(2)}) collective-permute-start(bf16[2,400,128]{2,1,0:T(8,128)(2,1)S(1)} %get-tuple-element.30), channel_id=1, source_target_pairs={{0,384},{128,0},{256,128},{384,256},{1,385},{129,1},{257,129},{385... | collective-permute-start | bytes 614408 | tf_op jit(solution)/shard_map/ppermute | solution.py:216
  66.5 1.2 copy-start
  72.8 42.0 %all-to-all-start.1 = ((bf16[4,320,1280]{2,1,0:T(8,128)(2,1)}), bf16[4,320,1280]{2,1,0:T(8,128)(2,1)}, u32[]{:S(2)}, u32[]{:S(2)}) async-start(bf16[4,320,1280]{2,1,0:T(8,128)(2,1)} %shard_map.92), calls=%async_computation.1 | async-start | bytes 6553600 | tf_op jit(solution)/shard_map/all_to_all | solution.py:253
  77.5 13.9 %copy-start.1 = (bf16[128,2,3200]{2,1,0:T(2,128)(2,1)S(1)}, bf16[128,2,3200]{2,1,0:T(2,128)(2,1)}, u32[]{:S(2)}) copy-start(bf16[128,2,3200]{2,1,0:T(2,128)(2,1)} %copy-done) | copy-start | bytes 4915204
  78.5 41.8 %collective-permute-start.7 = (bf16[2,400,128]{2,1,0:T(8,128)(2,1)}, bf16[2,400,128]{2,1,0:T(8,128)(2,1)S(1)}, u32[]{:S(2)}, u32[]{:S(2)}) collective-permute-start(bf16[2,400,128]{2,1,0:T(8,128)(2,1)} %get-tuple-element.23), channel_id=1, source_target_pairs={{0,24},{2,56},{4,88},{6,120},{8,0},{10,32},{12,64},{14,96},{16,8},... | collective-permute-start | bytes 614408 | tf_op jit(solution)/shard_map/ppermute | solution.py:232
  81.4 38.9 %collective-permute-start.6 = (bf16[2,400,128]{2,1,0:T(8,128)(2,1)}, bf16[2,400,128]{2,1,0:T(8,128)(2,1)S(1)}, u32[]{:S(2)}, u32[]{:S(2)}) collective-permute-start(bf16[2,400,128]{2,1,0:T(8,128)(2,1)} %get-tuple-element.24), channel_id=1, source_target_pairs={{0,16},{2,48},{4,80},{6,112},{8,24},{10,56},{12,88},{14,120},{16,0... | collective-permute-start | bytes 614408 | tf_op jit(solution)/shard_map/ppermute | solution.py:232
  86.1 34.2 %collective-permute-start.5 = (bf16[2,400,128]{2,1,0:T(8,128)(2,1)}, bf16[2,400,128]{2,1,0:T(8,128)(2,1)}, u32[]{:S(2)}, u32[]{:S(2)}) collective-permute-start(bf16[2,400,128]{2,1,0:T(8,128)(2,1)} %get-tuple-element.25), channel_id=1, source_target_pairs={{0,8},{2,40},{4,72},{6,104},{8,16},{10,48},{12,80},{14,112},{16,24... | collective-permute-start | bytes 614408 | tf_op jit(solution)/shard_map/ppermute | solution.py:232
  88.0 32.3 %collective-permute-start.4 = (bf16[2,400,128]{2,1,0:T(8,128)(2,1)}, bf16[2,400,128]{2,1,0:T(8,128)(2,1)}, u32[]{:S(2)}, u32[]{:S(2)}) collective-permute-start(bf16[2,400,128]{2,1,0:T(8,128)(2,1)} %get-tuple-element.26), channel_id=1, source_target_pairs={{0,0},{2,32},{4,64},{6,96},{8,8},{10,40},{12,72},{14,104},{16,16},... | collective-permute-start | bytes 614408 | tf_op jit(solution)/shard_map/ppermute | solution.py:232
  119.3 0.9 copy-start.2
  120.3 12.5 %copy-start.7 = (f32[128]{0:T(128)S(1)}, f32[128]{0:T(128)}, u32[]{:S(2)}) copy-start(f32[128]{0:T(128)} %param.17) | copy-start | bytes 1540
  120.3 38.0 %all-to-all-start.2 = ((bf16[128,2,1664]{2,1,0:T(2,128)(2,1)}), bf16[128,2,1664]{2,1,0:T(2,128)(2,1)S(1)}, u32[]{:S(2)}, u32[]{:S(2)}) async-start(bf16[128,2,1664]{2,1,0:T(2,128)(2,1)} %copy-done.2), calls=%async_computation.2 | async-start | bytes 1703936 | tf_op jit(solution)/shard_map/all_to_all | solution.py:163
  132.9 19.6 %copy-start.4 = (bf16[128,128]{1,0:T(8,128)(2,1)S(1)}, bf16[128,128]{1,0:T(8,128)(2,1)}, u32[]{:S(2)}) copy-start(bf16[128,128]{1,0:T(8,128)(2,1)} %weight_ref.1) | copy-start | bytes 98308
  132.9 19.6 %copy-start.5 = (f32[128]{0:T(128)S(1)}, f32[128]{0:T(128)}, u32[]{:S(2)}) copy-start(f32[128]{0:T(128)} %param.10) | copy-start | bytes 1540
  134.1 24.2 %copy-start.3 = (bf16[128,128]{1,0:T(8,128)(2,1)S(1)}, bf16[128,128]{1,0:T(8,128)(2,1)}, u32[]{:S(2)}) copy-start(bf16[128,128]{1,0:T(8,128)(2,1)} %proj_ref.1) | copy-start | bytes 98308
  134.2 9.3 %collective-permute-start.10 = (bf16[2,400,128]{2,1,0:T(8,128)(2,1)S(1)}, bf16[2,400,128]{2,1,0:T(8,128)(2,1)S(1)}, u32[]{:S(2)}, u32[]{:S(2)}) collective-permute-start(bf16[2,400,128]{2,1,0:T(8,128)(2,1)S(1)} %get-tuple-element.19), channel_id=1, source_target_pairs={{0,384},{128,0},{256,128},{384,256},{1,385},{129,1},{257,129},{385... | collective-permute-start | bytes 614408 | tf_op jit(solution)/shard_map/ppermute | solution.py:240
  138.4 8.8 %collective-permute-start.9 = (bf16[2,400,128]{2,1,0:T(8,128)(2,1)S(1)}, bf16[2,400,128]{2,1,0:T(8,128)(2,1)S(1)}, u32[]{:S(2)}, u32[]{:S(2)}) collective-permute-start(bf16[2,400,128]{2,1,0:T(8,128)(2,1)S(1)} %get-tuple-element.20), channel_id=1, source_target_pairs={{0,256},{128,384},{256,0},{384,128},{1,257},{129,385},{257,1},{385... | collective-permute-start | bytes 614408 | tf_op jit(solution)/shard_map/ppermute | solution.py:240
  140.9 11.6 %collective-permute-start.8 = (bf16[2,400,128]{2,1,0:T(8,128)(2,1)S(1)}, bf16[2,400,128]{2,1,0:T(8,128)(2,1)S(1)}, u32[]{:S(2)}, u32[]{:S(2)}) collective-permute-start(bf16[2,400,128]{2,1,0:T(8,128)(2,1)S(1)} %get-tuple-element.21), channel_id=1, source_target_pairs={{0,128},{128,256},{256,384},{384,0},{1,129},{129,257},{257,385},{3... | collective-permute-start | bytes 614408 | tf_op jit(solution)/shard_map/ppermute | solution.py:240

commit v4 on v3

--- a/solution.py
+++ b/solution.py
@@ -14,6 +14,8 @@
 SPLIT = 13 * 128
 VMEM_LIMIT = 20 * 1024 * 1024
 VMEM_MOST = 56 * 1024 * 1024
+VMEM_UNPACK = 50 * 1024 * 1024
+VMEM_TRIANGLE = 52 * 1024 * 1024
 
 
 def call(kernel, outs, scratch, flops, args, far=(), limit=VMEM_LIMIT):
@@ -110,10 +112,13 @@
         out_ref[:, pl.ds(yl * 128, 128)] = tall_ref[...].astype(BF16)
 
 
-def triangle_kernel(lefts_hbm, right_ref, out_ref, prod_ref, wide_ref, lefts_ref, sems):
+def triangle_kernel(lefts_hbm, right_hbm, out_hbm, prod_ref, wide_ref, lefts_ref, right_ref, out_ref, sems):
     copies = [pltpu.make_async_copy(lefts_hbm.at[n], lefts_ref.at[n], sems.at[n]) for n in range(4)]
-    for copy in copies:
+    first = pltpu.make_async_copy(right_hbm, right_ref, sems.at[4])
+    for copy in (first, *copies):
         copy.start()
+    stores = []
+    first.wait()
     right = right_ref[...]
     wide_ref[:, CELLS : 2 * SPLIT] = jnp.zeros((32, 2 * SPLIT - CELLS), F32)
     for n in range(4):
@@ -126,6 +131,11 @@
                 wide_ref[pl.ds(yl * 8, 8), pl.ds(i * ROWS, ROWS)] = prod_ref[yl, pl.ds(i, 8, stride=HALF), :][:, :ROWS]
         out_ref[n * 32 : n * 32 + 32, 0, :] = wide_ref[:, 0:SPLIT].astype(BF16)
         out_ref[n * 32 : n * 32 + 32, 1, :] = wide_ref[:, SPLIT : 2 * SPLIT].astype(BF16)
+        rows = pl.ds(n * 32, 32)
+        stores.append(pltpu.make_async_copy(out_ref.at[rows], out_hbm.at[rows], sems.at[5 + n]))
+        stores[-1].start()
+    for store in stores:
+        store.wait()
 
 
 def gate_kernel(place_ref, gain_ref, weight_ref, f0, f1, f2, f3, out_ref, open_ref):
@@ -181,7 +191,7 @@
 
 
 def left_unpack(pairs):
-    return call(left_unpack_kernel, (shape((4, 320, 1280)),), [FLAT_WIDE, TALL, pltpu.VMEM((320, 1280), BF16), pltpu.SemaphoreType.DMA((16,))], 10**7, (pairs,), (-1,), VMEM_MOST)
+    return call(left_unpack_kernel, (shape((4, 320, 1280)),), [FLAT_WIDE, TALL, pltpu.VMEM((320, 1280), BF16), pltpu.SemaphoreType.DMA((16,))], 10**7, (pairs,), (-1,), VMEM_UNPACK)
 
 
 def right_unpack(pairs):
@@ -189,8 +199,9 @@
 
 
 def triangle(lefts, right):
-    scratch = [pltpu.VMEM((4, 320, 128), F32), pltpu.VMEM((32, 2 * SPLIT), F32), pltpu.VMEM((4, 320, 1280), BF16), pltpu.SemaphoreType.DMA((4,))]
-    return call(triangle_kernel, (PAIRS,), scratch, 2 * 1280 * 1280 * 512, (lefts, right), (0,))
+    scratch = [pltpu.VMEM((4, 320, 128), F32), pltpu.VMEM((32, 2 * SPLIT), F32), pltpu.VMEM((4, 320, 1280), BF16)]
+    scratch += [pltpu.VMEM((1280, 512), BF16), pltpu.VMEM(PAIRS.shape, BF16), pltpu.SemaphoreType.DMA((9,))]
+    return call(triangle_kernel, (PAIRS,), scratch, 2 * 1280 * 1280 * 512, (lefts, right), (0, 1, -1), VMEM_TRIANGLE)
 
 
 def output_gate(*args):

time: 163 us -> 159 us (0.975)
  starting transfers between devices: 71.2 us -> 67.1 us
  waiting for transfers between devices: 62.4 us -> 66 us
  local copies, waits for them, and re-layouts: 3.33 us -> 1.4 us
    ppermute x4, starting transfers between devices: 12.9 us -> 10.2 us  [cross_plane(): lax.ppermute(pick(parts, x - zh - n & 3), ('yl', 'zh', 'z0', 'yh'), perm)]
    all_to_all x1, waiting for transfers between devices: 21.3 us -> 23.8 us  [body(): lefts = lax.all_to_all(own, 'x', split_axis=0, concat_axis=0)]
  transfers between devices with their start and end apart: 14 -> 14, of which waited for: 8 -> 8; matrix products, arithmetic and copies ran while one was open for 2% -> 0% of each run, Pallas kernels for 5% -> 6%
where the time goes in v4:
time: 159 us; the launch traced here: 158 us
  starting transfers between devices  67.1 us (42%)
  waiting for transfers between devices  66 us (42%)
  Pallas kernels  22.6 us (14%)
    all_to_all x2, starting transfers between devices, plane_swap(): lax.all_to_all(chunks, PLANE, split_axis=0, concat_axis=0, tiled=True)  29.6 us
    all_to_all x2, waiting for transfers between devices, plane_swap(): lax.all_to_all(chunks, PLANE, split_axis=0, concat_axis=0, tiled=True)  26.1 us
    all_to_all x1, waiting for transfers between devices, body(): lefts = lax.all_to_all(own, 'x', split_axis=0, concat_axis=0)  23.8 us
    pallas_call x6, Pallas kernels, call(): pl.pallas_call(kernel, out_shape=outs if len(outs) > 1 else outs[0], in_s...  22.6 us
    ppermute x3, starting transfers between devices, spread_x(): lax.ppermute(pick(pieces, x + d & 3), 'x', [(i, (i + d) % 4) for i in ran...  10.5 us
    ppermute x4, starting transfers between devices, cross_plane(): lax.ppermute(pick(parts, x - zh - n & 3), ('yl', 'zh', 'z0', 'yh'), perm)  10.2 us
    ppermute x3, starting transfers between devices, land_x(): lax.ppermute(part, 'x', [(i, (i + e) % 4) for i in range(4)])  9.2 us
    ppermute x3, waiting for transfers between devices, land_x(): lax.ppermute(part, 'x', [(i, (i + e) % 4) for i in range(4)])  9.04 us
  transfers between devices with their start and end apart: 14, of which 8 were waited for; matrix products, arithmetic and copies ran while one was open for 0% of the time, Pallas kernels for 6%

profile of v4, /device:TPU:1, one launch (start us, length us, event | category | flops | bytes accessed | tf_op | source)
XLA Modules:
  0.0 157.8 jit_solution(11233268286340604148)
XLA Ops:
  0.0 5.8 %shard_map.91 = bf16[128,2,3200]{2,1,0:T(2,128)(2,1)} custom-call(bf16[3200,128]{1,0:T(8,128)(2,1)} %bitcast.42, f32[1,128]{1,0:T(1,128)} %bitcast.40, bf16[128,128]{1,0:T(8,128)(2,1)} %refs_2_.1, bf16[128,128]{1,0:T(8,128)(2,1)} %refs_3_.1, bf16[128,128]{1,0:T(8,128)(2,1)} %refs_4_.1, bf16[128,128]{1,0:T(8,128)(2,1)} %refs_5_.1), custom_call_target="tpu_custom_call" | custom-call | flops 419430400 | bytes 2589184 | tf_op jit(solution)/shard_map/pallas_call | solution.py:23
  5.8 18.6 %all-to-all-start = ((bf16[128,2,3200]{2,1,0:T(2,128)(2,1)}), bf16[128,2,3200]{2,1,0:T(2,128)(2,1)S(1)}, u32[]{:S(2)}, u32[]{:S(2)}) async-start(bf16[128,2,3200]{2,1,0:T(2,128)(2,1)} %shard_map.91), calls=%async_computation | async-start | bytes 3276800 | tf_op jit(solution)/shard_map/all_to_all | solution.py:173
  24.5 2.8 %collective-permute-start = (bf16[4,400,128]{2,1,0:T(8,128)(2,1)S(1)}, bf16[4,400,128]{2,1,0:T(8,128)(2,1)S(1)}, u32[]{:S(2)}, u32[]{:S(2)}) collective-permute-start(bf16[4,400,128]{2,1,0:T(8,128)(2,1)S(1)} %get-tuple-element.31), channel_id=1, source_target_pairs={{0,1},{1,0},{2,3},{3,2},{4,5},{5,4},{6,7},{7,6},{8,9},{9,8},{10,11... | collective-permute-start | bytes 1228808 | tf_op jit(solution)/shard_map/ppermute | solution.py:221
  28.7 3.1 %collective-permute-start.1 = (bf16[2,400,128]{2,1,0:T(8,128)(2,1)S(1)}, bf16[2,400,128]{2,1,0:T(8,128)(2,1)S(1)}, u32[]{:S(2)}, u32[]{:S(2)}) collective-permute-start(bf16[2,400,128]{2,1,0:T(8,128)(2,1)S(1)} %get-tuple-element.28), channel_id=1, source_target_pairs={{0,128},{128,256},{256,384},{384,0},{1,129},{129,257},{257,385},{3... | collective-permute-start | bytes 614408 | tf_op jit(solution)/shard_map/ppermute | solution.py:227
  31.8 4.4 %collective-permute-start.2 = (bf16[2,400,128]{2,1,0:T(8,128)(2,1)S(1)}, bf16[2,400,128]{2,1,0:T(8,128)(2,1)S(1)}, u32[]{:S(2)}, u32[]{:S(2)}) collective-permute-start(bf16[2,400,128]{2,1,0:T(8,128)(2,1)S(1)} %get-tuple-element.29), channel_id=1, source_target_pairs={{0,256},{128,384},{256,0},{384,128},{1,257},{129,385},{257,1},{385... | collective-permute-start | bytes 614408 | tf_op jit(solution)/shard_map/ppermute | solution.py:227
  36.2 3.1 %collective-permute-start.3 = (bf16[2,400,128]{2,1,0:T(8,128)(2,1)S(1)}, bf16[2,400,128]{2,1,0:T(8,128)(2,1)S(1)}, u32[]{:S(2)}, u32[]{:S(2)}) collective-permute-start(bf16[2,400,128]{2,1,0:T(8,128)(2,1)S(1)} %get-tuple-element.30), channel_id=1, source_target_pairs={{0,384},{128,0},{256,128},{384,256},{1,385},{129,1},{257,129},{385... | collective-permute-start | bytes 614408 | tf_op jit(solution)/shard_map/ppermute | solution.py:227
  39.3 4.2 %collective-permute-done.2 = bf16[2,400,128]{2,1,0:T(8,128)(2,1)S(1)} collective-permute-done((bf16[2,400,128]{2,1,0:T(8,128)(2,1)S(1)}, bf16[2,400,128]{2,1,0:T(8,128)(2,1)S(1)}, u32[]{:S(2)}, u32[]{:S(2)}) %collective-permute-start.2) | collective-permute-done | bytes 204832 | tf_op jit(solution)/shard_map/ppermute | solution.py:227
  45.0 21.5 %all-to-all-done.pairs_ref = bf16[128,2,3200]{2,1,0:T(2,128)(2,1)S(1)} async-done(((bf16[128,2,3200]{2,1,0:T(2,128)(2,1)}), bf16[128,2,3200]{2,1,0:T(2,128)(2,1)S(1)}, u32[]{:S(2)}, u32[]{:S(2)}) %all-to-all-start) | async-done | bytes 1638432 | tf_op jit(solution)/shard_map/all_to_all | solution.py:173
  66.5 3.6 %shard_map.92 = bf16[4,320,1280]{2,1,0:T(8,128)(2,1)} custom-call(bf16[128,2,3200]{2,1,0:T(2,128)(2,1)S(1)} %all-to-all-done.pairs_ref), custom_call_target="tpu_custom_call" | custom-call | flops 10000000 | bytes 4915200 | tf_op jit(solution)/shard_map/pallas_call | solution.py:23
  70.2 4.7 %all-to-all-start.1 = ((bf16[4,320,1280]{2,1,0:T(8,128)(2,1)}), bf16[4,320,1280]{2,1,0:T(8,128)(2,1)}, u32[]{:S(2)}, u32[]{:S(2)}) async-start(bf16[4,320,1280]{2,1,0:T(8,128)(2,1)} %shard_map.92), calls=%async_computation.1 | async-start | bytes 6553600 | tf_op jit(solution)/shard_map/all_to_all | solution.py:264
  74.9 2.9 %collective-permute-start.7 = (bf16[2,400,128]{2,1,0:T(8,128)(2,1)S(1)}, bf16[2,400,128]{2,1,0:T(8,128)(2,1)S(1)}, u32[]{:S(2)}, u32[]{:S(2)}) collective-permute-start(bf16[2,400,128]{2,1,0:T(8,128)(2,1)S(1)} %get-tuple-element.23), channel_id=1, source_target_pairs={{0,24},{2,56},{4,88},{6,120},{8,0},{10,32},{12,64},{14,96},{16,8},... | collective-permute-start | bytes 614408 | tf_op jit(solution)/shard_map/ppermute | solution.py:243
  77.8 4.7 %collective-permute-start.6 = (bf16[2,400,128]{2,1,0:T(8,128)(2,1)S(1)}, bf16[2,400,128]{2,1,0:T(8,128)(2,1)S(1)}, u32[]{:S(2)}, u32[]{:S(2)}) collective-permute-start(bf16[2,400,128]{2,1,0:T(8,128)(2,1)S(1)} %get-tuple-element.24), channel_id=1, source_target_pairs={{0,16},{2,48},{4,80},{6,112},{8,24},{10,56},{12,88},{14,120},{16,0... | collective-permute-start | bytes 614408 | tf_op jit(solution)/shard_map/ppermute | solution.py:243
  85.2 2.0 %shard_map.93.right_hbm = bf16[1280,512]{1,0:T(8,128)(2,1)S(1)} custom-call(bf16[128,2,3200]{2,1,0:T(2,128)(2,1)S(1)} %all-to-all-done.pairs_ref), custom_call_target="tpu_custom_call" | custom-call | flops 10000000 | bytes 2949120 | tf_op jit(solution)/shard_map/pallas_call | solution.py:23
  88.3 23.8 %all-to-all-done.1.lefts_hbm = bf16[4,320,1280]{2,1,0:T(8,128)(2,1)} async-done(((bf16[4,320,1280]{2,1,0:T(8,128)(2,1)}), bf16[4,320,1280]{2,1,0:T(8,128)(2,1)}, u32[]{:S(2)}, u32[]{:S(2)}) %all-to-all-start.1) | async-done | bytes 3276832 | tf_op jit(solution)/shard_map/all_to_all | solution.py:264
  112.1 5.7 %shard_map.94 = bf16[128,2,1664]{2,1,0:T(2,128)(2,1)} custom-call(bf16[4,320,1280]{2,1,0:T(8,128)(2,1)} %all-to-all-done.1.lefts_hbm, bf16[1280,512]{1,0:T(8,128)(2,1)} %copy-done), custom_call_target="tpu_custom_call" | custom-call | flops 1677721600 | bytes 5439488 | tf_op jit(solution)/shard_map/pallas_call | solution.py:23
  117.9 11.1 %all-to-all-start.2 = ((bf16[128,2,1664]{2,1,0:T(2,128)(2,1)}), bf16[128,2,1664]{2,1,0:T(2,128)(2,1)S(1)}, u32[]{:S(2)}, u32[]{:S(2)}) async-start(bf16[128,2,1664]{2,1,0:T(2,128)(2,1)} %shard_map.94), calls=%async_computation.2 | async-start | bytes 1703936 | tf_op jit(solution)/shard_map/all_to_all | solution.py:173
  129.3 4.2 %collective-permute-start.10 = (bf16[2,400,128]{2,1,0:T(8,128)(2,1)S(1)}, bf16[2,400,128]{2,1,0:T(8,128)(2,1)S(1)}, u32[]{:S(2)}, u32[]{:S(2)}) collective-permute-start(bf16[2,400,128]{2,1,0:T(8,128)(2,1)S(1)} %get-tuple-element.19), channel_id=1, source_target_pairs={{0,384},{128,0},{256,128},{384,256},{1,385},{129,1},{257,129},{385... | collective-permute-start | bytes 614408 | tf_op jit(solution)/shard_map/ppermute | solution.py:251
  133.5 2.5 %collective-permute-start.9 = (bf16[2,400,128]{2,1,0:T(8,128)(2,1)S(1)}, bf16[2,400,128]{2,1,0:T(8,128)(2,1)S(1)}, u32[]{:S(2)}, u32[]{:S(2)}) collective-permute-start(bf16[2,400,128]{2,1,0:T(8,128)(2,1)S(1)} %get-tuple-element.20), channel_id=1, source_target_pairs={{0,256},{128,384},{256,0},{384,128},{1,257},{129,385},{257,1},{385... | collective-permute-start | bytes 614408 | tf_op jit(solution)/shard_map/ppermute | solution.py:251
  136.0 2.5 %collective-permute-start.8 = (bf16[2,400,128]{2,1,0:T(8,128)(2,1)S(1)}, bf16[2,400,128]{2,1,0:T(8,128)(2,1)S(1)}, u32[]{:S(2)}, u32[]{:S(2)}) collective-permute-start(bf16[2,400,128]{2,1,0:T(8,128)(2,1)S(1)} %get-tuple-element.21), channel_id=1, source_target_pairs={{0,128},{128,256},{256,384},{384,0},{1,129},{129,257},{257,385},{3... | collective-permute-start | bytes 614408 | tf_op jit(solution)/shard_map/ppermute | solution.py:251
  138.6 3.7 %collective-permute-done.9.f2 = bf16[2,400,128]{2,1,0:T(8,128)(2,1)S(1)} collective-permute-done((bf16[2,400,128]{2,1,0:T(8,128)(2,1)S(1)}, bf16[2,400,128]{2,1,0:T(8,128)(2,1)S(1)}, u32[]{:S(2)}, u32[]{:S(2)}) %collective-permute-start.9) | collective-permute-done | bytes 204832 | tf_op jit(solution)/shard_map/ppermute | solution.py:251
  142.3 5.3 %collective-permute-done.8.f1 = bf16[2,400,128]{2,1,0:T(8,128)(2,1)S(1)} collective-permute-done((bf16[2,400,128]{2,1,0:T(8,128)(2,1)S(1)}, bf16[2,400,128]{2,1,0:T(8,128)(2,1)S(1)}, u32[]{:S(2)}, u32[]{:S(2)}) %collective-permute-start.8) | collective-permute-done | bytes 204832 | tf_op jit(solution)/shard_map/ppermute | solution.py:251
  147.7 2.1 %shard_map.95.gate_ref = bf16[3200,128]{1,0:T(8,128)(2,1)S(1)} custom-call(s32[5]{0:T(128)S(1)} %pad_add_fusion.place_ref, f32[1,128]{1,0:T(1,128)S(1)} %bitcast.41, bf16[128,128]{1,0:T(8,128)(2,1)S(1)} %copy-done.2, bf16[2,400,128]{2,1,0:T(8,128)(2,1)S(1)} %get-tuple-element.22.f0, bf16[2,400,128]{2,1,0:T(8,128)(2,1)S(1)} %collective-permute-done.8.f1, ...), custom_call_target="tpu_custom_call" | custom-call | flops 104857600 | bytes 1671700 | tf_op jit(solution)/shard_map/pallas_call | solution.py:23
  149.8 4.6 %all-to-all-done.2.pairs_ref = bf16[128,2,1664]{2,1,0:T(2,128)(2,1)S(1)} async-done(((bf16[128,2,1664]{2,1,0:T(2,128)(2,1)}), bf16[128,2,1664]{2,1,0:T(2,128)(2,1)S(1)}, u32[]{:S(2)}, u32[]{:S(2)}) %all-to-all-start.2) | async-done | bytes 852000 | tf_op jit(solution)/shard_map/all_to_all | solution.py:173
  154.4 3.3 %shard_map.96 = bf16[3200,128]{1,0:T(8,128)(2,1)} custom-call(bf16[128,2,1664]{2,1,0:T(2,128)(2,1)S(1)} %all-to-all-done.2.pairs_ref, bf16[3200,128]{1,0:T(8,128)(2,1)S(1)} %shard_map.95.gate_ref, f32[128,1]{1,0:T(8,128)S(1)} %copy.10.gain_ref, bf16[128,128]{1,0:T(8,128)(2,1)S(1)} %copy-done.1), custom_call_target="tpu_custom_call" | custom-call | flops 104857600 | bytes 2523648 | tf_op jit(solution)/shard_map/pallas_call | solution.py:23
  (31 shorter events, 7.2 us)
Async XLA Ops:
  5.8 18.6 %copy-start.4 = (bf16[80,40,128]{2,1,0:T(8,128)(2,1)S(1)}, bf16[80,40,128]{2,1,0:T(8,128)(2,1)}, u32[]{:S(2)}) copy-start(bf16[80,40,128]{2,1,0:T(8,128)(2,1)} %param.9) | copy-start | bytes 2457604
  5.8 60.7 %all-to-all-start = ((bf16[128,2,3200]{2,1,0:T(2,128)(2,1)}), bf16[128,2,3200]{2,1,0:T(2,128)(2,1)S(1)}, u32[]{:S(2)}, u32[]{:S(2)}) async-start(bf16[128,2,3200]{2,1,0:T(2,128)(2,1)} %shard_map.91), calls=%async_computation | async-start | bytes 3276800 | tf_op jit(solution)/shard_map/all_to_all | solution.py:173
  24.5 4.2 %collective-permute-start = (bf16[4,400,128]{2,1,0:T(8,128)(2,1)S(1)}, bf16[4,400,128]{2,1,0:T(8,128)(2,1)S(1)}, u32[]{:S(2)}, u32[]{:S(2)}) collective-permute-start(bf16[4,400,128]{2,1,0:T(8,128)(2,1)S(1)} %get-tuple-element.31), channel_id=1, source_target_pairs={{0,1},{1,0},{2,3},{3,2},{4,5},{5,4},{6,7},{7,6},{8,9},{9,8},{10,11... | collective-permute-start | bytes 1228808 | tf_op jit(solution)/shard_map/ppermute | solution.py:221
  28.7 10.6 %collective-permute-start.1 = (bf16[2,400,128]{2,1,0:T(8,128)(2,1)S(1)}, bf16[2,400,128]{2,1,0:T(8,128)(2,1)S(1)}, u32[]{:S(2)}, u32[]{:S(2)}) collective-permute-start(bf16[2,400,128]{2,1,0:T(8,128)(2,1)S(1)} %get-tuple-element.28), channel_id=1, source_target_pairs={{0,128},{128,256},{256,384},{384,0},{1,129},{129,257},{257,385},{3... | collective-permute-start | bytes 614408 | tf_op jit(solution)/shard_map/ppermute | solution.py:227
  31.8 11.6 %collective-permute-start.2 = (bf16[2,400,128]{2,1,0:T(8,128)(2,1)S(1)}, bf16[2,400,128]{2,1,0:T(8,128)(2,1)S(1)}, u32[]{:S(2)}, u32[]{:S(2)}) collective-permute-start(bf16[2,400,128]{2,1,0:T(8,128)(2,1)S(1)} %get-tuple-element.29), channel_id=1, source_target_pairs={{0,256},{128,384},{256,0},{384,128},{1,257},{129,385},{257,1},{385... | collective-permute-start | bytes 614408 | tf_op jit(solution)/shard_map/ppermute | solution.py:227
  36.2 8.7 %collective-permute-start.3 = (bf16[2,400,128]{2,1,0:T(8,128)(2,1)S(1)}, bf16[2,400,128]{2,1,0:T(8,128)(2,1)S(1)}, u32[]{:S(2)}, u32[]{:S(2)}) collective-permute-start(bf16[2,400,128]{2,1,0:T(8,128)(2,1)S(1)} %get-tuple-element.30), channel_id=1, source_target_pairs={{0,384},{128,0},{256,128},{384,256},{1,385},{129,1},{257,129},{385... | collective-permute-start | bytes 614408 | tf_op jit(solution)/shard_map/ppermute | solution.py:227
  70.2 41.9 %all-to-all-start.1 = ((bf16[4,320,1280]{2,1,0:T(8,128)(2,1)}), bf16[4,320,1280]{2,1,0:T(8,128)(2,1)}, u32[]{:S(2)}, u32[]{:S(2)}) async-start(bf16[4,320,1280]{2,1,0:T(8,128)(2,1)} %shard_map.92), calls=%async_computation.1 | async-start | bytes 6553600 | tf_op jit(solution)/shard_map/all_to_all | solution.py:264
  74.9 42.9 %collective-permute-start.7 = (bf16[2,400,128]{2,1,0:T(8,128)(2,1)S(1)}, bf16[2,400,128]{2,1,0:T(8,128)(2,1)S(1)}, u32[]{:S(2)}, u32[]{:S(2)}) collective-permute-start(bf16[2,400,128]{2,1,0:T(8,128)(2,1)S(1)} %get-tuple-element.23), channel_id=1, source_target_pairs={{0,24},{2,56},{4,88},{6,120},{8,0},{10,32},{12,64},{14,96},{16,8},... | collective-permute-start | bytes 614408 | tf_op jit(solution)/shard_map/ppermute | solution.py:243
  77.8 40.0 %collective-permute-start.6 = (bf16[2,400,128]{2,1,0:T(8,128)(2,1)S(1)}, bf16[2,400,128]{2,1,0:T(8,128)(2,1)S(1)}, u32[]{:S(2)}, u32[]{:S(2)}) collective-permute-start(bf16[2,400,128]{2,1,0:T(8,128)(2,1)S(1)} %get-tuple-element.24), channel_id=1, source_target_pairs={{0,16},{2,48},{4,80},{6,112},{8,24},{10,56},{12,88},{14,120},{16,0... | collective-permute-start | bytes 614408 | tf_op jit(solution)/shard_map/ppermute | solution.py:243
  82.6 35.3 %collective-permute-start.5 = (bf16[2,400,128]{2,1,0:T(8,128)(2,1)S(1)}, bf16[2,400,128]{2,1,0:T(8,128)(2,1)S(1)}, u32[]{:S(2)}, u32[]{:S(2)}) collective-permute-start(bf16[2,400,128]{2,1,0:T(8,128)(2,1)S(1)} %get-tuple-element.25), channel_id=1, source_target_pairs={{0,8},{2,40},{4,72},{6,104},{8,16},{10,48},{12,80},{14,112},{16,24... | collective-permute-start | bytes 614408 | tf_op jit(solution)/shard_map/ppermute | solution.py:243
  84.5 33.4 %collective-permute-start.4 = (bf16[2,400,128]{2,1,0:T(8,128)(2,1)S(1)}, bf16[2,400,128]{2,1,0:T(8,128)(2,1)S(1)}, u32[]{:S(2)}, u32[]{:S(2)}) collective-permute-start(bf16[2,400,128]{2,1,0:T(8,128)(2,1)S(1)} %get-tuple-element.26), channel_id=1, source_target_pairs={{0,0},{2,32},{4,64},{6,96},{8,8},{10,40},{12,72},{14,104},{16,16},... | collective-permute-start | bytes 614408 | tf_op jit(solution)/shard_map/ppermute | solution.py:243
  87.2 1.1 copy-start
  117.8 11.1 %copy-start.5 = (f32[128]{0:T(128)S(1)}, f32[128]{0:T(128)}, u32[]{:S(2)}) copy-start(f32[128]{0:T(128)} %param.17) | copy-start | bytes 1540
  117.9 36.6 %all-to-all-start.2 = ((bf16[128,2,1664]{2,1,0:T(2,128)(2,1)}), bf16[128,2,1664]{2,1,0:T(2,128)(2,1)S(1)}, u32[]{:S(2)}, u32[]{:S(2)}) async-start(bf16[128,2,1664]{2,1,0:T(2,128)(2,1)} %shard_map.94), calls=%async_computation.2 | async-start | bytes 1703936 | tf_op jit(solution)/shard_map/all_to_all | solution.py:173
  129.1 18.6 %copy-start.2 = (bf16[128,128]{1,0:T(8,128)(2,1)S(1)}, bf16[128,128]{1,0:T(8,128)(2,1)}, u32[]{:S(2)}) copy-start(bf16[128,128]{1,0:T(8,128)(2,1)} %weight_ref.1) | copy-start | bytes 98308
  129.1 18.6 %copy-start.3 = (f32[128]{0:T(128)S(1)}, f32[128]{0:T(128)}, u32[]{:S(2)}) copy-start(f32[128]{0:T(128)} %param.10) | copy-start | bytes 1540
  129.2 25.2 %copy-start.1 = (bf16[128,128]{1,0:T(8,128)(2,1)S(1)}, bf16[128,128]{1,0:T(8,128)(2,1)}, u32[]{:S(2)}) copy-start(bf16[128,128]{1,0:T(8,128)(2,1)} %proj_ref.1) | copy-start | bytes 98308
  129.3 9.3 %collective-permute-start.10 = (bf16[2,400,128]{2,1,0:T(8,128)(2,1)S(1)}, bf16[2,400,128]{2,1,0:T(8,128)(2,1)S(1)}, u32[]{:S(2)}, u32[]{:S(2)}) collective-permute-start(bf16[2,400,128]{2,1,0:T(8,128)(2,1)S(1)} %get-tuple-element.19), channel_id=1, source_target_pairs={{0,384},{128,0},{256,128},{384,256},{1,385},{129,1},{257,129},{385... | collective-permute-start | bytes 614408 | tf_op jit(solution)/shard_map/ppermute | solution.py:251
  133.5 8.8 %collective-permute-start.9 = (bf16[2,400,128]{2,1,0:T(8,128)(2,1)S(1)}, bf16[2,400,128]{2,1,0:T(8,128)(2,1)S(1)}, u32[]{:S(2)}, u32[]{:S(2)}) collective-permute-start(bf16[2,400,128]{2,1,0:T(8,128)(2,1)S(1)} %get-tuple-element.20), channel_id=1, source_target_pairs={{0,256},{128,384},{256,0},{384,128},{1,257},{129,385},{257,1},{385... | collective-permute-start | bytes 614408 | tf_op jit(solution)/shard_map/ppermute | solution.py:251
  136.0 11.6 %collective-permute-start.8 = (bf16[2,400,128]{2,1,0:T(8,128)(2,1)S(1)}, bf16[2,400,128]{2,1,0:T(8,128)(2,1)S(1)}, u32[]{:S(2)}, u32[]{:S(2)}) collective-permute-start(bf16[2,400,128]{2,1,0:T(8,128)(2,1)S(1)} %get-tuple-element.21), channel_id=1, source_target_pairs={{0,128},{128,256},{256,384},{384,0},{1,129},{129,257},{257,385},{3... | collective-permute-start | bytes 614408 | tf_op jit(solution)/shard_map/ppermute | solution.py:251

commit v5 on v4

--- a/solution.py
+++ b/solution.py
@@ -40,7 +40,8 @@
 
 
 def edges_kernel(*refs):
-    sources, pairs_ref, landed, normed_ref, rows_ref, sems = refs[:6], refs[6], refs[7:13], refs[13], refs[14], refs[15]
+    sources, pairs_hbm, landed = refs[:6], refs[6], refs[7:13]
+    normed_ref, rows_ref, pairs_ref, sems = refs[13:]
     z_ref, gain_ref, a_gate, a_proj, b_gate, b_proj = landed
     copies = [pltpu.make_async_copy(source, target, sems.at[n]) for n, (source, target) in enumerate(zip(sources[1:], landed[1:]))]
     parts = [
@@ -61,6 +62,7 @@
         rows_ref[part, :] = centred * lax.rsqrt(var_val + 1e-05) * gain
     for copy in copies[1:]:
         copy.wait()
+    stores = []
     for k in range(COLS):
         normed_ref[pl.ds(k * ROWS, ROWS), :] = rows_ref[pl.ds(k, ROWS, stride=COLS), :].astype(BF16)
     for t in range(5):
@@ -69,6 +71,10 @@
         for row, gate_ref, proj_ref in ((0, a_gate, a_proj), (1, b_gate, b_proj)):
             edge = jax.nn.sigmoid(dot_nt(gate_ref[...], cells)) * dot_nt(proj_ref[...], cells)
             pairs_ref[:, row, part] = edge.astype(BF16)
+        stores.append(pltpu.make_async_copy(pairs_ref.at[:, :, part], pairs_hbm.at[:, :, part], sems.at[10 + t]))
+        stores[-1].start()
+    for store in stores:
+        store.wait()
 
 
 def widen(pairs_ref, places):
@@ -154,7 +160,8 @@
         out_ref[pl.ds(j * HALF, ROWS), :] = jnp.concatenate(pair, axis=0).astype(BF16)
 
 
-def output_kernel(pairs_ref, gate_ref, gain_ref, proj_ref, out_ref, prod_ref, tri_ref):
+def output_kernel(pairs_ref, gate_ref, gain_ref, proj_ref, out_hbm, prod_ref, tri_ref, out_ref, sems):
+    stores = []
     widen(pairs_ref, {0: (tri_ref, 0), 1: (tri_ref, SPLIT)})
     for t in range(25):
         lanes = pl.ds(t * 128, 128)
@@ -167,6 +174,12 @@
         rows = pl.ds(j * HALF, ROWS)
         pair = jnp.concatenate([prod_ref[pl.ds(j + n, HALF, stride=ROWS), :] for n in range(2)], axis=0)
         out_ref[rows, :] = (pair * gate_ref[rows, :].astype(F32)).astype(BF16)
+        if j % 16 == 14:
+            part = pl.ds((j // 16) * 640, 640)
+            stores.append(pltpu.make_async_copy(out_ref.at[part, :], out_hbm.at[part, :], sems.at[j // 16]))
+            stores[-1].start()
+    for store in stores:
+        store.wait()
 
 
 def plane_swap(chunks):
@@ -186,8 +199,8 @@
 
 def edges(*args):
     landing = [pltpu.VMEM(a.shape, a.dtype) for a in args]
-    scratch = [*landing, pltpu.VMEM((CELLS, CHANS), BF16), FLAT, pltpu.SemaphoreType.DMA((10,))]
-    return call(edges_kernel, (shape((CHANS, 2, CELLS)),), scratch, 8 * CELLS * CHANS * CHANS, args, range(6), VMEM_MOST)
+    scratch = [*landing, pltpu.VMEM((CELLS, CHANS), BF16), FLAT, pltpu.VMEM((CHANS, 2, CELLS), BF16), pltpu.SemaphoreType.DMA((15,))]
+    return call(edges_kernel, (shape((CHANS, 2, CELLS)),), scratch, 8 * CELLS * CHANS * CHANS, args, (*range(6), -1), VMEM_MOST)
 
 
 def left_unpack(pairs):
@@ -209,7 +222,7 @@
 
 
 def output(*args):
-    return call(output_kernel, (shape((CELLS, CHANS)),), [FLAT, WIDE], 2 * CELLS * CHANS * CHANS, args)
+    return call(output_kernel, (shape((CELLS, CHANS)),), [FLAT, WIDE, pltpu.VMEM((CELLS, CHANS), BF16), pltpu.SemaphoreType.DMA((5,))], 2 * CELLS * CHANS * CHANS, args, (-1,))
 
 
 def pick(parts, index):

time: 159 us -> 159 us (level)
  no operation moved by 1% of the time
where the time goes in v5:
time: 159 us; the launch traced here: 158 us
  starting transfers between devices  67.1 us (42%)
  waiting for transfers between devices  66 us (42%)
  Pallas kernels  22.3 us (14%)
    all_to_all x2, starting transfers between devices, plane_swap(): lax.all_to_all(chunks, PLANE, split_axis=0, concat_axis=0, tiled=True)  29.6 us
    all_to_all x2, waiting for transfers between devices, plane_swap(): lax.all_to_all(chunks, PLANE, split_axis=0, concat_axis=0, tiled=True)  26.1 us
    all_to_all x1, waiting for transfers between devices, body(): lefts = lax.all_to_all(own, 'x', split_axis=0, concat_axis=0)  23.8 us
    pallas_call x6, Pallas kernels, call(): pl.pallas_call(kernel, out_shape=outs if len(outs) > 1 else outs[0], in_s...  22.3 us
    ppermute x3, starting transfers between devices, spread_x(): lax.ppermute(pick(pieces, x + d & 3), 'x', [(i, (i + d) % 4) for i in ran...  10.5 us
    ppermute x4, starting transfers between devices, cross_plane(): lax.ppermute(pick(parts, x - zh - n & 3), ('yl', 'zh', 'z0', 'yh'), perm)  10.2 us
    ppermute x3, starting transfers between devices, land_x(): lax.ppermute(part, 'x', [(i, (i + e) % 4) for i in range(4)])  9.2 us
    ppermute x3, waiting for transfers between devices, land_x(): lax.ppermute(part, 'x', [(i, (i + e) % 4) for i in range(4)])  9.04 us
  transfers between devices with their start and end apart: 14, of which 8 were waited for; matrix products, arithmetic and copies ran while one was open for 0% of the time, Pallas kernels for 6%

profile of v5, /device:TPU:1, one launch (start us, length us, event | category | flops | bytes accessed | tf_op | source)
XLA Modules:
  0.0 157.6 jit_solution(12824409889817991392)
XLA Ops:
  0.0 5.4 %shard_map.91 = bf16[128,2,3200]{2,1,0:T(2,128)(2,1)} custom-call(bf16[3200,128]{1,0:T(8,128)(2,1)} %bitcast.42, f32[1,128]{1,0:T(1,128)} %bitcast.40, bf16[128,128]{1,0:T(8,128)(2,1)} %refs_2_.1, bf16[128,128]{1,0:T(8,128)(2,1)} %refs_3_.1, bf16[128,128]{1,0:T(8,128)(2,1)} %refs_4_.1, bf16[128,128]{1,0:T(8,128)(2,1)} %refs_5_.1), custom_call_target="tpu_custom_call" | custom-call | flops 419430400 | bytes 2589184 | tf_op jit(solution)/shard_map/pallas_call | solution.py:23
  5.4 18.6 %all-to-all-start = ((bf16[128,2,3200]{2,1,0:T(2,128)(2,1)}), bf16[128,2,3200]{2,1,0:T(2,128)(2,1)S(1)}, u32[]{:S(2)}, u32[]{:S(2)}) async-start(bf16[128,2,3200]{2,1,0:T(2,128)(2,1)} %shard_map.91), calls=%async_computation | async-start | bytes 3276800 | tf_op jit(solution)/shard_map/all_to_all | solution.py:186
  24.0 2.8 %collective-permute-start = (bf16[4,400,128]{2,1,0:T(8,128)(2,1)S(1)}, bf16[4,400,128]{2,1,0:T(8,128)(2,1)S(1)}, u32[]{:S(2)}, u32[]{:S(2)}) collective-permute-start(bf16[4,400,128]{2,1,0:T(8,128)(2,1)S(1)} %get-tuple-element.31), channel_id=1, source_target_pairs={{0,1},{1,0},{2,3},{3,2},{4,5},{5,4},{6,7},{7,6},{8,9},{9,8},{10,11... | collective-permute-start | bytes 1228808 | tf_op jit(solution)/shard_map/ppermute | solution.py:234
  28.3 3.1 %collective-permute-start.1 = (bf16[2,400,128]{2,1,0:T(8,128)(2,1)S(1)}, bf16[2,400,128]{2,1,0:T(8,128)(2,1)S(1)}, u32[]{:S(2)}, u32[]{:S(2)}) collective-permute-start(bf16[2,400,128]{2,1,0:T(8,128)(2,1)S(1)} %get-tuple-element.28), channel_id=1, source_target_pairs={{0,128},{128,256},{256,384},{384,0},{1,129},{129,257},{257,385},{3... | collective-permute-start | bytes 614408 | tf_op jit(solution)/shard_map/ppermute | solution.py:240
  31.4 4.4 %collective-permute-start.2 = (bf16[2,400,128]{2,1,0:T(8,128)(2,1)S(1)}, bf16[2,400,128]{2,1,0:T(8,128)(2,1)S(1)}, u32[]{:S(2)}, u32[]{:S(2)}) collective-permute-start(bf16[2,400,128]{2,1,0:T(8,128)(2,1)S(1)} %get-tuple-element.29), channel_id=1, source_target_pairs={{0,256},{128,384},{256,0},{384,128},{1,257},{129,385},{257,1},{385... | collective-permute-start | bytes 614408 | tf_op jit(solution)/shard_map/ppermute | solution.py:240
  35.8 3.1 %collective-permute-start.3 = (bf16[2,400,128]{2,1,0:T(8,128)(2,1)S(1)}, bf16[2,400,128]{2,1,0:T(8,128)(2,1)S(1)}, u32[]{:S(2)}, u32[]{:S(2)}) collective-permute-start(bf16[2,400,128]{2,1,0:T(8,128)(2,1)S(1)} %get-tuple-element.30), channel_id=1, source_target_pairs={{0,384},{128,0},{256,128},{384,256},{1,385},{129,1},{257,129},{385... | collective-permute-start | bytes 614408 | tf_op jit(solution)/shard_map/ppermute | solution.py:240
  38.9 4.2 %collective-permute-done.2 = bf16[2,400,128]{2,1,0:T(8,128)(2,1)S(1)} collective-permute-done((bf16[2,400,128]{2,1,0:T(8,128)(2,1)S(1)}, bf16[2,400,128]{2,1,0:T(8,128)(2,1)S(1)}, u32[]{:S(2)}, u32[]{:S(2)}) %collective-permute-start.2) | collective-permute-done | bytes 204832 | tf_op jit(solution)/shard_map/ppermute | solution.py:240
  44.6 21.5 %all-to-all-done.pairs_ref = bf16[128,2,3200]{2,1,0:T(2,128)(2,1)S(1)} async-done(((bf16[128,2,3200]{2,1,0:T(2,128)(2,1)}), bf16[128,2,3200]{2,1,0:T(2,128)(2,1)S(1)}, u32[]{:S(2)}, u32[]{:S(2)}) %all-to-all-start) | async-done | bytes 1638432 | tf_op jit(solution)/shard_map/all_to_all | solution.py:186
  66.1 3.6 %shard_map.92 = bf16[4,320,1280]{2,1,0:T(8,128)(2,1)} custom-call(bf16[128,2,3200]{2,1,0:T(2,128)(2,1)S(1)} %all-to-all-done.pairs_ref), custom_call_target="tpu_custom_call" | custom-call | flops 10000000 | bytes 4915200 | tf_op jit(solution)/shard_map/pallas_call | solution.py:23
  69.7 4.7 %all-to-all-start.1 = ((bf16[4,320,1280]{2,1,0:T(8,128)(2,1)}), bf16[4,320,1280]{2,1,0:T(8,128)(2,1)}, u32[]{:S(2)}, u32[]{:S(2)}) async-start(bf16[4,320,1280]{2,1,0:T(8,128)(2,1)} %shard_map.92), calls=%async_computation.1 | async-start | bytes 6553600 | tf_op jit(solution)/shard_map/all_to_all | solution.py:277
  74.5 2.9 %collective-permute-start.7 = (bf16[2,400,128]{2,1,0:T(8,128)(2,1)S(1)}, bf16[2,400,128]{2,1,0:T(8,128)(2,1)S(1)}, u32[]{:S(2)}, u32[]{:S(2)}) collective-permute-start(bf16[2,400,128]{2,1,0:T(8,128)(2,1)S(1)} %get-tuple-element.23), channel_id=1, source_target_pairs={{0,24},{2,56},{4,88},{6,120},{8,0},{10,32},{12,64},{14,96},{16,8},... | collective-permute-start | bytes 614408 | tf_op jit(solution)/shard_map/ppermute | solution.py:256
  77.4 4.7 %collective-permute-start.6 = (bf16[2,400,128]{2,1,0:T(8,128)(2,1)S(1)}, bf16[2,400,128]{2,1,0:T(8,128)(2,1)S(1)}, u32[]{:S(2)}, u32[]{:S(2)}) collective-permute-start(bf16[2,400,128]{2,1,0:T(8,128)(2,1)S(1)} %get-tuple-element.24), channel_id=1, source_target_pairs={{0,16},{2,48},{4,80},{6,112},{8,24},{10,56},{12,88},{14,120},{16,0... | collective-permute-start | bytes 614408 | tf_op jit(solution)/shard_map/ppermute | solution.py:256
  84.8 2.0 %shard_map.93.right_hbm = bf16[1280,512]{1,0:T(8,128)(2,1)S(1)} custom-call(bf16[128,2,3200]{2,1,0:T(2,128)(2,1)S(1)} %all-to-all-done.pairs_ref), custom_call_target="tpu_custom_call" | custom-call | flops 10000000 | bytes 2949120 | tf_op jit(solution)/shard_map/pallas_call | solution.py:23
  87.9 23.8 %all-to-all-done.1.lefts_hbm = bf16[4,320,1280]{2,1,0:T(8,128)(2,1)} async-done(((bf16[4,320,1280]{2,1,0:T(8,128)(2,1)}), bf16[4,320,1280]{2,1,0:T(8,128)(2,1)}, u32[]{:S(2)}, u32[]{:S(2)}) %all-to-all-start.1) | async-done | bytes 3276832 | tf_op jit(solution)/shard_map/all_to_all | solution.py:277
  111.7 5.7 %shard_map.94 = bf16[128,2,1664]{2,1,0:T(2,128)(2,1)} custom-call(bf16[4,320,1280]{2,1,0:T(8,128)(2,1)} %all-to-all-done.1.lefts_hbm, bf16[1280,512]{1,0:T(8,128)(2,1)} %copy-done), custom_call_target="tpu_custom_call" | custom-call | flops 1677721600 | bytes 5439488 | tf_op jit(solution)/shard_map/pallas_call | solution.py:23
  117.5 11.1 %all-to-all-start.2 = ((bf16[128,2,1664]{2,1,0:T(2,128)(2,1)}), bf16[128,2,1664]{2,1,0:T(2,128)(2,1)S(1)}, u32[]{:S(2)}, u32[]{:S(2)}) async-start(bf16[128,2,1664]{2,1,0:T(2,128)(2,1)} %shard_map.94), calls=%async_computation.2 | async-start | bytes 1703936 | tf_op jit(solution)/shard_map/all_to_all | solution.py:186
  128.9 4.2 %collective-permute-start.10 = (bf16[2,400,128]{2,1,0:T(8,128)(2,1)S(1)}, bf16[2,400,128]{2,1,0:T(8,128)(2,1)S(1)}, u32[]{:S(2)}, u32[]{:S(2)}) collective-permute-start(bf16[2,400,128]{2,1,0:T(8,128)(2,1)S(1)} %get-tuple-element.19), channel_id=1, source_target_pairs={{0,384},{128,0},{256,128},{384,256},{1,385},{129,1},{257,129},{385... | collective-permute-start | bytes 614408 | tf_op jit(solution)/shard_map/ppermute | solution.py:264
  133.1 2.5 %collective-permute-start.9 = (bf16[2,400,128]{2,1,0:T(8,128)(2,1)S(1)}, bf16[2,400,128]{2,1,0:T(8,128)(2,1)S(1)}, u32[]{:S(2)}, u32[]{:S(2)}) collective-permute-start(bf16[2,400,128]{2,1,0:T(8,128)(2,1)S(1)} %get-tuple-element.20), channel_id=1, source_target_pairs={{0,256},{128,384},{256,0},{384,128},{1,257},{129,385},{257,1},{385... | collective-permute-start | bytes 614408 | tf_op jit(solution)/shard_map/ppermute | solution.py:264
  135.6 2.5 %collective-permute-start.8 = (bf16[2,400,128]{2,1,0:T(8,128)(2,1)S(1)}, bf16[2,400,128]{2,1,0:T(8,128)(2,1)S(1)}, u32[]{:S(2)}, u32[]{:S(2)}) collective-permute-start(bf16[2,400,128]{2,1,0:T(8,128)(2,1)S(1)} %get-tuple-element.21), channel_id=1, source_target_pairs={{0,128},{128,256},{256,384},{384,0},{1,129},{129,257},{257,385},{3... | collective-permute-start | bytes 614408 | tf_op jit(solution)/shard_map/ppermute | solution.py:264
  138.2 3.7 %collective-permute-done.9.f2 = bf16[2,400,128]{2,1,0:T(8,128)(2,1)S(1)} collective-permute-done((bf16[2,400,128]{2,1,0:T(8,128)(2,1)S(1)}, bf16[2,400,128]{2,1,0:T(8,128)(2,1)S(1)}, u32[]{:S(2)}, u32[]{:S(2)}) %collective-permute-start.9) | collective-permute-done | bytes 204832 | tf_op jit(solution)/shard_map/ppermute | solution.py:264
  141.9 5.3 %collective-permute-done.8.f1 = bf16[2,400,128]{2,1,0:T(8,128)(2,1)S(1)} collective-permute-done((bf16[2,400,128]{2,1,0:T(8,128)(2,1)S(1)}, bf16[2,400,128]{2,1,0:T(8,128)(2,1)S(1)}, u32[]{:S(2)}, u32[]{:S(2)}) %collective-permute-start.8) | collective-permute-done | bytes 204832 | tf_op jit(solution)/shard_map/ppermute | solution.py:264
  147.2 2.1 %shard_map.95.gate_ref = bf16[3200,128]{1,0:T(8,128)(2,1)S(1)} custom-call(s32[5]{0:T(128)S(1)} %pad_add_fusion.place_ref, f32[1,128]{1,0:T(1,128)S(1)} %bitcast.41, bf16[128,128]{1,0:T(8,128)(2,1)S(1)} %copy-done.2, bf16[2,400,128]{2,1,0:T(8,128)(2,1)S(1)} %get-tuple-element.22.f0, bf16[2,400,128]{2,1,0:T(8,128)(2,1)S(1)} %collective-permute-done.8.f1, ...), custom_call_target="tpu_custom_call" | custom-call | flops 104857600 | bytes 1671700 | tf_op jit(solution)/shard_map/pallas_call | solution.py:23
  149.4 4.6 %all-to-all-done.2.pairs_ref = bf16[128,2,1664]{2,1,0:T(2,128)(2,1)S(1)} async-done(((bf16[128,2,1664]{2,1,0:T(2,128)(2,1)}), bf16[128,2,1664]{2,1,0:T(2,128)(2,1)S(1)}, u32[]{:S(2)}, u32[]{:S(2)}) %all-to-all-start.2) | async-done | bytes 852000 | tf_op jit(solution)/shard_map/all_to_all | solution.py:186
  154.0 3.5 %shard_map.96 = bf16[3200,128]{1,0:T(8,128)(2,1)} custom-call(bf16[128,2,1664]{2,1,0:T(2,128)(2,1)S(1)} %all-to-all-done.2.pairs_ref, bf16[3200,128]{1,0:T(8,128)(2,1)S(1)} %shard_map.95.gate_ref, f32[128,1]{1,0:T(8,128)S(1)} %copy.10.gain_ref, bf16[128,128]{1,0:T(8,128)(2,1)S(1)} %copy-done.1), custom_call_target="tpu_custom_call" | custom-call | flops 104857600 | bytes 2523648 | tf_op jit(solution)/shard_map/pallas_call | solution.py:23
  (31 shorter events, 7.2 us)
Async XLA Ops:
  5.4 18.6 %copy-start.4 = (bf16[80,40,128]{2,1,0:T(8,128)(2,1)S(1)}, bf16[80,40,128]{2,1,0:T(8,128)(2,1)}, u32[]{:S(2)}) copy-start(bf16[80,40,128]{2,1,0:T(8,128)(2,1)} %param.9) | copy-start | bytes 2457604
  5.4 60.7 %all-to-all-start = ((bf16[128,2,3200]{2,1,0:T(2,128)(2,1)}), bf16[128,2,3200]{2,1,0:T(2,128)(2,1)S(1)}, u32[]{:S(2)}, u32[]{:S(2)}) async-start(bf16[128,2,3200]{2,1,0:T(2,128)(2,1)} %shard_map.91), calls=%async_computation | async-start | bytes 3276800 | tf_op jit(solution)/shard_map/all_to_all | solution.py:186
  24.0 4.2 %collective-permute-start = (bf16[4,400,128]{2,1,0:T(8,128)(2,1)S(1)}, bf16[4,400,128]{2,1,0:T(8,128)(2,1)S(1)}, u32[]{:S(2)}, u32[]{:S(2)}) collective-permute-start(bf16[4,400,128]{2,1,0:T(8,128)(2,1)S(1)} %get-tuple-element.31), channel_id=1, source_target_pairs={{0,1},{1,0},{2,3},{3,2},{4,5},{5,4},{6,7},{7,6},{8,9},{9,8},{10,11... | collective-permute-start | bytes 1228808 | tf_op jit(solution)/shard_map/ppermute | solution.py:234
  28.3 10.6 %collective-permute-start.1 = (bf16[2,400,128]{2,1,0:T(8,128)(2,1)S(1)}, bf16[2,400,128]{2,1,0:T(8,128)(2,1)S(1)}, u32[]{:S(2)}, u32[]{:S(2)}) collective-permute-start(bf16[2,400,128]{2,1,0:T(8,128)(2,1)S(1)} %get-tuple-element.28), channel_id=1, source_target_pairs={{0,128},{128,256},{256,384},{384,0},{1,129},{129,257},{257,385},{3... | collective-permute-start | bytes 614408 | tf_op jit(solution)/shard_map/ppermute | solution.py:240
  31.4 11.6 %collective-permute-start.2 = (bf16[2,400,128]{2,1,0:T(8,128)(2,1)S(1)}, bf16[2,400,128]{2,1,0:T(8,128)(2,1)S(1)}, u32[]{:S(2)}, u32[]{:S(2)}) collective-permute-start(bf16[2,400,128]{2,1,0:T(8,128)(2,1)S(1)} %get-tuple-element.29), channel_id=1, source_target_pairs={{0,256},{128,384},{256,0},{384,128},{1,257},{129,385},{257,1},{385... | collective-permute-start | bytes 614408 | tf_op jit(solution)/shard_map/ppermute | solution.py:240
  35.8 8.7 %collective-permute-start.3 = (bf16[2,400,128]{2,1,0:T(8,128)(2,1)S(1)}, bf16[2,400,128]{2,1,0:T(8,128)(2,1)S(1)}, u32[]{:S(2)}, u32[]{:S(2)}) collective-permute-start(bf16[2,400,128]{2,1,0:T(8,128)(2,1)S(1)} %get-tuple-element.30), channel_id=1, source_target_pairs={{0,384},{128,0},{256,128},{384,256},{1,385},{129,1},{257,129},{385... | collective-permute-start | bytes 614408 | tf_op jit(solution)/shard_map/ppermute | solution.py:240
  69.7 41.9 %all-to-all-start.1 = ((bf16[4,320,1280]{2,1,0:T(8,128)(2,1)}), bf16[4,320,1280]{2,1,0:T(8,128)(2,1)}, u32[]{:S(2)}, u32[]{:S(2)}) async-start(bf16[4,320,1280]{2,1,0:T(8,128)(2,1)} %shard_map.92), calls=%async_computation.1 | async-start | bytes 6553600 | tf_op jit(solution)/shard_map/all_to_all | solution.py:277
  74.5 42.9 %collective-permute-start.7 = (bf16[2,400,128]{2,1,0:T(8,128)(2,1)S(1)}, bf16[2,400,128]{2,1,0:T(8,128)(2,1)S(1)}, u32[]{:S(2)}, u32[]{:S(2)}) collective-permute-start(bf16[2,400,128]{2,1,0:T(8,128)(2,1)S(1)} %get-tuple-element.23), channel_id=1, source_target_pairs={{0,24},{2,56},{4,88},{6,120},{8,0},{10,32},{12,64},{14,96},{16,8},... | collective-permute-start | bytes 614408 | tf_op jit(solution)/shard_map/ppermute | solution.py:256
  77.4 40.0 %collective-permute-start.6 = (bf16[2,400,128]{2,1,0:T(8,128)(2,1)S(1)}, bf16[2,400,128]{2,1,0:T(8,128)(2,1)S(1)}, u32[]{:S(2)}, u32[]{:S(2)}) collective-permute-start(bf16[2,400,128]{2,1,0:T(8,128)(2,1)S(1)} %get-tuple-element.24), channel_id=1, source_target_pairs={{0,16},{2,48},{4,80},{6,112},{8,24},{10,56},{12,88},{14,120},{16,0... | collective-permute-start | bytes 614408 | tf_op jit(solution)/shard_map/ppermute | solution.py:256
  82.2 35.3 %collective-permute-start.5 = (bf16[2,400,128]{2,1,0:T(8,128)(2,1)S(1)}, bf16[2,400,128]{2,1,0:T(8,128)(2,1)S(1)}, u32[]{:S(2)}, u32[]{:S(2)}) collective-permute-start(bf16[2,400,128]{2,1,0:T(8,128)(2,1)S(1)} %get-tuple-element.25), channel_id=1, source_target_pairs={{0,8},{2,40},{4,72},{6,104},{8,16},{10,48},{12,80},{14,112},{16,24... | collective-permute-start | bytes 614408 | tf_op jit(solution)/shard_map/ppermute | solution.py:256
  84.1 33.4 %collective-permute-start.4 = (bf16[2,400,128]{2,1,0:T(8,128)(2,1)S(1)}, bf16[2,400,128]{2,1,0:T(8,128)(2,1)S(1)}, u32[]{:S(2)}, u32[]{:S(2)}) collective-permute-start(bf16[2,400,128]{2,1,0:T(8,128)(2,1)S(1)} %get-tuple-element.26), channel_id=1, source_target_pairs={{0,0},{2,32},{4,64},{6,96},{8,8},{10,40},{12,72},{14,104},{16,16},... | collective-permute-start | bytes 614408 | tf_op jit(solution)/shard_map/ppermute | solution.py:256
  86.8 1.1 copy-start
  117.4 11.1 %copy-start.5 = (f32[128]{0:T(128)S(1)}, f32[128]{0:T(128)}, u32[]{:S(2)}) copy-start(f32[128]{0:T(128)} %param.17) | copy-start | bytes 1540
  117.5 36.6 %all-to-all-start.2 = ((bf16[128,2,1664]{2,1,0:T(2,128)(2,1)}), bf16[128,2,1664]{2,1,0:T(2,128)(2,1)S(1)}, u32[]{:S(2)}, u32[]{:S(2)}) async-start(bf16[128,2,1664]{2,1,0:T(2,128)(2,1)} %shard_map.94), calls=%async_computation.2 | async-start | bytes 1703936 | tf_op jit(solution)/shard_map/all_to_all | solution.py:186
  128.7 18.6 %copy-start.2 = (bf16[128,128]{1,0:T(8,128)(2,1)S(1)}, bf16[128,128]{1,0:T(8,128)(2,1)}, u32[]{:S(2)}) copy-start(bf16[128,128]{1,0:T(8,128)(2,1)} %weight_ref.1) | copy-start | bytes 98308
  128.7 18.6 %copy-start.3 = (f32[128]{0:T(128)S(1)}, f32[128]{0:T(128)}, u32[]{:S(2)}) copy-start(f32[128]{0:T(128)} %param.10) | copy-start | bytes 1540
  128.8 25.2 %copy-start.1 = (bf16[128,128]{1,0:T(8,128)(2,1)S(1)}, bf16[128,128]{1,0:T(8,128)(2,1)}, u32[]{:S(2)}) copy-start(bf16[128,128]{1,0:T(8,128)(2,1)} %proj_ref.1) | copy-start | bytes 98308
  128.9 9.3 %collective-permute-start.10 = (bf16[2,400,128]{2,1,0:T(8,128)(2,1)S(1)}, bf16[2,400,128]{2,1,0:T(8,128)(2,1)S(1)}, u32[]{:S(2)}, u32[]{:S(2)}) collective-permute-start(bf16[2,400,128]{2,1,0:T(8,128)(2,1)S(1)} %get-tuple-element.19), channel_id=1, source_target_pairs={{0,384},{128,0},{256,128},{384,256},{1,385},{129,1},{257,129},{385... | collective-permute-start | bytes 614408 | tf_op jit(solution)/shard_map/ppermute | solution.py:264
  133.1 8.8 %collective-permute-start.9 = (bf16[2,400,128]{2,1,0:T(8,128)(2,1)S(1)}, bf16[2,400,128]{2,1,0:T(8,128)(2,1)S(1)}, u32[]{:S(2)}, u32[]{:S(2)}) collective-permute-start(bf16[2,400,128]{2,1,0:T(8,128)(2,1)S(1)} %get-tuple-element.20), channel_id=1, source_target_pairs={{0,256},{128,384},{256,0},{384,128},{1,257},{129,385},{257,1},{385... | collective-permute-start | bytes 614408 | tf_op jit(solution)/shard_map/ppermute | solution.py:264
  135.6 11.6 %collective-permute-start.8 = (bf16[2,400,128]{2,1,0:T(8,128)(2,1)S(1)}, bf16[2,400,128]{2,1,0:T(8,128)(2,1)S(1)}, u32[]{:S(2)}, u32[]{:S(2)}) collective-permute-start(bf16[2,400,128]{2,1,0:T(8,128)(2,1)S(1)} %get-tuple-element.21), channel_id=1, source_target_pairs={{0,128},{128,256},{256,384},{384,0},{1,129},{129,257},{257,385},{3... | collective-permute-start | bytes 614408 | tf_op jit(solution)/shard_map/ppermute | solution.py:264
